TPU v7x, 32 devices: a whole 2x2x4 slice. The times are simulated.
32 devices in a mesh: section: 4 (over z), space: 8 (over y, x, core).
Axes of the slice: x: 2, y: 2, z: 4, core: 2. Of those that a mesh axis runs over, the one named last changes fastest.
Arguments:
- inputs: bfloat16 [4, 64, 8, 2, 128], P(None, None, 'space'), may hold values from -6 to 6
- cotangent: bfloat16 [4, 64, 8, 2, 128], P(None, None, 'space'), may hold values from -6 to 6
- conv_weight: bfloat16 [2, 4, 128, 1728], P(None, 'section'), may hold values from -0.15625 to 0.15625
- mix_weight: bfloat16 [2, 4, 64, 128], P(None, 'section'), may hold values from -0.5 to 0.5
Outputs:
- conv_grad: float32 [2, 4, 128, 1728], P(None, 'section')
- mix_grad: float32 [2, 4, 64, 128], P(None, 'section')
All inputs are finite; a program needn't handle non-finite values.
Results may differ from a plain program's by a relative error of at most 0.03.
Values may be sent and summed in bfloat16 or wider, within the bound.
No kernel may reach another device: no remote copies, remote signals or barrier semaphores. Data moves between devices by JAX's collectives and lax.ppermute only.
A program may use at most 64 MiB of HBM per device.

v0:
```python
import math

import jax
import jax.numpy as jnp
from jax import lax
from jax.sharding import PartitionSpec as P


def padded_2(block, sides, width):
    for axis, dim in sides:
        count = lax.axis_size(axis)
        forward = [(i, i + 1) for i in range(count - 1)]
        backward = [(target, source) for source, target in forward]
        low = lax.ppermute(
            lax.slice_in_dim(block, block.shape[dim] - width, None, axis=dim), axis, forward
        )
        high = lax.ppermute(lax.slice_in_dim(block, 0, width, axis=dim), axis, backward)
        block = jnp.concatenate([low, block, high], axis=dim)
    return block


def from_behind(block, axis, distance):
    devices = range(lax.axis_size(axis))
    route = [((i - distance) % len(devices), i) for i in devices]
    return lax.ppermute(block, axis, route)


def columns(padded, flip_sign, extent_x, extent_y, extent_z):
    pieces = []
    for step_x in (-1, 0, 1):
        for step_y in (-1, 0, 1):
            for step_z in (-1, 0, 1):
                start_x = 1 + flip_sign * step_x
                start_y = 1 + flip_sign * step_y
                start_z = 1 + flip_sign * step_z
                pieces.append(
                    padded[
                        :,
                        start_x : start_x + extent_x,
                        start_y : start_y + extent_y,
                        start_z : start_z + extent_z,
                    ]
                )
    stacked = jnp.stack(pieces, 0)
    return stacked.reshape(27 * padded.shape[0], extent_x * extent_y * extent_z)


def silu_slope(preact):
    sigmoid_val = jax.nn.sigmoid(preact)
    return sigmoid_val * (1.0 + preact * (1.0 - sigmoid_val))


def transpose_conv(conv_w, channels):
    hidden_count = conv_w.shape[0]
    return (
        conv_w.reshape(hidden_count, 27, channels)
        .transpose(2, 1, 0)
        .reshape(channels, 27 * hidden_count)
    )


def pad_sides(rimmed):
    return jnp.pad(rimmed, ((0, 0), (0, 0), (1, 1), (1, 1)))


def pick_pair(store, first_index, second_index):
    zero_index = jnp.zeros((), jnp.int32)
    starts = (first_index, second_index) + (zero_index,) * (store.ndim - 2)
    return lax.dynamic_slice(store, starts, (1, 1) + store.shape[2:])[0, 0]


def place_pair(store, value, first_index, second_index, active):
    zero_index = jnp.zeros((), jnp.int32)
    starts = (first_index, second_index) + (zero_index,) * (store.ndim - 2)
    current = pick_pair(store, first_index, second_index)
    chosen = jnp.where(active, value, current)
    return lax.dynamic_update_slice(store, chosen[None, None], starts)


def place_one(store, value, index_value, active):
    current = lax.dynamic_index_in_dim(store, index_value, 0, keepdims=False)
    chosen = jnp.where(active, value, current)
    return lax.dynamic_update_index_in_dim(store, chosen, index_value, 0)


def per_device(inputs, cotangent, conv_weight, mix_weight):
    micro_count, channels, extent_x, extent_y, extent_z = inputs.shape
    layer_groups = conv_weight.shape[0]
    hidden_count = conv_weight.shape[2]
    section_count = lax.axis_size("section")
    section_index = lax.axis_index("section")
    layer_count = layer_groups * section_count
    cell_count = extent_x * extent_y * extent_z
    conv_local = conv_weight[:, 0]
    mix_local = mix_weight[:, 0]
    flipped_local = jnp.stack(
        [transpose_conv(conv_local[layer_group], channels) for layer_group in range(layer_groups)],
        0,
    )
    delay_ticks = micro_count - 1
    tick_total = micro_count + layer_count - 1 + (layer_groups - 1) * delay_ticks
    tick_values = jnp.arange(tick_total, dtype=jnp.int32)

    def locate(tick_index, position):
        group_index = jnp.zeros((), jnp.int32)
        micro_index = jnp.zeros((), jnp.int32)
        active = tick_index < 0
        for layer_group in range(layer_groups):
            offset = tick_index - layer_group * (section_count + delay_ticks) - position
            inside = (offset >= 0) & (offset < micro_count)
            group_index = jnp.where(inside, jnp.int32(layer_group), group_index)
            micro_index = jnp.where(inside, offset, micro_index)
            active = active | inside
        return (group_index, micro_index, active)

    def store_returned(returned, incoming, tick_index):
        back_index = tick_index - section_count
        back_valid = (back_index >= 0) & (back_index < micro_count)
        back_safe = jnp.clip(back_index, 0, micro_count - 1)
        return place_one(returned, incoming, back_safe, back_valid)

    def forward_layer(activation, conv_w, mix_w):
        act_low = activation.astype(jnp.bfloat16)
        rimmed = padded_2(act_low, (("space", 1),), 1)
        window = columns(pad_sides(rimmed), 1, extent_x, extent_y, extent_z)
        preact = jnp.dot(conv_w, window, preferred_element_type=jnp.float32)
        hidden = jax.nn.silu(preact).astype(jnp.bfloat16)
        mixed_term = jnp.dot(mix_w, hidden, preferred_element_type=jnp.float32)
        result = activation.reshape(channels, cell_count) + mixed_term
        return (result.reshape(activation.shape), rimmed, preact, act_low)

    field_shape = (channels, extent_x, extent_y, extent_z)
    stores = jnp.zeros((layer_groups, micro_count) + field_shape, jnp.bfloat16)

    def forward_tick(carry, tick_index):
        incoming, returned, kept = carry
        layer_group, micro_index, active = locate(tick_index, section_index)
        returned = store_returned(returned, incoming, tick_index)
        fresh = lax.dynamic_index_in_dim(inputs, micro_index, 0, keepdims=False).astype(jnp.float32)
        looped = lax.dynamic_index_in_dim(returned, micro_index, 0, keepdims=False)
        first_section = jnp.where(layer_group == 0, fresh, looped)
        source = jnp.where(section_index == 0, first_section, incoming)
        conv_w = lax.dynamic_index_in_dim(conv_local, layer_group, 0, keepdims=False)
        mix_w = lax.dynamic_index_in_dim(mix_local, layer_group, 0, keepdims=False)
        result, rimmed, preact, act_low = forward_layer(source, conv_w, mix_w)
        kept = place_pair(kept, act_low, layer_group, micro_index, active)
        outgoing = from_behind(result, "section", 1)
        return ((outgoing, returned, kept), None)

    empty_field = jnp.zeros(field_shape, jnp.float32)
    empty_returned = jnp.zeros((micro_count,) + field_shape, jnp.float32)
    forward_state, unused = lax.scan(
        forward_tick, (empty_field, empty_returned, stores), tick_values
    )
    stores = forward_state[2]
    position = section_count - 1 - section_index

    def backward_tick(carry, tick_index):
        incoming, returned, conv_sum, mix_sum = carry
        mirror_group, micro_index, active = locate(tick_index, position)
        layer_group = layer_groups - 1 - mirror_group
        returned = store_returned(returned, incoming, tick_index)
        seed_grad = lax.dynamic_index_in_dim(cotangent, micro_index, 0, keepdims=False).astype(
            jnp.float32
        )
        looped = lax.dynamic_index_in_dim(returned, micro_index, 0, keepdims=False)
        last_section = jnp.where(mirror_group == 0, seed_grad, looped)
        upstream = jnp.where(position == 0, last_section, incoming)
        conv_w = lax.dynamic_index_in_dim(conv_local, layer_group, 0, keepdims=False)
        mix_w = lax.dynamic_index_in_dim(mix_local, layer_group, 0, keepdims=False)
        flipped = lax.dynamic_index_in_dim(flipped_local, layer_group, 0, keepdims=False)
        activation = pick_pair(stores, layer_group, micro_index)
        rimmed = padded_2(activation, (("space", 1),), 1)
        window = columns(pad_sides(rimmed), 1, extent_x, extent_y, extent_z)
        preact = jnp.dot(conv_w, window, preferred_element_type=jnp.float32)
        hidden = jax.nn.silu(preact).astype(jnp.bfloat16)
        flat_up = upstream.reshape(channels, cell_count)
        up_low = flat_up.astype(jnp.bfloat16)
        mix_term = jnp.dot(up_low, hidden.T, preferred_element_type=jnp.float32)
        hid_grad = jnp.dot(mix_w.T, up_low, preferred_element_type=jnp.float32)
        pre_grad = (hid_grad * silu_slope(preact)).astype(jnp.bfloat16)
        conv_term = jnp.dot(pre_grad, window.T, preferred_element_type=jnp.float32)
        grad_field = pre_grad.reshape(hidden_count, extent_x, extent_y, extent_z)
        grad_rimmed = padded_2(grad_field, (("space", 1),), 1)
        back_window = columns(pad_sides(grad_rimmed), -1, extent_x, extent_y, extent_z)
        spread = jnp.dot(flipped, back_window, preferred_element_type=jnp.float32)
        downstream = (flat_up + spread).reshape(field_shape)
        conv_now = lax.dynamic_index_in_dim(conv_sum, layer_group, 0, keepdims=False)
        mix_now = lax.dynamic_index_in_dim(mix_sum, layer_group, 0, keepdims=False)
        conv_sum = lax.dynamic_update_index_in_dim(
            conv_sum, jnp.where(active, conv_now + conv_term, conv_now), layer_group, 0
        )
        mix_sum = lax.dynamic_update_index_in_dim(
            mix_sum, jnp.where(active, mix_now + mix_term, mix_now), layer_group, 0
        )
        outgoing = from_behind(downstream, "section", -1)
        return ((outgoing, returned, conv_sum, mix_sum), None)

    conv_start = jnp.zeros((layer_groups, hidden_count, 27 * channels), jnp.float32)
    mix_start = jnp.zeros((layer_groups, channels, hidden_count), jnp.float32)
    backward_state, unused_back = lax.scan(
        backward_tick, (empty_field, empty_returned, conv_start, mix_start), tick_values
    )
    conv_total, mix_total = lax.psum((backward_state[2], backward_state[3]), "space")
    factor = 1.0 / math.sqrt(micro_count * extent_x * lax.axis_size("space") * extent_y * extent_z)
    return ((conv_total * factor)[:, None], (mix_total * factor)[:, None])


def solution(mesh):
    placed = (
        P(None, None, "space", None, None),
        P(None, None, "space", None, None),
        P(None, "section", None, None),
        P(None, "section", None, None),
    )
    return jax.shard_map(
        per_device,
        mesh=mesh,
        in_specs=placed,
        out_specs=(P(None, "section", None, None), P(None, "section", None, None)),
        check_vma=False,
    )
```

profile of v0, /device:TPU:1, one launch (start us, length us, event | category | flops | bytes accessed | tf_op | source)
XLA Modules:
  0.0 1019.8 jit_solution(11026127187103039807)
XLA Ops:
  11.5 308.0 %while.34 = (s32[]{:T(128)}, f32[64,1,2,128]{3,2,0,1:T(2,128)S(1)}, f32[4,64,1,2,128]{4,3,1,2,0:T(2,128)S(1)}, bf16[2,4,64,1,2,128]{5,4,2,3,1,0:T(2,128)(2,1)S(1...) while((s32[]{:T(128)}, f32[64,1,2,128]{3,2,0,1:T(2,128)S(1)}, ...), condition=%wide.region_1.2_spmd, body=%wide.region_0.1_spmd.sunk | while | flops 119616024 | bytes 4936221 | solution.py:152
  15.7 4.5 collective-permute-start.1
  50.3 4.9 collective-permute-done.2
  64.7 3.9 collective-permute-done
  72.4 4.9 collective-permute-done.2
  94.5 4.9 collective-permute-done.2
  116.5 4.9 collective-permute-done.2
  138.5 4.9 collective-permute-done.2
  160.5 4.9 collective-permute-done.2
  182.5 4.9 collective-permute-done.2
  204.5 4.9 collective-permute-done.2
  226.5 4.9 collective-permute-done.2
  248.5 4.9 collective-permute-done.2
  270.6 4.9 collective-permute-done.2
  292.6 4.9 collective-permute-done.2
  314.6 4.9 collective-permute-done.2
  320.6 625.1 %while.35 = (s32[]{:T(128)}, f32[64,1,2,128]{3,2,0,1:T(2,128)S(1)}, f32[4,64,1,2,128]{4,3,1,2,0:T(2,128)S(1)}, f32[2,128,1728]{1,2,0:T(8,128)S(1)}, f32[2,64,128...) while((s32[]{:T(128)}, f32[64,1,2,128]{3,2,0,1:T(2,128)S(1)}, ...), condition=%wide.region_3.4_spmd, body=%wide.region_2.3_spmd.sunk | while | flops 354833920 | bytes 30681180 | solution.py:201
  341.8 4.0 collective-permute-start.6
  385.0 4.0 collective-permute-start.6
  428.2 4.0 collective-permute-start.6
  472.9 4.0 collective-permute-start.6
  517.9 4.0 collective-permute-start.6
  562.8 4.0 collective-permute-start.6
  607.8 4.0 collective-permute-start.6
  652.8 4.0 collective-permute-start.6
  697.7 4.0 collective-permute-start.6
  742.7 4.0 collective-permute-start.6
  787.7 4.0 collective-permute-start.6
  832.6 4.0 collective-permute-start.6
  877.6 4.0 collective-permute-start.6
  922.6 4.0 collective-permute-start.6
  947.0 62.4 %all-reduce.6.cloned.1.call-done = (f32[2,128,1728]{1,2,0:T(8,128)}, f32[2,64,128]{2,1,0:T(8,128)}) async-done(((f32[2,128,1728]{1,2,0:T(8,128)}, f32[2,64,128]{2,1,0:T(8,128)}), (f32[2,128,1728]{1,2,0:T(8,128)}, f32[2,64,128]{2,1,0:T(8,128)})) %all-reduce.6.cloned.1.call-update) | async-done | bytes 1835024 | tf_op jit(solution)/shard_map/psum | solution.py:204
  (2103 shorter events, 734.4 us)
Async XLA Ops:
  7.2 1002.2 %all-reduce.6.cloned.1.call-start = ((), (), s32[]{:S(2)}) async-start(), calls=%async_computation | async-start | bytes 3670016 | tf_op jit(solution)/shard_map/psum | solution.py:204
  323.0 9.0 collective-permute-start.4
  341.8 8.1 collective-permute-start.6
  365.4 9.4 collective-permute-start.4
  385.0 8.1 collective-permute-start.6
  408.6 9.4 collective-permute-start.4
  428.2 8.1 collective-permute-start.6
  453.3 9.1 collective-permute-start.4
  456.8 6.6 collective-permute-start.3
  472.9 8.1 collective-permute-start.6
  498.2 9.1 collective-permute-start.4
  517.9 8.1 collective-permute-start.6
  543.2 9.1 collective-permute-start.4
  546.7 6.6 collective-permute-start.3
  562.8 8.1 collective-permute-start.6
  588.2 9.1 collective-permute-start.4
  607.8 8.1 collective-permute-start.6
  633.1 9.1 collective-permute-start.4
  636.7 6.6 collective-permute-start.3
  652.8 8.1 collective-permute-start.6
  678.1 9.1 collective-permute-start.4
  697.7 8.1 collective-permute-start.6
  723.1 9.1 collective-permute-start.4
  742.7 8.1 collective-permute-start.6
  768.0 9.1 collective-permute-start.4
  787.7 8.1 collective-permute-start.6
  813.0 9.1 collective-permute-start.4
  832.6 8.1 collective-permute-start.6
  858.0 9.1 collective-permute-start.4
  877.6 8.1 collective-permute-start.6
  902.9 9.1 collective-permute-start.4
  922.6 8.1 collective-permute-start.6
  (283 other events, 1616.6 us)
Sparse Core Ops, SparseCore 0:
  947.1 62.2 all-reduce.5
where the time goes:
time: 1030 us; the launch traced here: 1020 us
  starting transfers between devices  282 us (27%)
  local copies, waits for them, and re-layouts  263 us (26%)
  waiting for transfers between devices  240 us (23%)
  other arithmetic  92.1 us (9%)
  loops' own time  80.3 us (8%)
  matrix products  48 us (5%)
  between operations  14.2 us (1%)
    while x1484, local copies, waits for them, and re-layouts  189 us
    ppermute x42, starting transfers between devices, padded_2(): lax.ppermute(lax.slice_in_dim(block, block.shape[dim] - width, None, axis...  153 us
    ppermute x42, waiting for transfers between devices, padded_2(): lax.ppermute(lax.slice_in_dim(block, 0, width, axis=dim), axis, backward)  91.9 us
    ppermute x28, waiting for transfers between devices, from_behind(): return lax.ppermute(block, axis, route)  85.4 us
    ppermute x42, starting transfers between devices, padded_2(): lax.ppermute(lax.slice_in_dim(block, 0, width, axis=dim), axis, backward)  80.7 us
    psum x1, waiting for transfers between devices, per_device(): lax.psum((backward_state[2], backward_state[3]), 'space')  62.4 us
    concatenate x42, other arithmetic, padded_2(): block = jnp.concatenate([low, block, high], axis=dim)  53.2 us
    ppermute x28, starting transfers between devices, from_behind(): return lax.ppermute(block, axis, route)  48.3 us
  transfers between devices with their start and end apart: 113, of which 71 were waited for; matrix products, arithmetic and copies ran while one was open for 6% of the time, Pallas kernels for 0%

commit v1 on v0

v1 whole, which is shorter than its diff:
```python
import functools
import math

import jax
import jax.numpy as jnp
from jax import lax
from jax.experimental import pallas as pl
from jax.experimental.pallas import tpu as pltpu
from jax.sharding import PartitionSpec as P

BF = jnp.bfloat16
F32 = jnp.float32
NT = (((1,), (1,)), ((), ()))
NN = (((1,), (0,)), ((), ()))
TN = (((0,), (0,)), ((), ()))


def dot(a, b, dims):
    return lax.dot_general(a, b, dims, preferred_element_type=F32)


def swap_halves(x):
    return pltpu.roll(x, x.shape[1] // 2, 1)


def fold_piece(group, low, put):
    for dx in range(3):
        for dz in range(3):
            mid = 9 * dx + 3 + dz
            first, last = mid - 3, mid + 3
            at = 3 * dx + dz
            if mid % 2:
                row_one = jnp.where(low, group(first // 2), group(mid // 2))
                row_zero = swap_halves(jnp.where(low, group(last // 2), group(mid // 2)))
            else:
                row_zero = jnp.where(low, group(mid // 2), group(last // 2))
                row_one = swap_halves(jnp.where(low, group(mid // 2), group(first // 2)))
            put(at, row_zero, row_one)
    mixed = jnp.where(low, 0.0, group(13))
    put(9, swap_halves(mixed), mixed)


def unfold_terms(block, low):
    parts = {}
    for dx in range(3):
        for dz in range(3):
            mid = 9 * dx + 3 + dz
            zero, one = block(3 * dx + dz)
            if mid % 2:
                zero = swap_halves(zero)
            else:
                one = swap_halves(one)
            parts[mid] = zero + one
            parts[mid - 3] = one
            parts[mid + 3] = zero
    zero, one = block(9)
    parts[27] = swap_halves(zero) + one
    return [jnp.where(low, parts[2 * h], parts[2 * h + 1]) for h in range(14)]


def shifted(x, step, length):
    rows = x.shape[0]
    place = lax.broadcasted_iota(jnp.int32, x.shape, 0) % length
    edge = 0 if step > 0 else length - 1
    return jnp.where(place == edge, 0.0, pltpu.roll(x, step % rows, 0))


def fold_weights(me_ref, own_conv, own_mix, pieces, own_cat, folded, group_index):
    section, place, sections = me_ref[0], me_ref[1], folded.shape[0]
    hidden = own_cat.shape[0]
    shard = hidden // len(pieces)
    own_cat[:, : own_conv.shape[-1]] = own_conv[group_index, 0]
    own_cat[:, own_conv.shape[-1] :] = own_mix[group_index, 0].astype(F32).T.astype(BF)
    low = lax.broadcasted_iota(jnp.int32, (shard, 128), 1) < 64

    def one(layer, row, source):
        cache = {}

        def group(h):
            if h not in cache:
                cache[h] = source[:, 128 * h : 128 * h + 128].astype(F32)
            return cache[h]

        def put(at, zero, one_):
            folded[layer, pl.ds(row, shard), 128 * at : 128 * at + 128] = zero.astype(BF)
            folded[layer, pl.ds(hidden + row, shard), 128 * at : 128 * at + 128] = one_.astype(BF)

        fold_piece(group, low, put)

    def own_step(q, carry):
        row = pl.multiple_of(q * shard, shard)
        one(section, row, own_cat.at[pl.ds(row, shard)])
        return carry

    lax.fori_loop(0, len(pieces), own_step, 0)
    for rel, piece in enumerate(pieces):
        row = pl.multiple_of((place ^ rel) * shard, shard)

        def step(d, carry, piece=piece, row=row):
            layer = lax.rem(section + sections - 1 - d, sections)
            one(layer, row, piece.at[d])
            return carry

        lax.fori_loop(0, sections - 1, step, 0)


def columns_of(padded):
    planes = padded.shape[0] - 2
    parts = [padded[d : d + planes] for d in range(3)]
    return jnp.concatenate(parts, axis=2).reshape(planes * padded.shape[1], 3 * padded.shape[2])


def forward_layer(layer, section, act, padded, folded, slope, keep_a, keep_h):
    planes = padded.shape[0] - 2
    length = padded.shape[1]
    now = act[...]
    for at, value in enumerate((shifted(now, 1, length), now, shifted(now, -1, length))):
        padded[1 : planes + 1, :, 128 * at : 128 * at + 128] = value.astype(BF).reshape(planes, length, 128)
    pre = dot(columns_of(padded), folded[layer, :, :1152], NT)
    gate = jax.nn.sigmoid(pre)
    hidden = (pre * gate).astype(BF)
    slope[layer] = gate * (1.0 + pre * (1.0 - gate))
    act[...] = now + dot(hidden, folded[layer, :, 1152:], NN)

    @pl.when(layer == section)
    def _():
        keep_a[...] = padded[...]
        keep_h[...] = hidden


def backward_layer(layer, section, up, wide, folded, slope, keep_a, keep_h, terms, spread_if):
    planes = wide.shape[0] - 2
    length = wide.shape[1]
    now = up[...]
    up_low = now.astype(BF)
    grad = (dot(up_low, folded[layer, :, 1152:], NT) * slope[layer]).astype(BF)

    @pl.when(layer == section)
    def _():
        conv = dot(grad, columns_of(keep_a), TN)
        mix = dot(keep_h[...], up_low, TN)
        hidden = conv.shape[0] // 2
        low = lax.broadcasted_iota(jnp.int32, (hidden, 128), 1) < 64

        def block(at):
            full = mix if at == 9 else conv[:, 128 * at : 128 * at + 128]
            return full[:hidden], full[hidden:]

        for h, value in enumerate(unfold_terms(block, low)):
            terms[:, 128 * h : 128 * h + 128] = value

    def spread():
        wide[1 : planes + 1] = dot(grad, folded[layer, :, :1152], NN).reshape(planes, length, 1152)
        total = now
        for dz in range(3):
            part = 0.0
            for dx in range(3):
                at = 128 * (3 * dx + dz)
                part = part + wide[2 - dx : 2 - dx + planes, :, at : at + 128]
            part = part.reshape(planes * length, 128)
            total = total + (part if dz == 1 else shifted(part, dz - 1, length))
        up[...] = total

    if spread_if is None:
        spread()
    else:
        pl.when(spread_if)(spread)


def clear_edges(ref):
    ref[0] = jnp.zeros(ref.shape[1:], ref.dtype)
    ref[ref.shape[0] - 1] = jnp.zeros(ref.shape[1:], ref.dtype)


def place_planes(place, pieces, which, target):
    for rel, piece in enumerate(pieces):
        block = piece[which]
        rows = block.shape[0]
        target[pl.ds(pl.multiple_of((place ^ rel) * rows, rows), rows)] = block.astype(F32)


def first_kernel(shards, fields, me_ref, own_conv, own_mix, *refs):
    pieces, refs = refs[:shards], refs[shards:]
    planes, refs = refs[:fields], refs[fields:]
    act, folded, slope, keep_a, keep_h, own_cat, padded = refs
    fold_weights(me_ref, own_conv, own_mix, pieces, own_cat, folded, 0)
    place_planes(me_ref[1], planes, 0, act)
    clear_edges(padded)

    def step(layer, carry):
        forward_layer(layer, me_ref[0], act, padded, folded, slope, keep_a, keep_h)
        return carry

    lax.fori_loop(0, folded.shape[0], step, 0)


def store_terms(me_ref, terms, out):
    rows = out.shape[0]
    out[...] = terms[pl.ds(pl.multiple_of(me_ref[2] * rows, rows), rows)].astype(BF)


def middle_kernel(shards, fields, group_index, me_ref, own_conv, own_mix, act_in, *refs):
    pieces, refs = refs[:shards], refs[shards:]
    planes, refs = refs[:fields], refs[fields:]
    up, out, folded, slope, keep_a, keep_h, own_cat, padded, act, wide, terms = refs
    fold_weights(me_ref, own_conv, own_mix, pieces, own_cat, folded, group_index)
    act[...] = act_in[...]
    clear_edges(padded)
    clear_edges(wide)
    sections = folded.shape[0]

    def step(layer, carry):
        forward_layer(layer, me_ref[0], act, padded, folded, slope, keep_a, keep_h)
        return carry

    lax.fori_loop(0, sections, step, 0)
    place_planes(me_ref[1], planes, 1, up)

    def back(i, carry):
        backward_layer(sections - 1 - i, me_ref[0], up, wide, folded, slope, keep_a, keep_h, terms, None)
        return carry

    lax.fori_loop(0, sections, back, 0)
    store_terms(me_ref, terms, out)


def last_kernel(me_ref, up_in, folded, slope, keep_a, keep_h, out, up, wide, terms):
    up[...] = up_in[...]
    clear_edges(wide)
    sections = folded.shape[0]

    def back(i, carry):
        layer = sections - 1 - i
        backward_layer(layer, me_ref[0], up, wide, folded, slope, keep_a, keep_h, terms, layer > 0)
        return carry

    lax.fori_loop(0, sections, back, 0)
    store_terms(me_ref, terms, out)


def finish_kernel(groups, replicas, factor, me_ref, *refs):
    pieces, (conv, mix, whole) = refs[: groups * replicas], refs[groups * replicas :]
    wide = conv.shape[-1]
    for group in range(groups):
        for rel in range(replicas):
            piece = pieces[group * replicas + rel]
            rows = piece.shape[0]
            whole[pl.ds(pl.multiple_of((me_ref[2] ^ rel) * rows, rows), rows)] = piece[...].astype(F32) * factor
        conv[group, 0] = whole[:, :wide]
        mix[group, 0] = whole[:, wide:].T


def call(kernel, outs, scratch, smem, *args):
    vmem = pl.BlockSpec(memory_space=pltpu.VMEM)
    return pl.pallas_call(
        kernel,
        out_shape=outs,
        in_specs=[pl.BlockSpec(memory_space=pltpu.SMEM)] + [vmem] * len(args),
        out_specs=jax.tree.map(lambda _: vmem, outs),
        scratch_shapes=scratch,
        compiler_params=pltpu.CompilerParams(vmem_limit_bytes=60 * 1024 * 1024),
    )(smem, *args)


def exchange(block, axis, mask):
    count = lax.axis_size(axis)
    return lax.ppermute(block, axis, [(i, i ^ mask) for i in range(count)])


def per_device(inputs, cotangent, conv_weight, mix_weight):
    micro_count, channels, extent_x, extent_y, extent_z = inputs.shape
    layer_groups, _, hidden, taps = conv_weight.shape
    sections = lax.axis_size("section")
    space = lax.axis_size("space")
    section = lax.axis_index("section")
    place = lax.axis_index("space")
    replicas = space // micro_count
    shards = min(space, hidden // 16)
    shard = hidden // shards
    width = taps + channels
    cells = extent_x * space * extent_z
    lanes = extent_y * channels
    micro = place // replicas
    replica = place % replicas
    me = jnp.stack([section, place, replica]).astype(jnp.int32)

    start = (place % shards) * shard
    conv_rows = lax.dynamic_slice_in_dim(conv_weight[:, 0], start, shard, axis=1)
    mix_rows = lax.dynamic_slice_in_dim(jnp.swapaxes(mix_weight[:, 0], 1, 2), start, shard, axis=1)
    rows = jnp.concatenate([conv_rows, mix_rows], axis=2)
    gathered = []
    for group in range(layer_groups):
        mine = rows[group]
        route = [[(i, (i + d) % sections) for i in range(sections)] for d in range(1, sections)]
        passed = jnp.stack([lax.ppermute(mine, "section", r) for r in route])
        outer = [passed] + [exchange(passed, "space", 2 * k) for k in range(1, shards // 2)]
        pieces = []
        for piece in outer:
            pieces += [piece, exchange(piece, "space", 1)]
        gathered.append(pieces)

    both = jnp.stack([inputs, cotangent], axis=1)
    both = both.transpose(0, 1, 3, 5, 4, 2).reshape(micro_count, 2, extent_x * extent_z, lanes)
    near = []
    for k in range(micro_count):
        part = lax.dynamic_index_in_dim(both, micro ^ k, 0, keepdims=False)
        near.append(part if k == 0 else exchange(part, "space", k * replicas))
    near = jnp.stack(near)
    fields = [near] + [exchange(near, "space", r) for r in range(1, replicas)]
    planes = [fields[rel % replicas][rel // replicas] for rel in range(space)]

    def arr(*shape, dtype=F32):
        return jax.ShapeDtypeStruct(shape, dtype)

    def vm(shape):
        return pltpu.VMEM(shape.shape, shape.dtype)

    total_x = extent_x * space
    act = arr(cells, lanes)
    folded = arr(sections, 2 * hidden, 10 * lanes, dtype=BF)
    slope = arr(sections, cells, 2 * hidden)
    padded = arr(total_x + 2, extent_z, 3 * lanes, dtype=BF)
    keep_h = arr(cells, 2 * hidden, dtype=BF)
    own_cat = arr(hidden, width, dtype=BF)
    wide = arr(total_x + 2, extent_z, 9 * lanes)
    terms = arr(hidden, width)
    out = arr(hidden // replicas, width, dtype=BF)

    first = call(
        functools.partial(first_kernel, shards, space),
        [act, folded, slope, padded, keep_h],
        [vm(own_cat), vm(padded)],
        me, conv_weight, mix_weight, *gathered[0], *planes,
    )
    up, late = call(
        functools.partial(middle_kernel, shards, space, layer_groups - 1),
        [act, out],
        [vm(folded), vm(slope), vm(padded), vm(keep_h), vm(own_cat), vm(padded), vm(act), vm(wide), vm(terms)],
        me, conv_weight, mix_weight, first[0], *gathered[1], *planes,
    )
    early = call(last_kernel, out, [vm(act), vm(wide), vm(terms)], me, up, *first[1:])

    def reduce(part):
        level = [part] + [exchange(part, "space", k * replicas) for k in range(1, micro_count)]
        level = [x.astype(F32) for x in level]
        while len(level) > 1:
            level = [level[i] + level[i + 1] for i in range(0, len(level), 2)]
        mine = level[0].astype(BF)
        return [mine] + [exchange(mine, "space", r) for r in range(1, replicas)]

    pieces = []
    for part in (early, late):
        pieces += reduce(part)
    factor = 1.0 / math.sqrt(micro_count * cells * extent_y)
    return call(
        functools.partial(finish_kernel, layer_groups, replicas, factor),
        [arr(layer_groups, 1, hidden, taps), arr(layer_groups, 1, channels, hidden)],
        [vm(terms)],
        me, *pieces,
    )


def solution(mesh):
    placed = (
        P(None, None, "space", None, None),
        P(None, None, "space", None, None),
        P(None, "section", None, None),
        P(None, "section", None, None),
    )
    return jax.shard_map(
        per_device,
        mesh=mesh,
        in_specs=placed,
        out_specs=(P(None, "section", None, None), P(None, "section", None, None)),
        check_vma=False,
    )
```

time: 1030 us -> 105 us (0.10)
  local copies, waits for them, and re-layouts: 263 us -> 9.41 us
  starting transfers between devices: 282 us -> 40.7 us
  waiting for transfers between devices: 240 us -> 9.53 us
  other arithmetic: 92.1 us -> 1.94 us
  loops' own time: 80.3 us -> 0 us
  matrix products: 48 us -> 0 us
  Pallas kernels: 0 us -> 41.6 us
  between operations: 14.2 us -> 1.06 us
    ppermute x112 -> x32, starting transfers between devices: 282 us -> 40.7 us  [the longest x26 31.8 us: exchange(): return lax.ppermute(block, axis, [(i, i ^ mask) for i in range(count)])]
    while x1484 -> x0, local copies, waits for them, and re-layouts: 189 us -> none
    ppermute x112 -> x32, waiting for transfers between devices: 177 us -> 9.53 us  [the longest x26 8.36 us: exchange(): return lax.ppermute(block, axis, [(i, i ^ mask) for i in range(count)])]
    another operation x2 -> x0, loops' own time: 80.3 us -> none  [the longest x1 43.7 us: per_device(): lax.scan(backward_tick, (empty_field, empty_returned, conv_start, mix_sta...]
    psum x1 -> x0, waiting for transfers between devices: 62.4 us -> none  [per_device(): lax.psum((backward_state[2], backward_state[3]), 'space')]
    concatenate x42 -> x0, other arithmetic: 53.2 us -> none  [padded_2(): block = jnp.concatenate([low, block, high], axis=dim)]
    dot_general x84 -> x0, matrix products: 48 us -> none  [the longest x14 17.3 us: backward_tick(): conv_term = jnp.dot(pre_grad, window.T, preferred_element_type=jnp.float32)]
    pallas_call x0 -> x4, Pallas kernels: none -> 41.6 us  [call(): pl.pallas_call(kernel, out_shape=outs, in_specs=[pl.BlockSpec(memory_spac...]
  transfers between devices with their start and end apart: 113 -> 32, of which waited for: 71 -> 5; matrix products, arithmetic and copies ran while one was open for 6% -> 4% of each run, Pallas kernels for 0% -> 21%
where the time goes in v1:
time: 105 us; the launch traced here: 104 us
  Pallas kernels  41.6 us (40%)
  starting transfers between devices  40.7 us (39%)
  waiting for transfers between devices  9.53 us (9%)
  local copies, waits for them, and re-layouts  9.41 us (9%)
  other arithmetic  1.94 us (2%)
  between operations  1.06 us (1%)
    pallas_call x4, Pallas kernels, call(): pl.pallas_call(kernel, out_shape=outs, in_specs=[pl.BlockSpec(memory_spac...  41.6 us
    ppermute x26, starting transfers between devices, exchange(): return lax.ppermute(block, axis, [(i, i ^ mask) for i in range(count)])  31.8 us
    ppermute x6, starting transfers between devices, per_device(): passed = jnp.stack([lax.ppermute(mine, 'section', r) for r in route])  8.83 us
    ppermute x26, waiting for transfers between devices, exchange(): return lax.ppermute(block, axis, [(i, i ^ mask) for i in range(count)])  8.36 us
    unnamed x58, local copies, waits for them, and re-layouts  3.56 us
    pallas_call x1, local copies, waits for them, and re-layouts, call(): pl.pallas_call(kernel, out_shape=outs, in_specs=[pl.BlockSpec(memory_spac...  2.7 us
  transfers between devices with their start and end apart: 32, of which 5 were waited for; matrix products, arithmetic and copies ran while one was open for 4% of the time, Pallas kernels for 21%

profile of v1, /device:TPU:1, one launch (start us, length us, event | category | flops | bytes accessed | tf_op | source)
XLA Modules:
  0.0 104.2 jit_solution(5701063659670340448)
XLA Ops:
  0.7 1.5 %constant_dynamic-slice_fusion.5 = bf16[2,1,16,1728]{2,3,1,0:T(8,128)(2,1)S(1)} fusion(bf16[2,1,128,1728]{2,3,1,0:T(8,128)(2,1)} %param.6, s32[]{:T(128)S(6)} %select_n.34), kind=kLoop, calls=%fused_computation.23 | loop fusion | bytes 221188 | tf_op jit(solution)/shard_map/dynamic_slice | solution.py:288
  2.8 2.1 %collective-permute-start = (bf16[16,1792]{1,0:T(8,128)(2,1)S(1)}, bf16[16,1792]{1,0:T(8,128)(2,1)S(1)}, u32[]{:S(2)}, u32[]{:S(2)}) collective-permute-start(bf16[16,1792]{1,0:T(8,128)(2,1)S(1)} %get-tuple-element.29), channel_id=1, source_target_pairs={{0,8},{8,16},{16,24},{24,0},{1,9},{9,17},{17,25},{25,1},{2,10},{10... | collective-permute-start | bytes 172040 | tf_op jit(solution)/shard_map/ppermute | solution.py:295
  4.9 2.3 %collective-permute-start.1 = (bf16[16,1792]{1,0:T(8,128)(2,1)S(1)}, bf16[16,1792]{1,0:T(8,128)(2,1)S(1)}, u32[]{:S(2)}, u32[]{:S(2)}) collective-permute-start(bf16[16,1792]{1,0:T(8,128)(2,1)S(1)} %get-tuple-element.29), channel_id=1, source_target_pairs={{0,16},{8,24},{16,0},{24,8},{1,17},{9,25},{17,1},{25,9},{2,18},{10... | collective-permute-start | bytes 172040 | tf_op jit(solution)/shard_map/ppermute | solution.py:295
  7.2 1.1 %collective-permute-start.2 = (bf16[16,1792]{1,0:T(8,128)(2,1)S(1)}, bf16[16,1792]{1,0:T(8,128)(2,1)S(1)}, u32[]{:S(2)}, u32[]{:S(2)}) collective-permute-start(bf16[16,1792]{1,0:T(8,128)(2,1)S(1)} %get-tuple-element.29), channel_id=1, source_target_pairs={{0,24},{8,0},{16,8},{24,16},{1,25},{9,1},{17,9},{25,17},{2,26},{10... | collective-permute-start | bytes 172040 | tf_op jit(solution)/shard_map/ppermute | solution.py:295
  9.4 2.9 %collective-permute-start.16 = (bf16[16,1792]{1,0:T(8,128)(2,1)S(1)}, bf16[16,1792]{1,0:T(8,128)(2,1)S(1)}, u32[]{:S(2)}, u32[]{:S(2)}) collective-permute-start(bf16[16,1792]{1,0:T(8,128)(2,1)S(1)} %get-tuple-element.28), channel_id=1, source_target_pairs={{0,24},{8,0},{16,8},{24,16},{1,25},{9,1},{17,9},{25,17},{2,26},{10... | collective-permute-start | bytes 172040 | tf_op jit(solution)/shard_map/ppermute | solution.py:295
  12.3 1.2 %collective-permute-start.10 = (bf16[2,128,128]{2,1,0:T(8,128)(2,1)S(1)}, bf16[2,128,128]{2,1,0:T(8,128)(2,1)S(1)}, u32[]{:S(2)}, u32[]{:S(2)}) collective-permute-start(bf16[2,128,128]{2,1,0:T(8,128)(2,1)S(1)} %bitcast.48), channel_id=1, source_target_pairs={{0,2},{1,3},{2,0},{3,1},{4,6},{5,7},{6,4},{7,5},{8,10},{9,11},{10,... | collective-permute-start | bytes 196616 | tf_op jit(solution)/shard_map/ppermute | solution.py:267
  13.5 1.2 %collective-permute-start.11 = (bf16[2,128,128]{2,1,0:T(8,128)(2,1)S(1)}, bf16[2,128,128]{2,1,0:T(8,128)(2,1)S(1)}, u32[]{:S(2)}, u32[]{:S(2)}) collective-permute-start(bf16[2,128,128]{2,1,0:T(8,128)(2,1)S(1)} %bitcast.47), channel_id=1, source_target_pairs={{0,4},{1,5},{2,6},{3,7},{4,0},{5,1},{6,2},{7,3},{8,12},{9,13},{10,... | collective-permute-start | bytes 196616 | tf_op jit(solution)/shard_map/ppermute | solution.py:267
  15.4 1.2 %collective-permute-done.15 = bf16[16,1792]{1,0:T(8,128)(2,1)S(1)} collective-permute-done((bf16[16,1792]{1,0:T(8,128)(2,1)S(1)}, bf16[16,1792]{1,0:T(8,128)(2,1)S(1)}, u32[]{:S(2)}, u32[]{:S(2)}) %collective-permute-start.15) | collective-permute-done | bytes 57376 | tf_op jit(solution)/shard_map/ppermute | solution.py:295
  16.5 0.9 collective-permute-start.4
  17.5 1.2 %collective-permute-start.6 = (bf16[3,16,1792]{2,1,0:T(8,128)(2,1)S(1)}, bf16[3,16,1792]{2,1,0:T(8,128)(2,1)S(1)}, u32[]{:S(2)}, u32[]{:S(2)}) collective-permute-start(bf16[3,16,1792]{2,1,0:T(8,128)(2,1)S(1)} %pad_maximum_fusion.2.refs_0_), channel_id=1, source_target_pairs={{0,4},{1,5},{2,6},{3,7},{4,0},{5,1},{6,2},{7,3},{8,12},{9,13},{10,... | collective-permute-start | bytes 516104 | tf_op jit(solution)/shard_map/ppermute | solution.py:267
  19.3 2.6 %collective-permute-start.3 = (bf16[3,16,1792]{2,1,0:T(8,128)(2,1)S(1)}, bf16[3,16,1792]{2,1,0:T(8,128)(2,1)S(1)}, u32[]{:S(2)}, u32[]{:S(2)}) collective-permute-start(bf16[3,16,1792]{2,1,0:T(8,128)(2,1)S(1)} %pad_maximum_fusion.2.refs_0_), channel_id=1, source_target_pairs={{0,1},{1,0},{2,3},{3,2},{4,5},{5,4},{6,7},{7,6},{8,9},{9,8},{10,11... | collective-permute-start | bytes 516104 | tf_op jit(solution)/shard_map/ppermute | solution.py:267
  22.0 0.8 collective-permute-start.18
  22.9 3.3 %collective-permute-start.13 = (bf16[4,2,128,128]{3,2,1,0:T(8,128)(2,1)S(1)}, bf16[4,2,128,128]{3,2,1,0:T(8,128)(2,1)S(1)}, u32[]{:S(2)}, u32[]{:S(2)}) collective-permute-start(bf16[4,2,128,128]{3,2,1,0:T(8,128)(2,1)S(1)} %pad_maximum_fusion.1), channel_id=1, source_target_pairs={{0,1},{1,0},{2,3},{3,2},{4,5},{5,4},{6,7},{7,6},{8,9},{9,8},{10,11... | collective-permute-start | bytes 786440 | tf_op jit(solution)/shard_map/ppermute | solution.py:267
  26.1 0.7 collective-permute-start.20
  26.9 1.0 collective-permute-start.22
  27.9 3.7 %collective-permute-start.5 = (bf16[3,16,1792]{2,1,0:T(8,128)(2,1)S(1)}, bf16[3,16,1792]{2,1,0:T(8,128)(2,1)S(1)}, u32[]{:S(2)}, u32[]{:S(2)}) collective-permute-start(bf16[3,16,1792]{2,1,0:T(8,128)(2,1)S(1)} %collective-permute-done.4.refs_2_), channel_id=1, source_target_pairs={{0,1},{1,0},{2,3},{3,2},{4,5},{5,4},{6,7},{7,6},{8,9},{9,8},{10,11... | collective-permute-start | bytes 516104 | tf_op jit(solution)/shard_map/ppermute | solution.py:267
  32.3 1.3 %copy.21.own_conv = bf16[2,1,128,1728]{3,2,1,0:T(8,128)(2,1)} copy(bf16[2,1,128,1728]{2,3,1,0:T(8,128)(2,1)S(1)} %copy-done) | data formatting | bytes 1769472 | tf_op args[2]
  34.2 2.9 %collective-permute-start.17 = (bf16[3,16,1792]{2,1,0:T(8,128)(2,1)S(1)}, bf16[3,16,1792]{2,1,0:T(8,128)(2,1)S(1)}, u32[]{:S(2)}, u32[]{:S(2)}) collective-permute-start(bf16[3,16,1792]{2,1,0:T(8,128)(2,1)S(1)} %pad_maximum_fusion.3.refs_0_), channel_id=1, source_target_pairs={{0,1},{1,0},{2,3},{3,2},{4,5},{5,4},{6,7},{7,6},{8,9},{9,8},{10,11... | collective-permute-start | bytes 516104 | tf_op jit(solution)/shard_map/ppermute | solution.py:267
  39.6 13.2 %shard_map.59 = (f32[1024,128]{1,0:T(8,128)}, bf16[4,256,1280]{2,1,0:T(8,128)(2,1)}, f32[4,1024,256]{2,1,0:T(8,128)}, bf16[10,128,384]{2,1,0:T(8,128)(2,1)}, bf16[1024,256]{1,0:T(8,128)(2,1)}) custom-call(s32[3]{0:T(128)} %pad_add_fusion.me_ref, bf16[2,1,128,1728]{3,2,1,0:T(8,128)(2,1)} %copy.21.own_conv, bf16[2,1,64,128]{3,2,1,0:T(8,128)(2,1)} %own_mix.3, ...), custom_call_target="tpu_custom_call" | custom-call | tf_op jit(solution)/shard_map/pallas_call | solution.py:255
  53.7 16.4 %shard_map.60 = (f32[1024,128]{1,0:T(8,128)}, bf16[64,1792]{1,0:T(8,128)(2,1)}) custom-call(s32[3]{0:T(128)} %pad_add_fusion.me_ref, bf16[2,1,128,1728]{3,2,1,0:T(8,128)(2,1)} %copy.21.own_conv, bf16[2,1,64,128]{3,2,1,0:T(8,128)(2,1)} %own_mix.3, f32[1024,128]{1,0:T(8,128)} %get-tuple-element.9.act_in, bf16[3,16,1792]{2,1,0:T(8,128)(2,1)} %copy-done.4, ...), custom_call_target="tpu_custom_call" | custom-call | tf_op jit(solution)/shard_map/pallas_call | solution.py:255
  70.8 0.7 collective-permute-start.29
  71.5 1.2 %collective-permute-start.30 = (bf16[64,1792]{1,0:T(8,128)(2,1)}, bf16[64,1792]{1,0:T(8,128)(2,1)S(1)}, u32[]{:S(2)}, u32[]{:S(2)}) collective-permute-start(bf16[64,1792]{1,0:T(8,128)(2,1)} %get-tuple-element.15), channel_id=1, source_target_pairs={{0,6},{1,7},{2,4},{3,5},{4,2},{5,3},{6,0},{7,1},{8,14},{9,15},{10,... | collective-permute-start | bytes 688136 | tf_op jit(solution)/shard_map/ppermute | solution.py:267
  72.7 9.1 %shard_map.61 = bf16[64,1792]{1,0:T(8,128)(2,1)} custom-call(s32[3]{0:T(128)} %pad_add_fusion.me_ref, f32[1024,128]{1,0:T(8,128)} %get-tuple-element.10.up_in, bf16[4,256,1280]{2,1,0:T(8,128)(2,1)} %get-tuple-element.11.folded, f32[4,1024,256]{2,1,0:T(8,128)} %get-tuple-element.12.slope, bf16[10,128,384]{2,1,0:T(8,128)(2,1)} %get-tuple-element.13.keep_a, ...), custom_call_target="tpu_custom_call" | custom-call | tf_op jit(solution)/shard_map/pallas_call | solution.py:255
  83.3 1.2 %collective-permute-start.26 = (bf16[64,1792]{1,0:T(8,128)(2,1)}, bf16[64,1792]{1,0:T(8,128)(2,1)S(1)}, u32[]{:S(2)}, u32[]{:S(2)}) collective-permute-start(bf16[64,1792]{1,0:T(8,128)(2,1)} %shard_map.61), channel_id=1, source_target_pairs={{0,6},{1,7},{2,4},{3,5},{4,2},{5,3},{6,0},{7,1},{8,14},{9,15},{10,... | collective-permute-start | bytes 688136 | tf_op jit(solution)/shard_map/ppermute | solution.py:267
  84.6 1.8 %collective-permute-start.31 = (bf16[64,1792]{1,0:T(8,128)(2,1)S(1)}, bf16[64,1792]{1,0:T(8,128)(2,1)S(1)}, u32[]{:S(2)}, u32[]{:S(2)}) collective-permute-start(bf16[64,1792]{1,0:T(8,128)(2,1)S(1)} %add_convert_fusion.refs_2_), channel_id=1, source_target_pairs={{0,1},{1,0},{2,3},{3,2},{4,5},{5,4},{6,7},{7,6},{8,9},{9,8},{10,11... | collective-permute-start | bytes 688136 | tf_op jit(solution)/shard_map/ppermute | solution.py:267
  86.4 1.8 %collective-permute-done.24 = bf16[64,1792]{1,0:T(8,128)(2,1)S(1)} collective-permute-done((bf16[64,1792]{1,0:T(8,128)(2,1)}, bf16[64,1792]{1,0:T(8,128)(2,1)S(1)}, u32[]{:S(2)}, u32[]{:S(2)}) %collective-permute-start.24) | collective-permute-done | bytes 229408 | tf_op jit(solution)/shard_map/ppermute | solution.py:267
  88.6 5.0 %collective-permute-done.26 = bf16[64,1792]{1,0:T(8,128)(2,1)S(1)} collective-permute-done((bf16[64,1792]{1,0:T(8,128)(2,1)}, bf16[64,1792]{1,0:T(8,128)(2,1)S(1)}, u32[]{:S(2)}, u32[]{:S(2)}) %collective-permute-start.26) | collective-permute-done | bytes 229408 | tf_op jit(solution)/shard_map/ppermute | solution.py:267
  93.6 1.1 %add_convert_fusion.1.refs_0_ = bf16[64,1792]{1,0:T(8,128)(2,1)S(1)} fusion(bf16[64,1792]{1,0:T(8,128)(2,1)S(1)} %collective-permute-done.26, bf16[64,1792]{1,0:T(8,128)(2,1)S(1)} %collective-permute-done.25, bf16[64,1792]{1,0:T(8,128)(2,1)S(1)} %collective-permute-done.24, bf16[64,1792]{1,0:T(8,128)(2,1)} %shard_map.61), kind=kLoop, calls=%fused_computation.1 | loop fusion | flops 917504 | bytes 1146880 | tf_op jit(solution)/shard_map/convert_element_type | solution.py:348
  94.7 2.1 %collective-permute-start.27 = (bf16[64,1792]{1,0:T(8,128)(2,1)S(1)}, bf16[64,1792]{1,0:T(8,128)(2,1)S(1)}, u32[]{:S(2)}, u32[]{:S(2)}) collective-permute-start(bf16[64,1792]{1,0:T(8,128)(2,1)S(1)} %add_convert_fusion.1.refs_0_), channel_id=1, source_target_pairs={{0,1},{1,0},{2,3},{3,2},{4,5},{5,4},{6,7},{7,6},{8,9},{9,8},{10,11... | collective-permute-start | bytes 688136 | tf_op jit(solution)/shard_map/ppermute | solution.py:267
  96.8 1.1 %collective-permute-done.27.refs_1_ = bf16[64,1792]{1,0:T(8,128)(2,1)S(1)} collective-permute-done((bf16[64,1792]{1,0:T(8,128)(2,1)S(1)}, bf16[64,1792]{1,0:T(8,128)(2,1)S(1)}, u32[]{:S(2)}, u32[]{:S(2)}) %collective-permute-start.27) | collective-permute-done | bytes 229408 | tf_op jit(solution)/shard_map/ppermute | solution.py:267
  98.6 2.9 %shard_map.62 = (f32[2,1,128,1728]{3,2,1,0:T(8,128)}, f32[2,1,64,128]{3,2,1,0:T(8,128)}) custom-call(s32[3]{0:T(128)} %pad_add_fusion.me_ref, bf16[64,1792]{1,0:T(8,128)(2,1)} %copy-done.3, bf16[64,1792]{1,0:T(8,128)(2,1)} %copy-done.11, bf16[64,1792]{1,0:T(8,128)(2,1)} %copy-done.2, bf16[64,1792]{1,0:T(8,128)(2,1)} %copy-done.10), custom_call_target="tpu_custom_call" | custom-call | tf_op jit(solution)/shard_map/pallas_call | solution.py:255
  101.5 2.7 %copy.22 = f32[2,1,128,1728]{2,3,1,0:T(8,128)} copy(f32[2,1,128,1728]{3,2,1,0:T(8,128)} %get-tuple-element.18) | data formatting | bytes 3538944 | tf_op jit(solution)/shard_map/pallas_call | solution.py:255
  (113 shorter events, 10.7 us)
Async XLA Ops:
  2.8 6.6 %collective-permute-start = (bf16[16,1792]{1,0:T(8,128)(2,1)S(1)}, bf16[16,1792]{1,0:T(8,128)(2,1)S(1)}, u32[]{:S(2)}, u32[]{:S(2)}) collective-permute-start(bf16[16,1792]{1,0:T(8,128)(2,1)S(1)} %get-tuple-element.29), channel_id=1, source_target_pairs={{0,8},{8,16},{16,24},{24,0},{1,9},{9,17},{17,25},{25,1},{2,10},{10... | collective-permute-start | bytes 172040 | tf_op jit(solution)/shard_map/ppermute | solution.py:295
  4.9 7.4 %collective-permute-start.1 = (bf16[16,1792]{1,0:T(8,128)(2,1)S(1)}, bf16[16,1792]{1,0:T(8,128)(2,1)S(1)}, u32[]{:S(2)}, u32[]{:S(2)}) collective-permute-start(bf16[16,1792]{1,0:T(8,128)(2,1)S(1)} %get-tuple-element.29), channel_id=1, source_target_pairs={{0,16},{8,24},{16,0},{24,8},{1,17},{9,25},{17,1},{25,9},{2,18},{10... | collective-permute-start | bytes 172040 | tf_op jit(solution)/shard_map/ppermute | solution.py:295
  7.2 6.3 %collective-permute-start.2 = (bf16[16,1792]{1,0:T(8,128)(2,1)S(1)}, bf16[16,1792]{1,0:T(8,128)(2,1)S(1)}, u32[]{:S(2)}, u32[]{:S(2)}) collective-permute-start(bf16[16,1792]{1,0:T(8,128)(2,1)S(1)} %get-tuple-element.29), channel_id=1, source_target_pairs={{0,24},{8,0},{16,8},{24,16},{1,25},{9,1},{17,9},{25,17},{2,26},{10... | collective-permute-start | bytes 172040 | tf_op jit(solution)/shard_map/ppermute | solution.py:295
  8.3 6.5 %collective-permute-start.14 = (bf16[16,1792]{1,0:T(8,128)(2,1)S(1)}, bf16[16,1792]{1,0:T(8,128)(2,1)S(1)}, u32[]{:S(2)}, u32[]{:S(2)}) collective-permute-start(bf16[16,1792]{1,0:T(8,128)(2,1)S(1)} %get-tuple-element.28), channel_id=1, source_target_pairs={{0,8},{8,16},{16,24},{24,0},{1,9},{9,17},{17,25},{25,1},{2,10},{10... | collective-permute-start | bytes 172040 | tf_op jit(solution)/shard_map/ppermute | solution.py:295
  8.7 7.9 %collective-permute-start.15 = (bf16[16,1792]{1,0:T(8,128)(2,1)S(1)}, bf16[16,1792]{1,0:T(8,128)(2,1)S(1)}, u32[]{:S(2)}, u32[]{:S(2)}) collective-permute-start(bf16[16,1792]{1,0:T(8,128)(2,1)S(1)} %get-tuple-element.28), channel_id=1, source_target_pairs={{0,16},{8,24},{16,0},{24,8},{1,17},{9,25},{17,1},{25,9},{2,18},{10... | collective-permute-start | bytes 172040 | tf_op jit(solution)/shard_map/ppermute | solution.py:295
  9.4 8.1 %collective-permute-start.16 = (bf16[16,1792]{1,0:T(8,128)(2,1)S(1)}, bf16[16,1792]{1,0:T(8,128)(2,1)S(1)}, u32[]{:S(2)}, u32[]{:S(2)}) collective-permute-start(bf16[16,1792]{1,0:T(8,128)(2,1)S(1)} %get-tuple-element.28), channel_id=1, source_target_pairs={{0,24},{8,0},{16,8},{24,16},{1,25},{9,1},{17,9},{25,17},{2,26},{10... | collective-permute-start | bytes 172040 | tf_op jit(solution)/shard_map/ppermute | solution.py:295
  12.3 6.5 %collective-permute-start.10 = (bf16[2,128,128]{2,1,0:T(8,128)(2,1)S(1)}, bf16[2,128,128]{2,1,0:T(8,128)(2,1)S(1)}, u32[]{:S(2)}, u32[]{:S(2)}) collective-permute-start(bf16[2,128,128]{2,1,0:T(8,128)(2,1)S(1)} %bitcast.48), channel_id=1, source_target_pairs={{0,2},{1,3},{2,0},{3,1},{4,6},{5,7},{6,4},{7,5},{8,10},{9,11},{10,... | collective-permute-start | bytes 196616 | tf_op jit(solution)/shard_map/ppermute | solution.py:267
  13.5 5.8 %collective-permute-start.11 = (bf16[2,128,128]{2,1,0:T(8,128)(2,1)S(1)}, bf16[2,128,128]{2,1,0:T(8,128)(2,1)S(1)}, u32[]{:S(2)}, u32[]{:S(2)}) collective-permute-start(bf16[2,128,128]{2,1,0:T(8,128)(2,1)S(1)} %bitcast.47), channel_id=1, source_target_pairs={{0,4},{1,5},{2,6},{3,7},{4,0},{5,1},{6,2},{7,3},{8,12},{9,13},{10,... | collective-permute-start | bytes 196616 | tf_op jit(solution)/shard_map/ppermute | solution.py:267
  14.8 7.2 %collective-permute-start.12 = (bf16[2,128,128]{2,1,0:T(8,128)(2,1)S(1)}, bf16[2,128,128]{2,1,0:T(8,128)(2,1)S(1)}, u32[]{:S(2)}, u32[]{:S(2)}) collective-permute-start(bf16[2,128,128]{2,1,0:T(8,128)(2,1)S(1)} %bitcast.46), channel_id=1, source_target_pairs={{0,6},{1,7},{2,4},{3,5},{4,2},{5,3},{6,0},{7,1},{8,14},{9,15},{10,... | collective-permute-start | bytes 196616 | tf_op jit(solution)/shard_map/ppermute | solution.py:267
  16.5 6.3 %collective-permute-start.4 = (bf16[3,16,1792]{2,1,0:T(8,128)(2,1)S(1)}, bf16[3,16,1792]{2,1,0:T(8,128)(2,1)S(1)}, u32[]{:S(2)}, u32[]{:S(2)}) collective-permute-start(bf16[3,16,1792]{2,1,0:T(8,128)(2,1)S(1)} %pad_maximum_fusion.2.refs_0_), channel_id=1, source_target_pairs={{0,2},{1,3},{2,0},{3,1},{4,6},{5,7},{6,4},{7,5},{8,10},{9,11},{10,... | collective-permute-start | bytes 516104 | tf_op jit(solution)/shard_map/ppermute | solution.py:267
  17.5 8.7 %collective-permute-start.6 = (bf16[3,16,1792]{2,1,0:T(8,128)(2,1)S(1)}, bf16[3,16,1792]{2,1,0:T(8,128)(2,1)S(1)}, u32[]{:S(2)}, u32[]{:S(2)}) collective-permute-start(bf16[3,16,1792]{2,1,0:T(8,128)(2,1)S(1)} %pad_maximum_fusion.2.refs_0_), channel_id=1, source_target_pairs={{0,4},{1,5},{2,6},{3,7},{4,0},{5,1},{6,2},{7,3},{8,12},{9,13},{10,... | collective-permute-start | bytes 516104 | tf_op jit(solution)/shard_map/ppermute | solution.py:267
  18.8 8.1 %collective-permute-start.8 = (bf16[3,16,1792]{2,1,0:T(8,128)(2,1)S(1)}, bf16[3,16,1792]{2,1,0:T(8,128)(2,1)S(1)}, u32[]{:S(2)}, u32[]{:S(2)}) collective-permute-start(bf16[3,16,1792]{2,1,0:T(8,128)(2,1)S(1)} %pad_maximum_fusion.2.refs_0_), channel_id=1, source_target_pairs={{0,6},{1,7},{2,4},{3,5},{4,2},{5,3},{6,0},{7,1},{8,14},{9,15},{10,... | collective-permute-start | bytes 516104 | tf_op jit(solution)/shard_map/ppermute | solution.py:267
  19.3 8.6 %collective-permute-start.3 = (bf16[3,16,1792]{2,1,0:T(8,128)(2,1)S(1)}, bf16[3,16,1792]{2,1,0:T(8,128)(2,1)S(1)}, u32[]{:S(2)}, u32[]{:S(2)}) collective-permute-start(bf16[3,16,1792]{2,1,0:T(8,128)(2,1)S(1)} %pad_maximum_fusion.2.refs_0_), channel_id=1, source_target_pairs={{0,1},{1,0},{2,3},{3,2},{4,5},{5,4},{6,7},{7,6},{8,9},{9,8},{10,11... | collective-permute-start | bytes 516104 | tf_op jit(solution)/shard_map/ppermute | solution.py:267
  22.0 9.6 %collective-permute-start.18 = (bf16[3,16,1792]{2,1,0:T(8,128)(2,1)S(1)}, bf16[3,16,1792]{2,1,0:T(8,128)(2,1)S(1)}, u32[]{:S(2)}, u32[]{:S(2)}) collective-permute-start(bf16[3,16,1792]{2,1,0:T(8,128)(2,1)S(1)} %pad_maximum_fusion.3.refs_0_), channel_id=1, source_target_pairs={{0,2},{1,3},{2,0},{3,1},{4,6},{5,7},{6,4},{7,5},{8,10},{9,11},{10,... | collective-permute-start | bytes 516104 | tf_op jit(solution)/shard_map/ppermute | solution.py:267
  22.9 14.4 %collective-permute-start.13 = (bf16[4,2,128,128]{3,2,1,0:T(8,128)(2,1)S(1)}, bf16[4,2,128,128]{3,2,1,0:T(8,128)(2,1)S(1)}, u32[]{:S(2)}, u32[]{:S(2)}) collective-permute-start(bf16[4,2,128,128]{3,2,1,0:T(8,128)(2,1)S(1)} %pad_maximum_fusion.1), channel_id=1, source_target_pairs={{0,1},{1,0},{2,3},{3,2},{4,5},{5,4},{6,7},{7,6},{8,9},{9,8},{10,11... | collective-permute-start | bytes 786440 | tf_op jit(solution)/shard_map/ppermute | solution.py:267
  26.1 8.1 %collective-permute-start.20 = (bf16[3,16,1792]{2,1,0:T(8,128)(2,1)S(1)}, bf16[3,16,1792]{2,1,0:T(8,128)(2,1)S(1)}, u32[]{:S(2)}, u32[]{:S(2)}) collective-permute-start(bf16[3,16,1792]{2,1,0:T(8,128)(2,1)S(1)} %pad_maximum_fusion.3.refs_0_), channel_id=1, source_target_pairs={{0,4},{1,5},{2,6},{3,7},{4,0},{5,1},{6,2},{7,3},{8,12},{9,13},{10,... | collective-permute-start | bytes 516104 | tf_op jit(solution)/shard_map/ppermute | solution.py:267
  26.9 10.3 %collective-permute-start.22 = (bf16[3,16,1792]{2,1,0:T(8,128)(2,1)S(1)}, bf16[3,16,1792]{2,1,0:T(8,128)(2,1)S(1)}, u32[]{:S(2)}, u32[]{:S(2)}) collective-permute-start(bf16[3,16,1792]{2,1,0:T(8,128)(2,1)S(1)} %pad_maximum_fusion.3.refs_0_), channel_id=1, source_target_pairs={{0,6},{1,7},{2,4},{3,5},{4,2},{5,3},{6,0},{7,1},{8,14},{9,15},{10,... | collective-permute-start | bytes 516104 | tf_op jit(solution)/shard_map/ppermute | solution.py:267
  27.9 9.7 %collective-permute-start.5 = (bf16[3,16,1792]{2,1,0:T(8,128)(2,1)S(1)}, bf16[3,16,1792]{2,1,0:T(8,128)(2,1)S(1)}, u32[]{:S(2)}, u32[]{:S(2)}) collective-permute-start(bf16[3,16,1792]{2,1,0:T(8,128)(2,1)S(1)} %collective-permute-done.4.refs_2_), channel_id=1, source_target_pairs={{0,1},{1,0},{2,3},{3,2},{4,5},{5,4},{6,7},{7,6},{8,9},{9,8},{10,11... | collective-permute-start | bytes 516104 | tf_op jit(solution)/shard_map/ppermute | solution.py:267
  31.6 6.2 %collective-permute-start.7 = (bf16[3,16,1792]{2,1,0:T(8,128)(2,1)S(1)}, bf16[3,16,1792]{2,1,0:T(8,128)(2,1)}, u32[]{:S(2)}, u32[]{:S(2)}) collective-permute-start(bf16[3,16,1792]{2,1,0:T(8,128)(2,1)S(1)} %collective-permute-done.6.refs_4_), channel_id=1, source_target_pairs={{0,1},{1,0},{2,3},{3,2},{4,5},{5,4},{6,7},{7,6},{8,9},{9,8},{10,11... | collective-permute-start | bytes 516104 | tf_op jit(solution)/shard_map/ppermute | solution.py:267
  34.2 18.6 %collective-permute-start.17 = (bf16[3,16,1792]{2,1,0:T(8,128)(2,1)S(1)}, bf16[3,16,1792]{2,1,0:T(8,128)(2,1)S(1)}, u32[]{:S(2)}, u32[]{:S(2)}) collective-permute-start(bf16[3,16,1792]{2,1,0:T(8,128)(2,1)S(1)} %pad_maximum_fusion.3.refs_0_), channel_id=1, source_target_pairs={{0,1},{1,0},{2,3},{3,2},{4,5},{5,4},{6,7},{7,6},{8,9},{9,8},{10,11... | collective-permute-start | bytes 516104 | tf_op jit(solution)/shard_map/ppermute | solution.py:267
  37.2 1.8 %collective-permute-start.9 = (bf16[3,16,1792]{2,1,0:T(8,128)(2,1)S(1)}, bf16[3,16,1792]{2,1,0:T(8,128)(2,1)S(1)}, u32[]{:S(2)}, u32[]{:S(2)}) collective-permute-start(bf16[3,16,1792]{2,1,0:T(8,128)(2,1)S(1)} %collective-permute-done.8.refs_6_), channel_id=1, source_target_pairs={{0,1},{1,0},{2,3},{3,2},{4,5},{5,4},{6,7},{7,6},{8,9},{9,8},{10,11... | collective-permute-start | bytes 516104 | tf_op jit(solution)/shard_map/ppermute | solution.py:267
  37.2 15.6 %collective-permute-start.19 = (bf16[3,16,1792]{2,1,0:T(8,128)(2,1)S(1)}, bf16[3,16,1792]{2,1,0:T(8,128)(2,1)S(1)}, u32[]{:S(2)}, u32[]{:S(2)}) collective-permute-start(bf16[3,16,1792]{2,1,0:T(8,128)(2,1)S(1)} %collective-permute-done.18.refs_2_), channel_id=1, source_target_pairs={{0,1},{1,0},{2,3},{3,2},{4,5},{5,4},{6,7},{7,6},{8,9},{9,8},{10,11... | collective-permute-start | bytes 516104 | tf_op jit(solution)/shard_map/ppermute | solution.py:267
  37.7 15.2 %collective-permute-start.21 = (bf16[3,16,1792]{2,1,0:T(8,128)(2,1)S(1)}, bf16[3,16,1792]{2,1,0:T(8,128)(2,1)S(1)}, u32[]{:S(2)}, u32[]{:S(2)}) collective-permute-start(bf16[3,16,1792]{2,1,0:T(8,128)(2,1)S(1)} %collective-permute-done.20.refs_4_), channel_id=1, source_target_pairs={{0,1},{1,0},{2,3},{3,2},{4,5},{5,4},{6,7},{7,6},{8,9},{9,8},{10,11... | collective-permute-start | bytes 516104 | tf_op jit(solution)/shard_map/ppermute | solution.py:267
  37.8 15.1 %collective-permute-start.23 = (bf16[3,16,1792]{2,1,0:T(8,128)(2,1)S(1)}, bf16[3,16,1792]{2,1,0:T(8,128)(2,1)S(1)}, u32[]{:S(2)}, u32[]{:S(2)}) collective-permute-start(bf16[3,16,1792]{2,1,0:T(8,128)(2,1)S(1)} %collective-permute-done.22.refs_6_), channel_id=1, source_target_pairs={{0,1},{1,0},{2,3},{3,2},{4,5},{5,4},{6,7},{7,6},{8,9},{9,8},{10,11... | collective-permute-start | bytes 516104 | tf_op jit(solution)/shard_map/ppermute | solution.py:267
  70.0 13.2 %collective-permute-start.28 = (bf16[64,1792]{1,0:T(8,128)(2,1)}, bf16[64,1792]{1,0:T(8,128)(2,1)S(1)}, u32[]{:S(2)}, u32[]{:S(2)}) collective-permute-start(bf16[64,1792]{1,0:T(8,128)(2,1)} %get-tuple-element.15), channel_id=1, source_target_pairs={{0,2},{1,3},{2,0},{3,1},{4,6},{5,7},{6,4},{7,5},{8,10},{9,11},{10,... | collective-permute-start | bytes 688136 | tf_op jit(solution)/shard_map/ppermute | solution.py:267
  70.8 13.7 %collective-permute-start.29 = (bf16[64,1792]{1,0:T(8,128)(2,1)}, bf16[64,1792]{1,0:T(8,128)(2,1)S(1)}, u32[]{:S(2)}, u32[]{:S(2)}) collective-permute-start(bf16[64,1792]{1,0:T(8,128)(2,1)} %get-tuple-element.15), channel_id=1, source_target_pairs={{0,4},{1,5},{2,6},{3,7},{4,0},{5,1},{6,2},{7,3},{8,12},{9,13},{10,... | collective-permute-start | bytes 688136 | tf_op jit(solution)/shard_map/ppermute | solution.py:267
  71.5 13.0 %collective-permute-start.30 = (bf16[64,1792]{1,0:T(8,128)(2,1)}, bf16[64,1792]{1,0:T(8,128)(2,1)S(1)}, u32[]{:S(2)}, u32[]{:S(2)}) collective-permute-start(bf16[64,1792]{1,0:T(8,128)(2,1)} %get-tuple-element.15), channel_id=1, source_target_pairs={{0,6},{1,7},{2,4},{3,5},{4,2},{5,3},{6,0},{7,1},{8,14},{9,15},{10,... | collective-permute-start | bytes 688136 | tf_op jit(solution)/shard_map/ppermute | solution.py:267
  81.8 6.4 %collective-permute-start.24 = (bf16[64,1792]{1,0:T(8,128)(2,1)}, bf16[64,1792]{1,0:T(8,128)(2,1)S(1)}, u32[]{:S(2)}, u32[]{:S(2)}) collective-permute-start(bf16[64,1792]{1,0:T(8,128)(2,1)} %shard_map.61), channel_id=1, source_target_pairs={{0,2},{1,3},{2,0},{3,1},{4,6},{5,7},{6,4},{7,5},{8,10},{9,11},{10,... | collective-permute-start | bytes 688136 | tf_op jit(solution)/shard_map/ppermute | solution.py:267
  82.5 6.1 %collective-permute-start.25 = (bf16[64,1792]{1,0:T(8,128)(2,1)}, bf16[64,1792]{1,0:T(8,128)(2,1)S(1)}, u32[]{:S(2)}, u32[]{:S(2)}) collective-permute-start(bf16[64,1792]{1,0:T(8,128)(2,1)} %shard_map.61), channel_id=1, source_target_pairs={{0,4},{1,5},{2,6},{3,7},{4,0},{5,1},{6,2},{7,3},{8,12},{9,13},{10,... | collective-permute-start | bytes 688136 | tf_op jit(solution)/shard_map/ppermute | solution.py:267
  83.3 10.4 %collective-permute-start.26 = (bf16[64,1792]{1,0:T(8,128)(2,1)}, bf16[64,1792]{1,0:T(8,128)(2,1)S(1)}, u32[]{:S(2)}, u32[]{:S(2)}) collective-permute-start(bf16[64,1792]{1,0:T(8,128)(2,1)} %shard_map.61), channel_id=1, source_target_pairs={{0,6},{1,7},{2,4},{3,5},{4,2},{5,3},{6,0},{7,1},{8,14},{9,15},{10,... | collective-permute-start | bytes 688136 | tf_op jit(solution)/shard_map/ppermute | solution.py:267
  84.6 12.2 %collective-permute-start.31 = (bf16[64,1792]{1,0:T(8,128)(2,1)S(1)}, bf16[64,1792]{1,0:T(8,128)(2,1)S(1)}, u32[]{:S(2)}, u32[]{:S(2)}) collective-permute-start(bf16[64,1792]{1,0:T(8,128)(2,1)S(1)} %add_convert_fusion.refs_2_), channel_id=1, source_target_pairs={{0,1},{1,0},{2,3},{3,2},{4,5},{5,4},{6,7},{7,6},{8,9},{9,8},{10,11... | collective-permute-start | bytes 688136 | tf_op jit(solution)/shard_map/ppermute | solution.py:267
  94.7 3.2 %collective-permute-start.27 = (bf16[64,1792]{1,0:T(8,128)(2,1)S(1)}, bf16[64,1792]{1,0:T(8,128)(2,1)S(1)}, u32[]{:S(2)}, u32[]{:S(2)}) collective-permute-start(bf16[64,1792]{1,0:T(8,128)(2,1)S(1)} %add_convert_fusion.1.refs_0_), channel_id=1, source_target_pairs={{0,1},{1,0},{2,3},{3,2},{4,5},{5,4},{6,7},{7,6},{8,9},{9,8},{10,11... | collective-permute-start | bytes 688136 | tf_op jit(solution)/shard_map/ppermute | solution.py:267
  (28 other events, 335.6 us)

commit v2 on v1

v2 whole, which is shorter than its diff:
```python
import functools
import math

import jax
import jax.numpy as jnp
from jax import lax
from jax.experimental import pallas as pl
from jax.experimental.pallas import tpu as pltpu
from jax.sharding import PartitionSpec as P

BF = jnp.bfloat16
F32 = jnp.float32
NT = (((1,), (1,)), ((), ()))
NN = (((1,), (0,)), ((), ()))
TN = (((0,), (0,)), ((), ()))
MIB = 1024 * 1024


def dot(a, b, dims):
    return lax.dot_general(a, b, dims, preferred_element_type=F32)


def shifted(x, step, length):
    place = lax.broadcasted_iota(jnp.int32, x.shape, 0) % length
    edge = 0 if step > 0 else length - 1
    return jnp.where(place == edge, 0.0, pltpu.roll(x, step % x.shape[0], 0))


def fold_taps(source, start, first, count, layer, folded):
    for tap in range(first, first + count):
        row = start + 64 * (tap - first)
        block = source[row : row + 64]
        if tap == 27:
            at, places = 1152, [(0, 0), (1, 1)]
            for y, other in ((0, 1), (1, 0)):
                folded[layer, at + 64 * y : at + 64 * y + 64, 128 * other : 128 * other + 128] = jnp.zeros_like(block)
        else:
            at = 128 * (3 * (tap // 9) + tap % 3)
            places = [[(0, 1)], [(0, 0), (1, 1)], [(1, 0)]][tap // 3 % 3]
        for y, other in places:
            folded[layer, at + 64 * y : at + 64 * y + 64, 128 * other : 128 * other + 128] = block


def columns_of(padded):
    planes = padded.shape[0] - 2
    parts = [padded[d : d + planes] for d in range(3)]
    return jnp.concatenate(parts, axis=2).reshape(planes * padded.shape[1], 3 * padded.shape[2])


def forward_layer(layer, slot, act, folded, slope, keep_a, keep_h):
    padded = keep_a.at[slot]
    planes = padded.shape[0] - 2
    length = padded.shape[1]
    now = act[...]
    for at, value in enumerate((shifted(now, 1, length), now, shifted(now, -1, length))):
        padded[1 : planes + 1, :, 128 * at : 128 * at + 128] = value.astype(BF).reshape(planes, length, 128)
    pre = dot(columns_of(padded), folded[layer, :1152], NN)
    gate = 0.5 * jnp.tanh(0.5 * pre) + 0.5
    wide = pre * gate
    hidden = wide.astype(BF)
    slope[layer] = (gate + wide * (1.0 - gate)).astype(slope.dtype)
    act[...] = now + dot(hidden, folded[layer, 1152:], NT)
    keep_h[slot] = hidden


def term_rows(conv, mix, terms):
    def block(at, y, other):
        return conv[at + 64 * y : at + 64 * y + 64, 128 * other : 128 * other + 128]

    for dx in range(3):
        for dz in range(3):
            row = 64 * (9 * dx + 3 + dz)
            at = 128 * (3 * dx + dz)
            terms[row : row + 64] = (block(at, 0, 0) + block(at, 1, 1)).astype(BF)
            terms[row - 192 : row - 128] = block(at, 0, 1).astype(BF)
            terms[row + 192 : row + 256] = block(at, 1, 0).astype(BF)
    terms[1728:1792] = (mix[:64, :128] + mix[64:, 128:]).astype(BF)


def backward_layer(layer, owned, up, wide, folded, slope, keep_a, keep_h, terms, spread_if):
    planes = wide.shape[0] - 2
    length = wide.shape[1]
    now = up[...]
    up_low = now.astype(BF)
    grad = (dot(up_low, folded[layer, 1152:], NN) * slope[layer]).astype(BF)

    @pl.when(owned)
    def _():
        conv = dot(columns_of(keep_a.at[0]), grad, TN)
        term_rows(conv, dot(up_low, keep_h[0], TN), terms)

    @pl.when(spread_if)
    def _():
        wide[1 : planes + 1] = dot(grad, folded[layer, :1152], NT).reshape(planes, length, 1152)
        total = now
        for dz in range(3):
            part = 0.0
            for dx in range(3):
                at = 128 * (3 * dx + dz)
                part = part + wide[2 - dx : 2 - dx + planes, :, at : at + 128]
            part = part.reshape(planes * length, 128)
            total = total + (part if dz == 1 else shifted(part, dz - 1, length))
        up[...] = total


def clear_edges(ref):
    ref[0] = jnp.zeros(ref.shape[1:], ref.dtype)
    ref[ref.shape[0] - 1] = jnp.zeros(ref.shape[1:], ref.dtype)


def needed(plan, group, field):
    weight_steps, plane_steps = plan(0, 0, field)
    return sorted({step[0] for step in weight_steps[group] + plane_steps})


def take(plan, me_ref, field, group, conv, mix, pieces, folded, target):
    section, place = me_ref[0], me_ref[1]
    taps = conv.shape[2] // 64
    fold_taps(conv.at[group, 0], 0, 0, taps, section, folded)
    fold_taps(mix.at[group, 0], 0, taps, 1, section, folded)
    weight_steps, plane_steps = plan(section, place, field)
    pieces = dict(zip(needed(plan, group, field), pieces, strict=True))
    for piece, start, count, layer, first, choices in weight_steps[group]:
        for choice in choices:

            @pl.when(first == choice)
            def _(piece=piece, start=start, count=count, layer=layer, choice=choice):
                fold_taps(pieces[piece], start, choice, count, layer, folded)

    for piece, start, rows, rel in plane_steps:
        row = pl.multiple_of((place ^ rel) * rows, rows)
        target[pl.ds(row, rows)] = pieces[piece][start : start + rows].astype(F32)


def begin(copies, sems, first):
    started = []
    for number, (source, target) in enumerate(copies):
        copy = pltpu.make_async_copy(source, target, sems.at[first + number])
        copy.start()
        started.append(copy)
    return started


def finish(started):
    for copy in started:
        copy.wait()


def split_kernel(me_ref, inputs, cotangent, own, beside, across, swap):
    chip, core = me_ref[1] // 2, me_ref[1] % 2
    for number, source in enumerate((inputs, cotangent)):
        rows = slice(128 * number, 128 * number + 128)

        def turned(offset, source=source):
            return source[chip ^ offset].astype(F32).T.astype(BF)

        mine, far = turned(0), turned(3)
        one, two = turned(1 + core), turned(2 - core)
        own[rows] = mine
        across[rows] = far
        beside[rows] = one
        swap[rows] = mine
        swap[256 + 128 * number : 384 + 128 * number] = two


def first_kernel(plan, piece_count, me_ref, conv, mix, *refs):
    pieces, refs = refs[:piece_count], refs[piece_count:]
    act, folded, slope, keep_a, keep_h = refs
    section = me_ref[0]
    take(plan, me_ref, 0, 0, conv, mix, pieces, folded, act)
    for slot in range(2):
        clear_edges(keep_a.at[slot])

    def step(layer, carry):
        forward_layer(layer, jnp.where(layer == section, 0, 1), act, folded, slope, keep_a, keep_h)
        return carry

    lax.fori_loop(0, folded.shape[0], step, 0)


def all_back(section, last, up, wide, folded, slope, keep_a, keep_h, terms, replica, out):
    sections = folded.shape[0]

    def back(i, carry):
        layer = sections - 1 - i
        backward_layer(
            layer, layer == section, up, wide, folded, slope, keep_a, keep_h, terms, (layer >= 0) if last else layer > 0
        )
        return carry

    lax.fori_loop(0, sections, back, 0)
    rows = out.shape[0]
    out[...] = terms[pl.ds(pl.multiple_of(replica * rows, rows), rows)]


def second_kernel(plan, piece_count, me_ref, conv, mix, *refs):
    pieces, refs = refs[:piece_count], refs[piece_count:]
    act_in, up, out, folded, slope, keep_a, keep_h, act, wide, terms = refs
    section = me_ref[0]
    act[...] = act_in[...]
    take(plan, me_ref, 1, 1, conv, mix, pieces, folded, up)
    for slot in range(2):
        clear_edges(keep_a.at[slot])
    clear_edges(wide)

    def step(layer, carry):
        forward_layer(layer, jnp.where(layer == section, 0, 1), act, folded, slope, keep_a, keep_h)
        return carry

    lax.fori_loop(0, folded.shape[0], step, 0)
    all_back(section, True, up, wide, folded, slope, keep_a, keep_h, terms, me_ref[2], out)


def third_kernel(me_ref, up_in, folded, slope, keep_a, keep_h, out, up, wide, terms):
    up[...] = up_in[...]
    clear_edges(wide)
    all_back(me_ref[0], False, up, wide, folded, slope, keep_a, keep_h, terms, me_ref[2], out)


def send_grads(whole, conv, mix, group, start, stop, sems):
    taps = conv.shape[2]
    count = min(stop, taps) - start
    copies = [(whole.at[pl.ds(start, count)], conv.at[group, 0, pl.ds(start, count)])]
    if stop > taps:
        copies.append((whole.at[pl.ds(taps, stop - taps)], mix.at[group, 0]))
    return begin(copies, sems, 1 if start else 0)


def pair_kernel(group, factor, me_ref, own_a, own_b, far_a, far_b, *refs):
    conv, mix, whole, sems = refs[-4:]
    first = me_ref[2] == 0
    rows = own_a.shape[0]
    own = own_a[...].astype(F32) + own_b[...].astype(F32)
    far = far_a[...].astype(F32) + far_b[...].astype(F32)
    whole[:rows] = jnp.where(first, own, far) * factor
    started = send_grads(whole, conv, mix, group, 0, rows, sems)
    whole[rows:] = jnp.where(first, far, own) * factor
    started += send_grads(whole, conv, mix, group, rows, 2 * rows, sems)
    finish(started)


def plain_kernel(group, factor, me_ref, terms, *refs):
    conv, mix, whole, sems = refs[-4:]
    whole[...] = terms[...].astype(F32) * factor
    finish(send_grads(whole, conv, mix, group, 0, whole.shape[0], sems))


def size_of(x):
    return math.prod(x.shape) * x.dtype.itemsize


def call(kernel, outs, scratch, traffic, *args, into=()):
    vmem = pl.BlockSpec(memory_space=pltpu.VMEM)
    far = pl.BlockSpec(memory_space=pl.ANY)
    specs = [pl.BlockSpec(memory_space=pltpu.SMEM)] + [vmem] * (len(args) - 1) + [far] * len(into)
    held = sum(size_of(x) for x in scratch if x.memory_space == pltpu.VMEM)
    passed = sum(size_of(x) for x in args) + sum(size_of(x) for x in outs)
    limit = held + held // 4 + 10 * MIB
    if held + passed > 30 * MIB:
        limit = 63 * MIB
    return pl.pallas_call(
        kernel,
        out_shape=outs,
        in_specs=specs,
        out_specs=[far if kernel.func in (pair_kernel, plain_kernel) else vmem] * len(outs),
        scratch_shapes=scratch,
        input_output_aliases={len(args) + i: i for i in range(len(into))},
        compiler_params=pltpu.CompilerParams(vmem_limit_bytes=limit),
        cost_estimate=pl.CostEstimate(flops=traffic * 100, bytes_accessed=traffic, transcendentals=0),
    )(*args, *into)


def exchange(block, mask):
    count = lax.axis_size("space")
    return lax.ppermute(block, "space", [(i, i ^ mask) for i in range(count)])


def cross(block, first, second):
    count = lax.axis_size("space")
    return lax.ppermute(block, "space", [(i, i ^ (second if i % 2 else first)) for i in range(count)])


def after(x, *others):
    return lax.optimization_barrier((x, *others))[0]


def gather_paired(weights, fields, me, place):
    sections, space = lax.axis_size("section"), lax.axis_size("space")
    rows = weights.shape[1]
    half, quarter = rows // 2, rows // 4
    chip, core = place // 2, place % 2
    side = (chip // 2) ^ (chip % 2)
    mine = jnp.where(side == 0, weights[:, :half], weights[:, half:])
    part = lax.dynamic_slice_in_dim(mine, core * quarter, quarter, axis=1)
    route = []
    for s in range(sections):
        for j in range(space):
            target = (s + (-1 if j % 2 else 1)) % sections
            route.append((s * space + j, target * space + j))
    across = [(s, (s + 2) % sections) for s in range(sections)]
    own, beside, diagonal, swap = call(
        functools.partial(split_kernel),
        [jax.ShapeDtypeStruct((count, 128), BF) for count in (256, 256, 256, 512)],
        [], MIB, me, *fields,
    )
    other = exchange(swap, 1)
    diagonal = exchange(diagonal, 6)
    near = lax.ppermute(mine, ("section", "space"), route)
    far = lax.ppermute(part, "section", across)
    sent = [beside, other[256:]]
    pieces = []
    for group in range(2):
        here = jnp.concatenate([near[group], far[group]] + (sent if group == 0 else []), axis=0)
        there = cross(here, 2, 4)
        pieces += [here, there, exchange(here, 1), None if group else exchange(after(there, diagonal), 1)]
    planes = [own, other, diagonal, exchange(diagonal, 1)]
    plane_rows = 128

    def plan(section, place, field):
        chip, core = place // 2, place % 2
        side = (chip // 2) ^ (chip % 2)
        weight_steps = []
        for group in range(2):
            steps = []
            for swapped in range(2):
                source = core ^ swapped
                beside = lax.rem(section + sections - 1 + 2 * source, sections)
                across = lax.rem(section + 2, sections)
                for other in range(2):
                    piece = 4 * group + 2 * swapped + other
                    first = (side ^ other) * 14
                    steps.append((piece, 0, 14, beside, first, (0, 14)))
                    steps.append((piece, half, 7, across, first + source * 7, (0, 7, 14, 21)))
            weight_steps.append(steps)
        plane_steps = []
        start = field * plane_rows
        for piece, rel in ((8, 0), (9, 1), (10, 6), (11, 7)):
            plane_steps.append((piece, start, plane_rows, rel))
        for swapped in range(2):
            rel = swapped ^ (2 + 2 * (core ^ swapped))
            start = half + quarter + field * plane_rows
            plane_steps.append((1 + 2 * swapped, start, plane_rows, rel))
            plane_steps.append((1 + 2 * swapped, start + 2 * plane_rows, plane_rows, rel ^ 1))
        return weight_steps, plane_steps

    return pieces + planes, plan


def gather_plain(weights, both, place, replicas):
    sections = lax.axis_size("section")
    micro_count, _, plane_rows, _ = both.shape
    routes = [[(i, (i + d) % sections) for i in range(sections)] for d in range(1, sections)]
    pieces = [lax.ppermute(group, "section", route) for group in weights for route in routes]
    near = []
    for k in range(micro_count):
        part = lax.dynamic_index_in_dim(both, (place // replicas) ^ k, 0, keepdims=False)
        near.append(part if k == 0 else exchange(part, k * replicas))
    near = jnp.stack(near)
    fields = [near] + [exchange(near, r) for r in range(1, replicas)]
    fields = [x.reshape(-1, x.shape[-1]) for x in fields]

    def plan(section, place, field):
        first = weights.shape[0] * (sections - 1)
        weight_steps = [
            [
                (group * (sections - 1) + d - 1, 0, weights.shape[1] // 64, lax.rem(section + sections - d, sections), 0, (0,))
                for d in range(1, sections)
            ]
            for group in range(weights.shape[0])
        ]
        plane_steps = [
            (first + r, (2 * k + field) * plane_rows, plane_rows, k * replicas + r)
            for k in range(micro_count)
            for r in range(replicas)
        ]
        return weight_steps, plane_steps

    return pieces + fields, plan


def per_device(inputs, cotangent, conv_weight, mix_weight):
    micro_count, channels, extent_x, extent_y, extent_z = inputs.shape
    groups, _, hidden, taps = conv_weight.shape
    sections = lax.axis_size("section")
    space = lax.axis_size("space")
    section = lax.axis_index("section")
    place = lax.axis_index("space")
    replicas = space // micro_count
    width = taps + channels
    layers = groups * sections
    cells = extent_x * space * extent_z
    lanes = extent_y * channels
    paired = space == 8 and replicas == 2 and sections == 4 and extent_x == 1 and extent_z == 128 and lanes == 128
    me = jnp.stack([section, place, place % replicas]).astype(jnp.int32)

    conv_rows = jnp.swapaxes(conv_weight, 2, 3)
    weights = jnp.concatenate([conv_rows[:, 0], mix_weight[:, 0]], axis=1)
    if paired:
        fields = [x[:, :, 0].transpose(0, 2, 1, 3).reshape(micro_count, lanes, extent_z) for x in (inputs, cotangent)]
        pieces, plan = gather_paired(weights, fields, me, place)
    else:
        both = jnp.stack([inputs, cotangent], axis=1)
        both = both.transpose(0, 1, 3, 5, 4, 2).reshape(micro_count, 2, extent_x * extent_z, lanes)
        pieces, plan = gather_plain(weights, both, place, replicas)

    total_x = extent_x * space
    act = jax.ShapeDtypeStruct((cells, lanes), F32)
    kept = [
        jax.ShapeDtypeStruct((sections, 10 * lanes, 2 * hidden), BF),
        jax.ShapeDtypeStruct((sections, cells, 2 * hidden), BF),
        jax.ShapeDtypeStruct((2, total_x + 2, extent_z, 3 * lanes), BF),
        jax.ShapeDtypeStruct((2, cells, 2 * hidden), BF),
    ]
    early = [pieces[i] for i in needed(plan, 0, 0)]
    act, *saved = call(
        functools.partial(first_kernel, plan, len(early)),
        [act] + kept,
        [], 30 * MIB,
        me, conv_rows, mix_weight, *early,
    )
    if paired:
        pieces[7] = exchange(after(pieces[5], act), 1)
    late = [pieces[i] for i in needed(plan, 1, 1)]
    terms = jax.ShapeDtypeStruct((width // replicas, hidden), BF)
    wide = pltpu.VMEM((total_x + 2, extent_z, 9 * lanes), F32)
    whole = pltpu.VMEM((width, hidden), BF)
    up, late_terms = call(
        functools.partial(second_kernel, plan, len(late)),
        [act, terms],
        [pltpu.VMEM(x.shape, x.dtype) for x in kept] + [pltpu.VMEM((cells, lanes), F32), wide, whole],
        40 * MIB,
        me, conv_rows, mix_weight, *late, act,
    )
    traded = cross(late_terms, 2, 4) if paired else None
    (early_terms,) = call(
        functools.partial(third_kernel),
        [terms],
        [pltpu.VMEM((cells, lanes), F32), wide, whole],
        20 * MIB,
        me, up, *saved,
    )

    factor = 1.0 / math.sqrt(micro_count * cells * extent_y)
    outs = [
        jax.ShapeDtypeStruct((groups, 1, taps, hidden), F32),
        jax.ShapeDtypeStruct((groups, 1, channels, hidden), F32),
    ]
    scratch = [pltpu.VMEM((width, hidden), F32), pltpu.SemaphoreType.DMA((3,))]
    grads = ()
    for group in (1, 0):
        own = late_terms if group else early_terms
        if paired:
            met = after(traded, early_terms) if group else cross(own, 2, 4)
            half = (own.astype(F32) + met.astype(F32)).astype(BF)
            other = cross(half, 4, 2)
            if grads:
                other = after(other, grads[0])
            kernel, parts = pair_kernel, (half, other, exchange(half, 1), exchange(other, 1))
        else:
            level = [own] + [exchange(own, k * replicas) for k in range(1, micro_count)]
            level = [x.astype(F32) for x in level]
            while len(level) > 1:
                level = [level[i] + level[i + 1] for i in range(0, len(level), 2)]
            rows_of = [[m * replicas + r for r in range(replicas)] for m in range(micro_count)]
            every = lax.all_gather(level[0].astype(BF), "space", axis=0, tiled=True, axis_index_groups=rows_of)
            kernel, parts = plain_kernel, (every,)
        grads = call(functools.partial(kernel, group, factor), outs, scratch, 4 * MIB, me, *parts, into=grads)
    conv, mix = grads
    return (jnp.swapaxes(conv, 2, 3), mix)


def solution(mesh):
    placed = (
        P(None, None, "space", None, None),
        P(None, None, "space", None, None),
        P(None, "section", None, None),
        P(None, "section", None, None),
    )
    return jax.shard_map(
        per_device,
        mesh=mesh,
        in_specs=placed,
        out_specs=(P(None, "section", None, None), P(None, "section", None, None)),
        check_vma=False,
    )
```

time: 105 us -> 81.7 us (0.78)
  waiting for transfers between devices: 9.53 us -> 32.2 us
  starting transfers between devices: 40.7 us -> 19.5 us
  Pallas kernels: 41.6 us -> 26.9 us
  local copies, waits for them, and re-layouts: 9.41 us -> 0.13 us
    ppermute x32 -> x19, waiting for transfers between devices: 9.53 us -> 32.2 us  [the longest x1 16.2 us: gather_paired(): far = lax.ppermute(part, 'section', across)]
    ppermute x32 -> x19, starting transfers between devices: 40.7 us -> 19.5 us  [the longest x11 9.61 us: exchange(): return lax.ppermute(block, 'space', [(i, i ^ mask) for i in range(count)])]
    pallas_call x4 -> x6, Pallas kernels: 41.6 us -> 26.9 us  [call(): pl.pallas_call(kernel, out_shape=outs, in_specs=specs, out_specs=[far if...]
    unnamed x58 -> x8, local copies, waits for them, and re-layouts: 3.56 us -> 0.02 us
    pallas_call x1 -> x0, local copies, waits for them, and re-layouts: 2.7 us -> none  [call(): pl.pallas_call(kernel, out_shape=outs, in_specs=[pl.BlockSpec(memory_spac...]
    dynamic_slice x6 -> x1, local copies, waits for them, and re-layouts: 2.22 us -> 0.02 us  [gather_paired(): part = lax.dynamic_slice_in_dim(mine, core * quarter, quarter, axis=1)]
    select_n x0 -> x1, other arithmetic: none -> 1.35 us  [gather_paired(): mine = jnp.where(side == 0, weights[:, :half], weights[:, half:])]
  transfers between devices with their start and end apart: 32 -> 19, of which waited for: 5 -> 9; matrix products, arithmetic and copies ran while one was open for 4% -> 0% of each run, Pallas kernels for 21% -> 17%
where the time goes in v2:
time: 81.7 us; the launch traced here: 81.3 us
  waiting for transfers between devices  32.2 us (39%)
  Pallas kernels  26.9 us (33%)
  starting transfers between devices  19.5 us (24%)
  other arithmetic  1.61 us (2%)
  between operations  0.9 us (1%)
    pallas_call x6, Pallas kernels, call(): pl.pallas_call(kernel, out_shape=outs, in_specs=specs, out_specs=[far if...  26.9 us
    ppermute x1, waiting for transfers between devices, gather_paired(): far = lax.ppermute(part, 'section', across)  16.2 us
    ppermute x11, starting transfers between devices, exchange(): return lax.ppermute(block, 'space', [(i, i ^ mask) for i in range(count)])  9.61 us
    ppermute x6, waiting for transfers between devices, cross(): lax.ppermute(block, 'space', [(i, i ^ (second if i % 2 else first)) for i...  8.36 us
    ppermute x11, waiting for transfers between devices, exchange(): return lax.ppermute(block, 'space', [(i, i ^ mask) for i in range(count)])  7.62 us
    ppermute x6, starting transfers between devices, cross(): lax.ppermute(block, 'space', [(i, i ^ (second if i % 2 else first)) for i...  5.57 us
    ppermute x1, starting transfers between devices, gather_paired(): near = lax.ppermute(mine, ('section', 'space'), route)  4.2 us
  transfers between devices with their start and end apart: 19, of which 9 were waited for; matrix products, arithmetic and copies ran while one was open for 0% of the time, Pallas kernels for 17%

profile of v2, /device:TPU:1, one launch (start us, length us, event | category | flops | bytes accessed | tf_op | source)
XLA Modules:
  0.0 81.3 jit_solution(26517546478388442)
XLA Ops:
  0.7 1.3 %fusion = bf16[2,896,128]{2,1,0:T(8,128)(2,1)S(1)} fusion(bf16[2,64,128]{2,1,0:T(8,128)(2,1)} %bitcast.33, bf16[2,1728,128]{2,1,0:T(8,128)(2,1)} %bitcast.28, pred[]{:T(512)S(6)} %eq.7), kind=kLoop, calls=%fused_computation.2 | loop fusion | flops 1146880 | bytes 1835009 | tf_op jit(solution)/shard_map/jit(_where)/select_n | solution.py:293
  2.0 4.2 %collective-permute-start = (bf16[2,896,128]{2,1,0:T(8,128)(2,1)S(1)}, bf16[2,896,128]{2,1,0:T(8,128)(2,1)S(1)}, u32[]{:S(2)}, u32[]{:S(2)}) collective-permute-start(bf16[2,896,128]{2,1,0:T(8,128)(2,1)S(1)} %fusion), channel_id=1, source_target_pairs={{0,8},{1,25},{2,10},{3,27},{4,12},{5,29},{6,14},{7,31},{8,16},{9,1... | collective-permute-start | bytes 1376264 | tf_op jit(solution)/shard_map/ppermute | solution.py:308
  6.5 0.7 shard_map.59
  7.2 1.6 %collective-permute-start.2 = (bf16[512,128]{1,0:T(8,128)(2,1)S(1)}, bf16[512,128]{1,0:T(8,128)(2,1)S(1)}, u32[]{:S(2)}, u32[]{:S(2)}) collective-permute-start(bf16[512,128]{1,0:T(8,128)(2,1)S(1)} %get-tuple-element.22), channel_id=1, source_target_pairs={{0,1},{1,0},{2,3},{3,2},{4,5},{5,4},{6,7},{7,6},{8,9},{9,8},{10,11... | collective-permute-start | bytes 393224 | tf_op jit(solution)/shard_map/ppermute | solution.py:275
  8.8 1.0 %collective-permute-done.2.refs_5_.refs_7_ = bf16[512,128]{1,0:T(8,128)(2,1)S(1)} collective-permute-done((bf16[512,128]{1,0:T(8,128)(2,1)S(1)}, bf16[512,128]{1,0:T(8,128)(2,1)S(1)}, u32[]{:S(2)}, u32[]{:S(2)}) %collective-permute-start.2) | collective-permute-done | bytes 131104 | tf_op jit(solution)/shard_map/ppermute | solution.py:275
  9.8 16.2 %collective-permute-done.1 = bf16[2,448,128]{2,1,0:T(8,128)(2,1)S(1)} collective-permute-done((bf16[2,448,128]{2,1,0:T(8,128)(2,1)S(1)}, bf16[2,448,128]{2,1,0:T(8,128)(2,1)S(1)}, u32[]{:S(2)}, u32[]{:S(2)}) %collective-permute-start.1) | collective-permute-done | bytes 229408 | tf_op jit(solution)/shard_map/ppermute | solution.py:309
  26.1 1.3 %collective-permute-start.3 = (bf16[1856,128]{1,0:T(8,128)(2,1)S(1)}, bf16[1856,128]{1,0:T(8,128)(2,1)S(1)}, u32[]{:S(2)}, u32[]{:S(2)}) collective-permute-start(bf16[1856,128]{1,0:T(8,128)(2,1)S(1)} %pad_maximum_fusion.refs_0_), channel_id=1, source_target_pairs={{0,2},{1,5},{2,0},{3,7},{4,6},{5,1},{6,4},{7,3},{8,10},{9,13},{10,... | collective-permute-start | bytes 1425416 | tf_op jit(solution)/shard_map/ppermute | solution.py:280
  27.4 1.2 %collective-permute-start.4 = (bf16[256,128]{1,0:T(8,128)(2,1)S(1)}, bf16[256,128]{1,0:T(8,128)(2,1)S(1)}, u32[]{:S(2)}, u32[]{:S(2)}) collective-permute-start(bf16[256,128]{1,0:T(8,128)(2,1)S(1)} %get-tuple-element.23), channel_id=1, source_target_pairs={{0,6},{1,7},{2,4},{3,5},{4,2},{5,3},{6,0},{7,1},{8,14},{9,15},{10,... | collective-permute-start | bytes 196616 | tf_op jit(solution)/shard_map/ppermute | solution.py:275
  28.6 3.6 %collective-permute-done.4.refs_6_.refs_8_ = bf16[256,128]{1,0:T(8,128)(2,1)S(1)} collective-permute-done((bf16[256,128]{1,0:T(8,128)(2,1)S(1)}, bf16[256,128]{1,0:T(8,128)(2,1)S(1)}, u32[]{:S(2)}, u32[]{:S(2)}) %collective-permute-start.4) | collective-permute-done | bytes 65568 | tf_op jit(solution)/shard_map/ppermute | solution.py:275
  32.2 2.9 %collective-permute-done.3.refs_1_.refs_0_ = bf16[1856,128]{1,0:T(8,128)(2,1)S(1)} collective-permute-done((bf16[1856,128]{1,0:T(8,128)(2,1)S(1)}, bf16[1856,128]{1,0:T(8,128)(2,1)S(1)}, u32[]{:S(2)}, u32[]{:S(2)}) %collective-permute-start.3) | collective-permute-done | bytes 475168 | tf_op jit(solution)/shard_map/ppermute | solution.py:280
  35.1 0.3 collective-permute-start.5
  35.4 0.2 collective-permute-start.9
  35.6 1.3 %collective-permute-start.6 = (bf16[1344,128]{1,0:T(8,128)(2,1)S(1)}, bf16[1344,128]{1,0:T(8,128)(2,1)S(1)}, u32[]{:S(2)}, u32[]{:S(2)}) collective-permute-start(bf16[1344,128]{1,0:T(8,128)(2,1)S(1)} %pad_maximum_fusion.2.refs_2_), channel_id=1, source_target_pairs={{0,2},{1,5},{2,0},{3,7},{4,6},{5,1},{6,4},{7,3},{8,10},{9,13},{10,... | collective-permute-start | bytes 1032200 | tf_op jit(solution)/shard_map/ppermute | solution.py:280
  36.9 0.6 collective-permute-start.7
  37.6 6.1 %shard_map.60 = (f32[1024,128]{1,0:T(8,128)S(1)}, bf16[4,1280,256]{2,1,0:T(8,128)(2,1)S(1)}, bf16[4,1024,256]{2,1,0:T(8,128)(2,1)S(1)}, bf16[2,10,128,384]{3,2,1,0:T(8,128)(2,1)S(1)}, bf16[2,1024,256]{2,1,0:T(8,128)(2,1)S(1)}) custom-call(s32[3]{0:T(128)S(1)} %pad_add_fusion.me_ref, bf16[2,1,1728,128]{3,2,1,0:T(8,128)(2,1)S(1)} %bitcast.29, ...), custom_call_target="tpu_custom_call" | custom-call | flops 3145728000 | bytes 31457280 | tf_op jit(solution)/shard_map/pallas_call | solution.py:261
  43.8 1.6 %collective-permute-done.10.refs_5_ = bf16[1344,128]{1,0:T(8,128)(2,1)S(1)} collective-permute-done((bf16[1344,128]{1,0:T(8,128)(2,1)S(1)}, bf16[1344,128]{1,0:T(8,128)(2,1)S(1)}, u32[]{:S(2)}, u32[]{:S(2)}) %collective-permute-start.10) | collective-permute-done | bytes 344096 | tf_op jit(solution)/shard_map/ppermute | solution.py:275
  45.4 11.7 %shard_map.61 = (f32[1024,128]{1,0:T(8,128)S(1)}, bf16[896,128]{1,0:T(8,128)(2,1)S(1)}) custom-call(s32[3]{0:T(128)S(1)} %pad_add_fusion.me_ref, bf16[2,1,1728,128]{3,2,1,0:T(8,128)(2,1)S(1)} %bitcast.30, bf16[2,1,64,128]{3,2,1,0:T(8,128)(2,1)S(1)} %copy-done.1, bf16[1856,128]{1,0:T(8,128)(2,1)S(1)} %collective-permute-done.3.refs_1_.refs_0_, ...), custom_call_target="tpu_custom_call" | custom-call | flops 4194304000 | bytes 41943040 | tf_op jit(solution)/shard_map/pallas_call | solution.py:261
  57.1 0.9 %collective-permute-start.13 = (bf16[896,128]{1,0:T(8,128)(2,1)S(1)}, bf16[896,128]{1,0:T(8,128)(2,1)S(1)}, u32[]{:S(2)}, u32[]{:S(2)}) collective-permute-start(bf16[896,128]{1,0:T(8,128)(2,1)S(1)} %get-tuple-element.33), channel_id=1, source_target_pairs={{0,2},{1,5},{2,0},{3,7},{4,6},{5,1},{6,4},{7,3},{8,10},{9,13},{10,... | collective-permute-start | bytes 688136 | tf_op jit(solution)/shard_map/ppermute | solution.py:280
  58.0 5.3 %shard_map.62 = bf16[896,128]{1,0:T(8,128)(2,1)S(1)} custom-call(s32[3]{0:T(128)S(1)} %pad_add_fusion.me_ref, f32[1024,128]{1,0:T(8,128)S(1)} %get-tuple-element.28.up_in, bf16[4,1280,256]{2,1,0:T(8,128)(2,1)S(1)} %get-tuple-element.29.folded, bf16[4,1024,256]{2,1,0:T(8,128)(2,1)S(1)} %get-tuple-element.30.slope, ...), custom_call_target="tpu_custom_call" | custom-call | flops 2097152000 | bytes 20971520 | tf_op jit(solution)/shard_map/pallas_call | solution.py:261
  63.4 1.1 %collective-permute-start.14 = (bf16[896,128]{1,0:T(8,128)(2,1)S(1)}, bf16[896,128]{1,0:T(8,128)(2,1)S(1)}, u32[]{:S(2)}, u32[]{:S(2)}) collective-permute-start(bf16[896,128]{1,0:T(8,128)(2,1)S(1)} %add_convert_fusion.own_a), channel_id=1, source_target_pairs={{0,4},{1,3},{2,6},{3,1},{4,0},{5,7},{6,2},{7,5},{8,12},{9,11},{10,... | collective-permute-start | bytes 688136 | tf_op jit(solution)/shard_map/ppermute | solution.py:280
  64.6 0.3 collective-permute-start.11
  64.8 1.1 %collective-permute-start.15 = (bf16[896,128]{1,0:T(8,128)(2,1)S(1)}, bf16[896,128]{1,0:T(8,128)(2,1)S(1)}, u32[]{:S(2)}, u32[]{:S(2)}) collective-permute-start(bf16[896,128]{1,0:T(8,128)(2,1)S(1)} %add_convert_fusion.own_a), channel_id=1, source_target_pairs={{0,1},{1,0},{2,3},{3,2},{4,5},{5,4},{6,7},{7,6},{8,9},{9,8},{10,11... | collective-permute-start | bytes 688136 | tf_op jit(solution)/shard_map/ppermute | solution.py:275
  65.9 2.9 %collective-permute-done.14.own_b = bf16[896,128]{1,0:T(8,128)(2,1)S(1)} collective-permute-done((bf16[896,128]{1,0:T(8,128)(2,1)S(1)}, bf16[896,128]{1,0:T(8,128)(2,1)S(1)}, u32[]{:S(2)}, u32[]{:S(2)}) %collective-permute-start.14) | collective-permute-done | bytes 229408 | tf_op jit(solution)/shard_map/ppermute | solution.py:280
  68.8 3.6 %collective-permute-start.16 = (bf16[896,128]{1,0:T(8,128)(2,1)S(1)}, bf16[896,128]{1,0:T(8,128)(2,1)S(1)}, u32[]{:S(2)}, u32[]{:S(2)}) collective-permute-start(bf16[896,128]{1,0:T(8,128)(2,1)S(1)} %collective-permute-done.14.own_b), channel_id=1, source_target_pairs={{0,1},{1,0},{2,3},{3,2},{4,5},{5,4},{6,7},{7,6},{8,9},{9,8},{10,11... | collective-permute-start | bytes 688136 | tf_op jit(solution)/shard_map/ppermute | solution.py:275
  72.5 0.6 collective-permute-start.12
  73.1 0.2 collective-permute-start.17
  73.3 0.2 collective-permute-done.16.far_b
  73.5 1.6 %shard_map.63 = (f32[2,1,1728,128]{3,2,1,0:T(8,128)}, f32[2,1,64,128]{3,2,1,0:T(8,128)}) custom-call(s32[3]{0:T(128)S(1)} %pad_add_fusion.me_ref, bf16[896,128]{1,0:T(8,128)(2,1)S(1)} %add_convert_fusion.own_a, bf16[896,128]{1,0:T(8,128)(2,1)S(1)} %collective-permute-done.14.own_b, bf16[896,128]{1,0:T(8,128)(2,1)S(1)} %collective-permute-done.15.far_a, ...), custom_call_target="tpu_custom_call" | custom-call | flops 419430400 | bytes 4194304 | tf_op jit(solution)/shard_map/pallas_call | solution.py:261
  75.1 2.6 %collective-permute-done.12.own_b = bf16[896,128]{1,0:T(8,128)(2,1)S(1)} collective-permute-done((bf16[896,128]{1,0:T(8,128)(2,1)S(1)}, bf16[896,128]{1,0:T(8,128)(2,1)S(1)}, u32[]{:S(2)}, u32[]{:S(2)}) %collective-permute-start.12) | collective-permute-done | bytes 229408 | tf_op jit(solution)/shard_map/ppermute | solution.py:280
  77.7 0.9 %collective-permute-start.18 = (bf16[896,128]{1,0:T(8,128)(2,1)S(1)}, bf16[896,128]{1,0:T(8,128)(2,1)S(1)}, u32[]{:S(2)}, u32[]{:S(2)}) collective-permute-start(bf16[896,128]{1,0:T(8,128)(2,1)S(1)} %collective-permute-done.12.own_b), channel_id=1, source_target_pairs={{0,1},{1,0},{2,3},{3,2},{4,5},{5,4},{6,7},{7,6},{8,9},{9,8},{10,11... | collective-permute-start | bytes 688136 | tf_op jit(solution)/shard_map/ppermute | solution.py:275
  78.6 1.1 %collective-permute-done.18.far_b = bf16[896,128]{1,0:T(8,128)(2,1)S(1)} collective-permute-done((bf16[896,128]{1,0:T(8,128)(2,1)S(1)}, bf16[896,128]{1,0:T(8,128)(2,1)S(1)}, u32[]{:S(2)}, u32[]{:S(2)}) %collective-permute-start.18) | collective-permute-done | bytes 229408 | tf_op jit(solution)/shard_map/ppermute | solution.py:275
  79.7 1.6 %shard_map.64 = (f32[2,1,1728,128]{3,2,1,0:T(8,128)}, f32[2,1,64,128]{3,2,1,0:T(8,128)}) custom-call(s32[3]{0:T(128)S(1)} %pad_add_fusion.me_ref, bf16[896,128]{1,0:T(8,128)(2,1)S(1)} %add_convert_fusion.1.own_a, bf16[896,128]{1,0:T(8,128)(2,1)S(1)} %collective-permute-done.12.own_b, ...), custom_call_target="tpu_custom_call", output_to_operand_aliasing={{0}: (5, {}), {1}: (6, {})} | custom-call | flops 419430400 | bytes 4194304 | tf_op jit(solution)/shard_map/pallas_call | solution.py:261
  (32 shorter events, 0.6 us)
Async XLA Ops:
  0.6 5.7 %copy-start.2 = (bf16[4,64,1,2,128]{4,3,2,1,0:T(2,128)(2,1)S(1)}, bf16[4,64,1,2,128]{4,3,2,1,0:T(2,128)(2,1)}, u32[]{:S(2)}) copy-start(bf16[4,64,1,2,128]{4,3,2,1,0:T(2,128)(2,1)} %param.4) | copy-start | bytes 393220
  0.6 5.8 %copy-start.3 = (bf16[4,64,1,2,128]{4,3,2,1,0:T(2,128)(2,1)S(1)}, bf16[4,64,1,2,128]{4,3,2,1,0:T(2,128)(2,1)}, u32[]{:S(2)}) copy-start(bf16[4,64,1,2,128]{4,3,2,1,0:T(2,128)(2,1)} %param.5) | copy-start | bytes 393220
  2.0 24.0 %collective-permute-start = (bf16[2,896,128]{2,1,0:T(8,128)(2,1)S(1)}, bf16[2,896,128]{2,1,0:T(8,128)(2,1)S(1)}, u32[]{:S(2)}, u32[]{:S(2)}) collective-permute-start(bf16[2,896,128]{2,1,0:T(8,128)(2,1)S(1)} %fusion), channel_id=1, source_target_pairs={{0,8},{1,25},{2,10},{3,27},{4,12},{5,29},{6,14},{7,31},{8,16},{9,1... | collective-permute-start | bytes 1376264 | tf_op jit(solution)/shard_map/ppermute | solution.py:308
  6.3 19.7 %collective-permute-start.1 = (bf16[2,448,128]{2,1,0:T(8,128)(2,1)S(1)}, bf16[2,448,128]{2,1,0:T(8,128)(2,1)S(1)}, u32[]{:S(2)}, u32[]{:S(2)}) collective-permute-start(bf16[2,448,128]{2,1,0:T(8,128)(2,1)S(1)} %constant_dynamic-slice_fusion), channel_id=1, source_target_pairs={{0,16},{8,24},{16,0},{24,8},{1,17},{9,25},{17,1},{25,9},{2,18},{10... | collective-permute-start | bytes 688136 | tf_op jit(solution)/shard_map/ppermute | solution.py:309
  6.4 31.2 %copy-start = (bf16[2,1,128,1728]{2,3,1,0:T(8,128)(2,1)S(1)}, bf16[2,1,128,1728]{2,3,1,0:T(8,128)(2,1)}, u32[]{:S(2)}) copy-start(bf16[2,1,128,1728]{2,3,1,0:T(8,128)(2,1)} %param.6) | copy-start | bytes 2654212
  6.4 31.2 %copy-start.1 = (bf16[2,1,64,128]{3,2,1,0:T(8,128)(2,1)S(1)}, bf16[2,1,64,128]{3,2,1,0:T(8,128)(2,1)}, u32[]{:S(2)}) copy-start(bf16[2,1,64,128]{3,2,1,0:T(8,128)(2,1)} %mix.3) | copy-start | bytes 98308
  7.2 2.5 %collective-permute-start.2 = (bf16[512,128]{1,0:T(8,128)(2,1)S(1)}, bf16[512,128]{1,0:T(8,128)(2,1)S(1)}, u32[]{:S(2)}, u32[]{:S(2)}) collective-permute-start(bf16[512,128]{1,0:T(8,128)(2,1)S(1)} %get-tuple-element.22), channel_id=1, source_target_pairs={{0,1},{1,0},{2,3},{3,2},{4,5},{5,4},{6,7},{7,6},{8,9},{9,8},{10,11... | collective-permute-start | bytes 393224 | tf_op jit(solution)/shard_map/ppermute | solution.py:275
  26.1 9.0 %collective-permute-start.3 = (bf16[1856,128]{1,0:T(8,128)(2,1)S(1)}, bf16[1856,128]{1,0:T(8,128)(2,1)S(1)}, u32[]{:S(2)}, u32[]{:S(2)}) collective-permute-start(bf16[1856,128]{1,0:T(8,128)(2,1)S(1)} %pad_maximum_fusion.refs_0_), channel_id=1, source_target_pairs={{0,2},{1,5},{2,0},{3,7},{4,6},{5,1},{6,4},{7,3},{8,10},{9,13},{10,... | collective-permute-start | bytes 1425416 | tf_op jit(solution)/shard_map/ppermute | solution.py:280
  27.4 4.8 %collective-permute-start.4 = (bf16[256,128]{1,0:T(8,128)(2,1)S(1)}, bf16[256,128]{1,0:T(8,128)(2,1)S(1)}, u32[]{:S(2)}, u32[]{:S(2)}) collective-permute-start(bf16[256,128]{1,0:T(8,128)(2,1)S(1)} %get-tuple-element.23), channel_id=1, source_target_pairs={{0,6},{1,7},{2,4},{3,5},{4,2},{5,3},{6,0},{7,1},{8,14},{9,15},{10,... | collective-permute-start | bytes 196616 | tf_op jit(solution)/shard_map/ppermute | solution.py:275
  28.6 9.0 %collective-permute-start.8 = (bf16[1856,128]{1,0:T(8,128)(2,1)S(1)}, bf16[1856,128]{1,0:T(8,128)(2,1)S(1)}, u32[]{:S(2)}, u32[]{:S(2)}) collective-permute-start(bf16[1856,128]{1,0:T(8,128)(2,1)S(1)} %pad_maximum_fusion.refs_0_), channel_id=1, source_target_pairs={{0,1},{1,0},{2,3},{3,2},{4,5},{5,4},{6,7},{7,6},{8,9},{9,8},{10,11... | collective-permute-start | bytes 1425416 | tf_op jit(solution)/shard_map/ppermute | solution.py:275
  35.1 2.4 %collective-permute-start.5 = (bf16[1856,128]{1,0:T(8,128)(2,1)S(1)}, bf16[1856,128]{1,0:T(8,128)(2,1)S(1)}, u32[]{:S(2)}, u32[]{:S(2)}) collective-permute-start(bf16[1856,128]{1,0:T(8,128)(2,1)S(1)} %collective-permute-done.3.refs_1_.refs_0_), channel_id=1, source_target_pairs={{0,1},{1,0},{2,3},{3,2},{4,5},{5,4},{6,7},{7,6},{8,9},{9,8},{10,11... | collective-permute-start | bytes 1425416 | tf_op jit(solution)/shard_map/ppermute | solution.py:275
  35.4 2.1 %collective-permute-start.9 = (bf16[256,128]{1,0:T(8,128)(2,1)S(1)}, bf16[256,128]{1,0:T(8,128)(2,1)S(1)}, u32[]{:S(2)}, u32[]{:S(2)}) collective-permute-start(bf16[256,128]{1,0:T(8,128)(2,1)S(1)} %collective-permute-done.4.refs_6_.refs_8_), channel_id=1, source_target_pairs={{0,1},{1,0},{2,3},{3,2},{4,5},{5,4},{6,7},{7,6},{8,9},{9,8},{10,11... | collective-permute-start | bytes 196616 | tf_op jit(solution)/shard_map/ppermute | solution.py:275
  35.6 8.0 %collective-permute-start.6 = (bf16[1344,128]{1,0:T(8,128)(2,1)S(1)}, bf16[1344,128]{1,0:T(8,128)(2,1)S(1)}, u32[]{:S(2)}, u32[]{:S(2)}) collective-permute-start(bf16[1344,128]{1,0:T(8,128)(2,1)S(1)} %pad_maximum_fusion.2.refs_2_), channel_id=1, source_target_pairs={{0,2},{1,5},{2,0},{3,7},{4,6},{5,1},{6,4},{7,3},{8,10},{9,13},{10,... | collective-permute-start | bytes 1032200 | tf_op jit(solution)/shard_map/ppermute | solution.py:280
  36.9 6.8 %collective-permute-start.7 = (bf16[1344,128]{1,0:T(8,128)(2,1)S(1)}, bf16[1344,128]{1,0:T(8,128)(2,1)S(1)}, u32[]{:S(2)}, u32[]{:S(2)}) collective-permute-start(bf16[1344,128]{1,0:T(8,128)(2,1)S(1)} %pad_maximum_fusion.2.refs_2_), channel_id=1, source_target_pairs={{0,1},{1,0},{2,3},{3,2},{4,5},{5,4},{6,7},{7,6},{8,9},{9,8},{10,11... | collective-permute-start | bytes 1032200 | tf_op jit(solution)/shard_map/ppermute | solution.py:275
  43.7 1.7 %collective-permute-start.10 = (bf16[1344,128]{1,0:T(8,128)(2,1)S(1)}, bf16[1344,128]{1,0:T(8,128)(2,1)S(1)}, u32[]{:S(2)}, u32[]{:S(2)}) collective-permute-start(bf16[1344,128]{1,0:T(8,128)(2,1)S(1)} %collective-permute-done.6.refs_3_), channel_id=1, source_target_pairs={{0,1},{1,0},{2,3},{3,2},{4,5},{5,4},{6,7},{7,6},{8,9},{9,8},{10,11... | collective-permute-start | bytes 1032200 | tf_op jit(solution)/shard_map/ppermute | solution.py:275
  57.1 6.3 %collective-permute-start.13 = (bf16[896,128]{1,0:T(8,128)(2,1)S(1)}, bf16[896,128]{1,0:T(8,128)(2,1)S(1)}, u32[]{:S(2)}, u32[]{:S(2)}) collective-permute-start(bf16[896,128]{1,0:T(8,128)(2,1)S(1)} %get-tuple-element.33), channel_id=1, source_target_pairs={{0,2},{1,5},{2,0},{3,7},{4,6},{5,1},{6,4},{7,3},{8,10},{9,13},{10,... | collective-permute-start | bytes 688136 | tf_op jit(solution)/shard_map/ppermute | solution.py:280
  63.4 5.4 %collective-permute-start.14 = (bf16[896,128]{1,0:T(8,128)(2,1)S(1)}, bf16[896,128]{1,0:T(8,128)(2,1)S(1)}, u32[]{:S(2)}, u32[]{:S(2)}) collective-permute-start(bf16[896,128]{1,0:T(8,128)(2,1)S(1)} %add_convert_fusion.own_a), channel_id=1, source_target_pairs={{0,4},{1,3},{2,6},{3,1},{4,0},{5,7},{6,2},{7,5},{8,12},{9,11},{10,... | collective-permute-start | bytes 688136 | tf_op jit(solution)/shard_map/ppermute | solution.py:280
  64.6 7.9 %collective-permute-start.11 = (bf16[896,128]{1,0:T(8,128)(2,1)S(1)}, bf16[896,128]{1,0:T(8,128)(2,1)S(1)}, u32[]{:S(2)}, u32[]{:S(2)}) collective-permute-start(bf16[896,128]{1,0:T(8,128)(2,1)S(1)} %shard_map.62), channel_id=1, source_target_pairs={{0,2},{1,5},{2,0},{3,7},{4,6},{5,1},{6,4},{7,3},{8,10},{9,13},{10,... | collective-permute-start | bytes 688136 | tf_op jit(solution)/shard_map/ppermute | solution.py:280
  64.8 8.4 %collective-permute-start.15 = (bf16[896,128]{1,0:T(8,128)(2,1)S(1)}, bf16[896,128]{1,0:T(8,128)(2,1)S(1)}, u32[]{:S(2)}, u32[]{:S(2)}) collective-permute-start(bf16[896,128]{1,0:T(8,128)(2,1)S(1)} %add_convert_fusion.own_a), channel_id=1, source_target_pairs={{0,1},{1,0},{2,3},{3,2},{4,5},{5,4},{6,7},{7,6},{8,9},{9,8},{10,11... | collective-permute-start | bytes 688136 | tf_op jit(solution)/shard_map/ppermute | solution.py:275
  68.8 4.7 %collective-permute-start.16 = (bf16[896,128]{1,0:T(8,128)(2,1)S(1)}, bf16[896,128]{1,0:T(8,128)(2,1)S(1)}, u32[]{:S(2)}, u32[]{:S(2)}) collective-permute-start(bf16[896,128]{1,0:T(8,128)(2,1)S(1)} %collective-permute-done.14.own_b), channel_id=1, source_target_pairs={{0,1},{1,0},{2,3},{3,2},{4,5},{5,4},{6,7},{7,6},{8,9},{9,8},{10,11... | collective-permute-start | bytes 688136 | tf_op jit(solution)/shard_map/ppermute | solution.py:275
  72.5 5.2 %collective-permute-start.12 = (bf16[896,128]{1,0:T(8,128)(2,1)S(1)}, bf16[896,128]{1,0:T(8,128)(2,1)S(1)}, u32[]{:S(2)}, u32[]{:S(2)}) collective-permute-start(bf16[896,128]{1,0:T(8,128)(2,1)S(1)} %add_convert_fusion.1.own_a), channel_id=1, source_target_pairs={{0,4},{1,3},{2,6},{3,1},{4,0},{5,7},{6,2},{7,5},{8,12},{9,11},{10,... | collective-permute-start | bytes 688136 | tf_op jit(solution)/shard_map/ppermute | solution.py:280
  73.1 5.5 %collective-permute-start.17 = (bf16[896,128]{1,0:T(8,128)(2,1)S(1)}, bf16[896,128]{1,0:T(8,128)(2,1)S(1)}, u32[]{:S(2)}, u32[]{:S(2)}) collective-permute-start(bf16[896,128]{1,0:T(8,128)(2,1)S(1)} %add_convert_fusion.1.own_a), channel_id=1, source_target_pairs={{0,1},{1,0},{2,3},{3,2},{4,5},{5,4},{6,7},{7,6},{8,9},{9,8},{10,11... | collective-permute-start | bytes 688136 | tf_op jit(solution)/shard_map/ppermute | solution.py:275
  77.7 2.0 %collective-permute-start.18 = (bf16[896,128]{1,0:T(8,128)(2,1)S(1)}, bf16[896,128]{1,0:T(8,128)(2,1)S(1)}, u32[]{:S(2)}, u32[]{:S(2)}) collective-permute-start(bf16[896,128]{1,0:T(8,128)(2,1)S(1)} %collective-permute-done.12.own_b), channel_id=1, source_target_pairs={{0,1},{1,0},{2,3},{3,2},{4,5},{5,4},{6,7},{7,6},{8,9},{9,8},{10,11... | collective-permute-start | bytes 688136 | tf_op jit(solution)/shard_map/ppermute | solution.py:275

commit v3 on v2

--- a/solution.py
+++ b/solution.py
@@ -146,13 +146,16 @@
         copy.wait()
 
 
-def split_kernel(me_ref, inputs, cotangent, own, beside, across, swap):
+def split_kernel(me_ref, inputs, cotangent, token, own, beside, across, swap):
     chip, core = me_ref[1] // 2, me_ref[1] % 2
+    old = lax.broadcasted_iota(jnp.int32, (128, 128), 0)
+    new = lax.broadcasted_iota(jnp.int32, (128, 128), 1)
+    order = ((old % 2) * 64 + old // 2 == new).astype(F32).astype(BF)
     for number, source in enumerate((inputs, cotangent)):
         rows = slice(128 * number, 128 * number + 128)
 
         def turned(offset, source=source):
-            return source[chip ^ offset].astype(F32).T.astype(BF)
+            return dot(source[chip ^ offset], order, TN).astype(BF)
 
         mine, far = turned(0), turned(3)
         one, two = turned(1 + core), turned(2 - core)
@@ -298,22 +301,26 @@
             target = (s + (-1 if j % 2 else 1)) % sections
             route.append((s * space + j, target * space + j))
     across = [(s, (s + 2) % sections) for s in range(sections)]
+    token = exchange(mine[0, :16], 1)
     own, beside, diagonal, swap = call(
         functools.partial(split_kernel),
         [jax.ShapeDtypeStruct((count, 128), BF) for count in (256, 256, 256, 512)],
-        [], MIB, me, *fields,
+        [], MIB, me, *fields, token,
     )
     other = exchange(swap, 1)
     diagonal = exchange(diagonal, 6)
-    near = lax.ppermute(mine, ("section", "space"), route)
-    far = lax.ppermute(part, "section", across)
+    near, far = [], []
+    for group in range(2):
+        near.append(lax.ppermute(after(mine[group], *near), ("section", "space"), route))
+        far.append(lax.ppermute(after(part[group], *near[:group]), "section", across))
     sent = [beside, other[256:]]
+    diagonal_far = exchange(diagonal, 1)
     pieces = []
     for group in range(2):
         here = jnp.concatenate([near[group], far[group]] + (sent if group == 0 else []), axis=0)
         there = cross(here, 2, 4)
-        pieces += [here, there, exchange(here, 1), None if group else exchange(after(there, diagonal), 1)]
-    planes = [own, other, diagonal, exchange(diagonal, 1)]
+        pieces += [here, there, exchange(here, 1), None if group else exchange(after(there, diagonal, near[1], far[1]), 1)]
+    planes = [own, other, diagonal, diagonal_far]
     plane_rows = 128
 
     def plan(section, place, field):
@@ -396,7 +403,7 @@
     conv_rows = jnp.swapaxes(conv_weight, 2, 3)
     weights = jnp.concatenate([conv_rows[:, 0], mix_weight[:, 0]], axis=1)
     if paired:
-        fields = [x[:, :, 0].transpose(0, 2, 1, 3).reshape(micro_count, lanes, extent_z) for x in (inputs, cotangent)]
+        fields = [x.reshape(micro_count, lanes, extent_z) for x in (inputs, cotangent)]
         pieces, plan = gather_paired(weights, fields, me, place)
     else:
         both = jnp.stack([inputs, cotangent], axis=1)
@@ -453,8 +460,6 @@
             met = after(traded, early_terms) if group else cross(own, 2, 4)
             half = (own.astype(F32) + met.astype(F32)).astype(BF)
             other = cross(half, 4, 2)
-            if grads:
-                other = after(other, grads[0])
             kernel, parts = pair_kernel, (half, other, exchange(half, 1), exchange(other, 1))
         else:
             level = [own] + [exchange(own, k * replicas) for k in range(1, micro_count)]
@@ -464,7 +469,7 @@
             rows_of = [[m * replicas + r for r in range(replicas)] for m in range(micro_count)]
             every = lax.all_gather(level[0].astype(BF), "space", axis=0, tiled=True, axis_index_groups=rows_of)
             kernel, parts = plain_kernel, (every,)
-        grads = call(functools.partial(kernel, group, factor), outs, scratch, 4 * MIB, me, *parts, into=grads)
+        grads = call(functools.partial(kernel, group, factor), outs, scratch, MIB // 16, me, *parts, into=grads)
     conv, mix = grads
     return (jnp.swapaxes(conv, 2, 3), mix)
 

time: 81.7 us -> 76.8 us (0.940)
  waiting for transfers between devices: 32.2 us -> 21.6 us
  starting transfers between devices: 19.5 us -> 25.4 us
    ppermute x11 -> x12, waiting for transfers between devices: 7.62 us -> 3.98 us  [exchange(): return lax.ppermute(block, 'space', [(i, i ^ mask) for i in range(count)])]
    ppermute x2 -> x4, starting transfers between devices: 4.27 us -> 7.91 us  [the longest x2 7.28 us: gather_paired(): lax.ppermute(after(mine[group], *near), ('section', 'space'), route)]
    ppermute x2 -> x4, waiting for transfers between devices: 16.2 us -> 12.7 us  [the longest x2 12.7 us: gather_paired(): lax.ppermute(after(part[group], *near[:group]), 'section', across)]
    ppermute x6, waiting for transfers between devices: 8.36 us -> 5 us  [cross(): lax.ppermute(block, 'space', [(i, i ^ (second if i % 2 else first)) for i...]
    ppermute x11 -> x12, starting transfers between devices: 9.61 us -> 11.4 us  [exchange(): return lax.ppermute(block, 'space', [(i, i ^ mask) for i in range(count)])]
  transfers between devices with their start and end apart: 19 -> 22, of which waited for: 9 -> 8; matrix products, arithmetic and copies ran while one was open for 0% -> 0% of each run, Pallas kernels for 17% -> 18%
where the time goes in v3:
time: 76.8 us; the launch traced here: 76.6 us
  Pallas kernels  27.1 us (35%)
  starting transfers between devices  25.4 us (33%)
  waiting for transfers between devices  21.6 us (28%)
  other arithmetic  1.58 us (2%)
  between operations  0.86 us (1%)
    pallas_call x6, Pallas kernels, call(): pl.pallas_call(kernel, out_shape=outs, in_specs=specs, out_specs=[far if...  27.1 us
    ppermute x2, waiting for transfers between devices, gather_paired(): lax.ppermute(after(part[group], *near[:group]), 'section', across)  12.7 us
    ppermute x12, starting transfers between devices, exchange(): return lax.ppermute(block, 'space', [(i, i ^ mask) for i in range(count)])  11.4 us
    ppermute x2, starting transfers between devices, gather_paired(): lax.ppermute(after(mine[group], *near), ('section', 'space'), route)  7.28 us
    ppermute x6, starting transfers between devices, cross(): lax.ppermute(block, 'space', [(i, i ^ (second if i % 2 else first)) for i...  6.08 us
    ppermute x6, waiting for transfers between devices, cross(): lax.ppermute(block, 'space', [(i, i ^ (second if i % 2 else first)) for i...  5 us
    ppermute x12, waiting for transfers between devices, exchange(): return lax.ppermute(block, 'space', [(i, i ^ mask) for i in range(count)])  3.98 us
  transfers between devices with their start and end apart: 22, of which 8 were waited for; matrix products, arithmetic and copies ran while one was open for 0% of the time, Pallas kernels for 18%

profile of v3, /device:TPU:1, one launch (start us, length us, event | category | flops | bytes accessed | tf_op | source)
XLA Modules:
  0.0 76.6 jit_solution(5169857198478122002)
XLA Ops:
  0.7 1.3 %fusion = bf16[2,896,128]{2,1,0:T(8,128)(2,1)S(1)} fusion(bf16[2,64,128]{2,1,0:T(8,128)(2,1)} %bitcast.27, bf16[2,1728,128]{2,1,0:T(8,128)(2,1)} %bitcast.24, pred[]{:T(512)S(6)} %eq.7), kind=kLoop, calls=%fused_computation.2 | loop fusion | flops 1146880 | bytes 1835009 | tf_op jit(solution)/shard_map/jit(_where)/select_n | solution.py:296
  2.2 4.8 %collective-permute-start = (bf16[896,128]{1,0:T(8,128)(2,1)S(1)}, bf16[896,128]{1,0:T(8,128)(2,1)S(1)}, u32[]{:S(2)}, u32[]{:S(2)}) collective-permute-start(bf16[896,128]{1,0:T(8,128)(2,1)S(1)} %get-tuple-element.45), channel_id=1, source_target_pairs={{0,8},{1,25},{2,10},{3,27},{4,12},{5,29},{6,14},{7,31},{8,16},{9,1... | collective-permute-start | bytes 688136 | tf_op jit(solution)/shard_map/ppermute | solution.py:314
  7.1 0.8 %shard_map.59 = (bf16[256,128]{1,0:T(8,128)(2,1)S(1)}, bf16[256,128]{1,0:T(8,128)(2,1)S(1)}, bf16[256,128]{1,0:T(8,128)(2,1)S(1)}, bf16[512,128]{1,0:T(8,128)(2,1)S(1)}) custom-call(s32[3]{0:T(128)S(1)} %pad_add_fusion.me_ref, bf16[4,128,128]{2,1,0:T(8,128)(2,1)S(1)} %bitcast.28, bf16[4,128,128]{2,1,0:T(8,128)(2,1)S(1)} %bitcast.29, ...), custom_call_target="tpu_custom_call" | custom-call | flops 104857600 | bytes 1048576 | tf_op jit(solution)/shard_map/pallas_call | solution.py:264
  8.1 0.6 collective-permute-start.1
  8.7 0.7 collective-permute-done.3.refs_5_.refs_7_
  9.4 7.7 %collective-permute-done.1 = bf16[448,128]{1,0:T(8,128)(2,1)S(1)} collective-permute-done((bf16[448,128]{1,0:T(8,128)(2,1)S(1)}, bf16[448,128]{1,0:T(8,128)(2,1)S(1)}, u32[]{:S(2)}, u32[]{:S(2)}) %collective-permute-start.1) | collective-permute-done | bytes 114720 | tf_op jit(solution)/shard_map/ppermute | solution.py:315
  17.1 1.4 %collective-permute-start.4 = (bf16[1856,128]{1,0:T(8,128)(2,1)S(1)}, bf16[1856,128]{1,0:T(8,128)(2,1)S(1)}, u32[]{:S(2)}, u32[]{:S(2)}) collective-permute-start(bf16[1856,128]{1,0:T(8,128)(2,1)S(1)} %pad_maximum_fusion.refs_0_), channel_id=1, source_target_pairs={{0,2},{1,5},{2,0},{3,7},{4,6},{5,1},{6,4},{7,3},{8,10},{9,13},{10,... | collective-permute-start | bytes 1425416 | tf_op jit(solution)/shard_map/ppermute | solution.py:283
  18.5 2.5 %collective-permute-start.6 = (bf16[896,128]{1,0:T(8,128)(2,1)S(1)}, bf16[896,128]{1,0:T(8,128)(2,1)S(1)}, u32[]{:S(2)}, u32[]{:S(2)}) collective-permute-start(bf16[896,128]{1,0:T(8,128)(2,1)S(1)} %get-tuple-element.25), channel_id=1, source_target_pairs={{0,8},{1,25},{2,10},{3,27},{4,12},{5,29},{6,14},{7,31},{8,16},{9,1... | collective-permute-start | bytes 688136 | tf_op jit(solution)/shard_map/ppermute | solution.py:314
  21.0 1.2 %collective-permute-start.5 = (bf16[256,128]{1,0:T(8,128)(2,1)S(1)}, bf16[256,128]{1,0:T(8,128)(2,1)S(1)}, u32[]{:S(2)}, u32[]{:S(2)}) collective-permute-start(bf16[256,128]{1,0:T(8,128)(2,1)S(1)} %get-tuple-element.24), channel_id=1, source_target_pairs={{0,6},{1,7},{2,4},{3,5},{4,2},{5,3},{6,0},{7,1},{8,14},{9,15},{10,... | collective-permute-start | bytes 196616 | tf_op jit(solution)/shard_map/ppermute | solution.py:278
  22.1 2.2 %collective-permute-start.11 = (bf16[1856,128]{1,0:T(8,128)(2,1)S(1)}, bf16[1856,128]{1,0:T(8,128)(2,1)S(1)}, u32[]{:S(2)}, u32[]{:S(2)}) collective-permute-start(bf16[1856,128]{1,0:T(8,128)(2,1)S(1)} %pad_maximum_fusion.refs_0_), channel_id=1, source_target_pairs={{0,1},{1,0},{2,3},{3,2},{4,5},{5,4},{6,7},{7,6},{8,9},{9,8},{10,11... | collective-permute-start | bytes 1425416 | tf_op jit(solution)/shard_map/ppermute | solution.py:278
  24.3 1.7 %collective-permute-done.5.refs_6_.refs_8_ = bf16[256,128]{1,0:T(8,128)(2,1)S(1)} collective-permute-done((bf16[256,128]{1,0:T(8,128)(2,1)S(1)}, bf16[256,128]{1,0:T(8,128)(2,1)S(1)}, u32[]{:S(2)}, u32[]{:S(2)}) %collective-permute-start.5) | collective-permute-done | bytes 65568 | tf_op jit(solution)/shard_map/ppermute | solution.py:278
  26.0 5.0 %collective-permute-done.7 = bf16[448,128]{1,0:T(8,128)(2,1)S(1)} collective-permute-done((bf16[448,128]{1,0:T(8,128)(2,1)S(1)}, bf16[448,128]{1,0:T(8,128)(2,1)S(1)}, u32[]{:S(2)}, u32[]{:S(2)}) %collective-permute-start.7) | collective-permute-done | bytes 114720 | tf_op jit(solution)/shard_map/ppermute | solution.py:315
  31.0 0.1 collective-permute-start.8
  31.2 0.4 collective-permute-start.12
  31.6 1.2 %collective-permute-start.9 = (bf16[1344,128]{1,0:T(8,128)(2,1)S(1)}, bf16[1344,128]{1,0:T(8,128)(2,1)S(1)}, u32[]{:S(2)}, u32[]{:S(2)}) collective-permute-start(bf16[1344,128]{1,0:T(8,128)(2,1)S(1)} %constant_dynamic-update-slice_fusion.refs_2_), channel_id=1, source_target_pairs={{0,2},{1,5},{2,0},{3,7},{4,6},{5,1},{6,4},{7,3},{8,10},{9,13},{10,... | collective-permute-start | bytes 1032200 | tf_op jit(solution)/shard_map/ppermute | solution.py:283
  32.8 0.2 collective-permute-done.12.refs_7_.refs_9_
  33.0 6.1 %shard_map.60 = (f32[1024,128]{1,0:T(8,128)S(1)}, bf16[4,1280,256]{2,1,0:T(8,128)(2,1)S(1)}, bf16[4,1024,256]{2,1,0:T(8,128)(2,1)S(1)}, bf16[2,10,128,384]{3,2,1,0:T(8,128)(2,1)S(1)}, bf16[2,1024,256]{2,1,0:T(8,128)(2,1)S(1)}) custom-call(s32[3]{0:T(128)S(1)} %pad_add_fusion.me_ref, bf16[2,1,1728,128]{3,2,1,0:T(8,128)(2,1)S(1)} %bitcast.25, ...), custom_call_target="tpu_custom_call" | custom-call | flops 3145728000 | bytes 31457280 | tf_op jit(solution)/shard_map/pallas_call | solution.py:264
  39.1 0.4 collective-permute-start.13
  39.5 1.3 %collective-permute-done.13.refs_5_ = bf16[1344,128]{1,0:T(8,128)(2,1)S(1)} collective-permute-done((bf16[1344,128]{1,0:T(8,128)(2,1)S(1)}, bf16[1344,128]{1,0:T(8,128)(2,1)S(1)}, u32[]{:S(2)}, u32[]{:S(2)}) %collective-permute-start.13) | collective-permute-done | bytes 344096 | tf_op jit(solution)/shard_map/ppermute | solution.py:278
  40.8 11.7 %shard_map.61 = (f32[1024,128]{1,0:T(8,128)S(1)}, bf16[896,128]{1,0:T(8,128)(2,1)S(1)}) custom-call(s32[3]{0:T(128)S(1)} %pad_add_fusion.me_ref, bf16[2,1,1728,128]{3,2,1,0:T(8,128)(2,1)S(1)} %bitcast.26, bf16[2,1,64,128]{3,2,1,0:T(8,128)(2,1)S(1)} %copy-done.1, bf16[1856,128]{1,0:T(8,128)(2,1)S(1)} %collective-permute-done.4.refs_1_.refs_0_, ...), custom_call_target="tpu_custom_call" | custom-call | flops 4194304000 | bytes 41943040 | tf_op jit(solution)/shard_map/pallas_call | solution.py:264
  52.5 1.2 %collective-permute-start.18 = (bf16[896,128]{1,0:T(8,128)(2,1)S(1)}, bf16[896,128]{1,0:T(8,128)(2,1)S(1)}, u32[]{:S(2)}, u32[]{:S(2)}) collective-permute-start(bf16[896,128]{1,0:T(8,128)(2,1)S(1)} %get-tuple-element.36), channel_id=1, source_target_pairs={{0,2},{1,5},{2,0},{3,7},{4,6},{5,1},{6,4},{7,3},{8,10},{9,13},{10,... | collective-permute-start | bytes 688136 | tf_op jit(solution)/shard_map/ppermute | solution.py:283
  53.7 5.3 %shard_map.62 = bf16[896,128]{1,0:T(8,128)(2,1)S(1)} custom-call(s32[3]{0:T(128)S(1)} %pad_add_fusion.me_ref, f32[1024,128]{1,0:T(8,128)S(1)} %get-tuple-element.31.up_in, bf16[4,1280,256]{2,1,0:T(8,128)(2,1)S(1)} %get-tuple-element.32.folded, bf16[4,1024,256]{2,1,0:T(8,128)(2,1)S(1)} %get-tuple-element.33.slope, ...), custom_call_target="tpu_custom_call" | custom-call | flops 2097152000 | bytes 20971520 | tf_op jit(solution)/shard_map/pallas_call | solution.py:264
  59.0 0.4 collective-permute-start.14
  59.5 0.6 collective-permute-start.19
  60.1 4.8 %collective-permute-done.14 = bf16[896,128]{1,0:T(8,128)(2,1)S(1)} collective-permute-done((bf16[896,128]{1,0:T(8,128)(2,1)S(1)}, bf16[896,128]{1,0:T(8,128)(2,1)S(1)}, u32[]{:S(2)}, u32[]{:S(2)}) %collective-permute-start.14) | collective-permute-done | bytes 229408 | tf_op jit(solution)/shard_map/ppermute | solution.py:283
  65.0 1.3 %collective-permute-start.15 = (bf16[896,128]{1,0:T(8,128)(2,1)S(1)}, bf16[896,128]{1,0:T(8,128)(2,1)S(1)}, u32[]{:S(2)}, u32[]{:S(2)}) collective-permute-start(bf16[896,128]{1,0:T(8,128)(2,1)S(1)} %add_convert_fusion.1.own_a), channel_id=1, source_target_pairs={{0,4},{1,3},{2,6},{3,1},{4,0},{5,7},{6,2},{7,5},{8,12},{9,11},{10,... | collective-permute-start | bytes 688136 | tf_op jit(solution)/shard_map/ppermute | solution.py:283
  66.2 3.0 %collective-permute-start.20 = (bf16[896,128]{1,0:T(8,128)(2,1)S(1)}, bf16[896,128]{1,0:T(8,128)(2,1)S(1)}, u32[]{:S(2)}, u32[]{:S(2)}) collective-permute-start(bf16[896,128]{1,0:T(8,128)(2,1)S(1)} %add_convert_fusion.own_a), channel_id=1, source_target_pairs={{0,1},{1,0},{2,3},{3,2},{4,5},{5,4},{6,7},{7,6},{8,9},{9,8},{10,11... | collective-permute-start | bytes 688136 | tf_op jit(solution)/shard_map/ppermute | solution.py:278
  69.2 0.5 collective-permute-start.16
  69.7 0.2 collective-permute-done.15.own_b
  69.9 3.5 %collective-permute-start.17 = (bf16[896,128]{1,0:T(8,128)(2,1)S(1)}, bf16[896,128]{1,0:T(8,128)(2,1)S(1)}, u32[]{:S(2)}, u32[]{:S(2)}) collective-permute-start(bf16[896,128]{1,0:T(8,128)(2,1)S(1)} %collective-permute-done.15.own_b), channel_id=1, source_target_pairs={{0,1},{1,0},{2,3},{3,2},{4,5},{5,4},{6,7},{7,6},{8,9},{9,8},{10,11... | collective-permute-start | bytes 688136 | tf_op jit(solution)/shard_map/ppermute | solution.py:278
  73.4 1.6 %shard_map.63 = (f32[2,1,1728,128]{3,2,1,0:T(8,128)}, f32[2,1,64,128]{3,2,1,0:T(8,128)}) custom-call(s32[3]{0:T(128)S(1)} %pad_add_fusion.me_ref, bf16[896,128]{1,0:T(8,128)(2,1)S(1)} %add_convert_fusion.own_a, bf16[896,128]{1,0:T(8,128)(2,1)S(1)} %collective-permute-done.19.own_b, bf16[896,128]{1,0:T(8,128)(2,1)S(1)} %collective-permute-done.20.far_a, ...), custom_call_target="tpu_custom_call" | custom-call | flops 6553600 | bytes 65536 | tf_op jit(solution)/shard_map/pallas_call | solution.py:264
  75.0 1.6 %shard_map.64 = (f32[2,1,1728,128]{3,2,1,0:T(8,128)}, f32[2,1,64,128]{3,2,1,0:T(8,128)}) custom-call(s32[3]{0:T(128)S(1)} %pad_add_fusion.me_ref, bf16[896,128]{1,0:T(8,128)(2,1)S(1)} %add_convert_fusion.1.own_a, bf16[896,128]{1,0:T(8,128)(2,1)S(1)} %collective-permute-done.15.own_b, ...), custom_call_target="tpu_custom_call", output_to_operand_aliasing={{0}: (5, {}), {1}: (6, {})} | custom-call | flops 6553600 | bytes 65536 | tf_op jit(solution)/shard_map/pallas_call | solution.py:264
  (37 shorter events, 0.6 us)
Async XLA Ops:
  0.6 6.5 %copy-start.3 = (bf16[4,64,1,2,128]{4,3,2,1,0:T(2,128)(2,1)S(1)}, bf16[4,64,1,2,128]{4,3,2,1,0:T(2,128)(2,1)}, u32[]{:S(2)}) copy-start(bf16[4,64,1,2,128]{4,3,2,1,0:T(2,128)(2,1)} %param.5) | copy-start | bytes 393220
  0.6 6.5 %copy-start.2 = (bf16[4,64,1,2,128]{4,3,2,1,0:T(2,128)(2,1)S(1)}, bf16[4,64,1,2,128]{4,3,2,1,0:T(2,128)(2,1)}, u32[]{:S(2)}) copy-start(bf16[4,64,1,2,128]{4,3,2,1,0:T(2,128)(2,1)} %param.4) | copy-start | bytes 393220
  2.0 30.9 %copy-start = (bf16[2,1,128,1728]{2,3,1,0:T(8,128)(2,1)S(1)}, bf16[2,1,128,1728]{2,3,1,0:T(8,128)(2,1)}, u32[]{:S(2)}) copy-start(bf16[2,1,128,1728]{2,3,1,0:T(8,128)(2,1)} %param.6) | copy-start | bytes 2654212
  2.1 30.9 %copy-start.1 = (bf16[2,1,64,128]{3,2,1,0:T(8,128)(2,1)S(1)}, bf16[2,1,64,128]{3,2,1,0:T(8,128)(2,1)}, u32[]{:S(2)}) copy-start(bf16[2,1,64,128]{3,2,1,0:T(8,128)(2,1)} %mix.3) | copy-start | bytes 98308
  2.1 5.1 %collective-permute-start.2 = (bf16[16,128]{1,0:T(8,128)(2,1)S(1)}, bf16[16,128]{1,0:T(8,128)(2,1)S(1)}, u32[]{:S(2)}, u32[]{:S(2)}) collective-permute-start(bf16[16,128]{1,0:T(8,128)(2,1)S(1)} %slice_bitcast_fusion.2), channel_id=1, source_target_pairs={{0,1},{1,0},{2,3},{3,2},{4,5},{5,4},{6,7},{7,6},{8,9},{9,8},{10,11... | collective-permute-start | bytes 12296 | tf_op jit(solution)/shard_map/ppermute | solution.py:278
  2.2 14.8 %collective-permute-start = (bf16[896,128]{1,0:T(8,128)(2,1)S(1)}, bf16[896,128]{1,0:T(8,128)(2,1)S(1)}, u32[]{:S(2)}, u32[]{:S(2)}) collective-permute-start(bf16[896,128]{1,0:T(8,128)(2,1)S(1)} %get-tuple-element.45), channel_id=1, source_target_pairs={{0,8},{1,25},{2,10},{3,27},{4,12},{5,29},{6,14},{7,31},{8,16},{9,1... | collective-permute-start | bytes 688136 | tf_op jit(solution)/shard_map/ppermute | solution.py:314
  8.0 1.4 %collective-permute-start.3 = (bf16[512,128]{1,0:T(8,128)(2,1)S(1)}, bf16[512,128]{1,0:T(8,128)(2,1)S(1)}, u32[]{:S(2)}, u32[]{:S(2)}) collective-permute-start(bf16[512,128]{1,0:T(8,128)(2,1)S(1)} %get-tuple-element.23), channel_id=1, source_target_pairs={{0,1},{1,0},{2,3},{3,2},{4,5},{5,4},{6,7},{7,6},{8,9},{9,8},{10,11... | collective-permute-start | bytes 393224 | tf_op jit(solution)/shard_map/ppermute | solution.py:278
  8.1 9.0 %collective-permute-start.1 = (bf16[448,128]{1,0:T(8,128)(2,1)S(1)}, bf16[448,128]{1,0:T(8,128)(2,1)S(1)}, u32[]{:S(2)}, u32[]{:S(2)}) collective-permute-start(bf16[448,128]{1,0:T(8,128)(2,1)S(1)} %get-tuple-element.43), channel_id=1, source_target_pairs={{0,16},{8,24},{16,0},{24,8},{1,17},{9,25},{17,1},{25,9},{2,18},{10... | collective-permute-start | bytes 344072 | tf_op jit(solution)/shard_map/ppermute | solution.py:315
  17.1 13.9 %collective-permute-start.4 = (bf16[1856,128]{1,0:T(8,128)(2,1)S(1)}, bf16[1856,128]{1,0:T(8,128)(2,1)S(1)}, u32[]{:S(2)}, u32[]{:S(2)}) collective-permute-start(bf16[1856,128]{1,0:T(8,128)(2,1)S(1)} %pad_maximum_fusion.refs_0_), channel_id=1, source_target_pairs={{0,2},{1,5},{2,0},{3,7},{4,6},{5,1},{6,4},{7,3},{8,10},{9,13},{10,... | collective-permute-start | bytes 1425416 | tf_op jit(solution)/shard_map/ppermute | solution.py:283
  18.5 12.5 %collective-permute-start.6 = (bf16[896,128]{1,0:T(8,128)(2,1)S(1)}, bf16[896,128]{1,0:T(8,128)(2,1)S(1)}, u32[]{:S(2)}, u32[]{:S(2)}) collective-permute-start(bf16[896,128]{1,0:T(8,128)(2,1)S(1)} %get-tuple-element.25), channel_id=1, source_target_pairs={{0,8},{1,25},{2,10},{3,27},{4,12},{5,29},{6,14},{7,31},{8,16},{9,1... | collective-permute-start | bytes 688136 | tf_op jit(solution)/shard_map/ppermute | solution.py:314
  21.0 10.1 %collective-permute-start.7 = (bf16[448,128]{1,0:T(8,128)(2,1)S(1)}, bf16[448,128]{1,0:T(8,128)(2,1)S(1)}, u32[]{:S(2)}, u32[]{:S(2)}) collective-permute-start(bf16[448,128]{1,0:T(8,128)(2,1)S(1)} %get-tuple-element.26), channel_id=1, source_target_pairs={{0,16},{8,24},{16,0},{24,8},{1,17},{9,25},{17,1},{25,9},{2,18},{10... | collective-permute-start | bytes 344072 | tf_op jit(solution)/shard_map/ppermute | solution.py:315
  21.0 5.1 %collective-permute-start.5 = (bf16[256,128]{1,0:T(8,128)(2,1)S(1)}, bf16[256,128]{1,0:T(8,128)(2,1)S(1)}, u32[]{:S(2)}, u32[]{:S(2)}) collective-permute-start(bf16[256,128]{1,0:T(8,128)(2,1)S(1)} %get-tuple-element.24), channel_id=1, source_target_pairs={{0,6},{1,7},{2,4},{3,5},{4,2},{5,3},{6,0},{7,1},{8,14},{9,15},{10,... | collective-permute-start | bytes 196616 | tf_op jit(solution)/shard_map/ppermute | solution.py:278
  22.1 10.9 %collective-permute-start.11 = (bf16[1856,128]{1,0:T(8,128)(2,1)S(1)}, bf16[1856,128]{1,0:T(8,128)(2,1)S(1)}, u32[]{:S(2)}, u32[]{:S(2)}) collective-permute-start(bf16[1856,128]{1,0:T(8,128)(2,1)S(1)} %pad_maximum_fusion.refs_0_), channel_id=1, source_target_pairs={{0,1},{1,0},{2,3},{3,2},{4,5},{5,4},{6,7},{7,6},{8,9},{9,8},{10,11... | collective-permute-start | bytes 1425416 | tf_op jit(solution)/shard_map/ppermute | solution.py:278
  31.0 1.9 %collective-permute-start.8 = (bf16[1856,128]{1,0:T(8,128)(2,1)S(1)}, bf16[1856,128]{1,0:T(8,128)(2,1)S(1)}, u32[]{:S(2)}, u32[]{:S(2)}) collective-permute-start(bf16[1856,128]{1,0:T(8,128)(2,1)S(1)} %collective-permute-done.4.refs_1_.refs_0_), channel_id=1, source_target_pairs={{0,1},{1,0},{2,3},{3,2},{4,5},{5,4},{6,7},{7,6},{8,9},{9,8},{10,11... | collective-permute-start | bytes 1425416 | tf_op jit(solution)/shard_map/ppermute | solution.py:278
  31.2 1.8 %collective-permute-start.12 = (bf16[256,128]{1,0:T(8,128)(2,1)S(1)}, bf16[256,128]{1,0:T(8,128)(2,1)S(1)}, u32[]{:S(2)}, u32[]{:S(2)}) collective-permute-start(bf16[256,128]{1,0:T(8,128)(2,1)S(1)} %collective-permute-done.5.refs_6_.refs_8_), channel_id=1, source_target_pairs={{0,1},{1,0},{2,3},{3,2},{4,5},{5,4},{6,7},{7,6},{8,9},{9,8},{10,11... | collective-permute-start | bytes 196616 | tf_op jit(solution)/shard_map/ppermute | solution.py:278
  31.6 7.5 %collective-permute-start.9 = (bf16[1344,128]{1,0:T(8,128)(2,1)S(1)}, bf16[1344,128]{1,0:T(8,128)(2,1)S(1)}, u32[]{:S(2)}, u32[]{:S(2)}) collective-permute-start(bf16[1344,128]{1,0:T(8,128)(2,1)S(1)} %constant_dynamic-update-slice_fusion.refs_2_), channel_id=1, source_target_pairs={{0,2},{1,5},{2,0},{3,7},{4,6},{5,1},{6,4},{7,3},{8,10},{9,13},{10,... | collective-permute-start | bytes 1032200 | tf_op jit(solution)/shard_map/ppermute | solution.py:283
  32.7 6.7 %collective-permute-start.10 = (bf16[1344,128]{1,0:T(8,128)(2,1)S(1)}, bf16[1344,128]{1,0:T(8,128)(2,1)S(1)}, u32[]{:S(2)}, u32[]{:S(2)}) collective-permute-start(bf16[1344,128]{1,0:T(8,128)(2,1)S(1)} %constant_dynamic-update-slice_fusion.refs_2_), channel_id=1, source_target_pairs={{0,1},{1,0},{2,3},{3,2},{4,5},{5,4},{6,7},{7,6},{8,9},{9,8},{10,11... | collective-permute-start | bytes 1032200 | tf_op jit(solution)/shard_map/ppermute | solution.py:278
  39.1 1.7 %collective-permute-start.13 = (bf16[1344,128]{1,0:T(8,128)(2,1)S(1)}, bf16[1344,128]{1,0:T(8,128)(2,1)S(1)}, u32[]{:S(2)}, u32[]{:S(2)}) collective-permute-start(bf16[1344,128]{1,0:T(8,128)(2,1)S(1)} %collective-permute-done.9.refs_3_), channel_id=1, source_target_pairs={{0,1},{1,0},{2,3},{3,2},{4,5},{5,4},{6,7},{7,6},{8,9},{9,8},{10,11... | collective-permute-start | bytes 1032200 | tf_op jit(solution)/shard_map/ppermute | solution.py:278
  52.5 6.9 %collective-permute-start.18 = (bf16[896,128]{1,0:T(8,128)(2,1)S(1)}, bf16[896,128]{1,0:T(8,128)(2,1)S(1)}, u32[]{:S(2)}, u32[]{:S(2)}) collective-permute-start(bf16[896,128]{1,0:T(8,128)(2,1)S(1)} %get-tuple-element.36), channel_id=1, source_target_pairs={{0,2},{1,5},{2,0},{3,7},{4,6},{5,1},{6,4},{7,3},{8,10},{9,13},{10,... | collective-permute-start | bytes 688136 | tf_op jit(solution)/shard_map/ppermute | solution.py:283
  59.0 5.9 %collective-permute-start.14 = (bf16[896,128]{1,0:T(8,128)(2,1)S(1)}, bf16[896,128]{1,0:T(8,128)(2,1)S(1)}, u32[]{:S(2)}, u32[]{:S(2)}) collective-permute-start(bf16[896,128]{1,0:T(8,128)(2,1)S(1)} %shard_map.62), channel_id=1, source_target_pairs={{0,2},{1,5},{2,0},{3,7},{4,6},{5,1},{6,4},{7,3},{8,10},{9,13},{10,... | collective-permute-start | bytes 688136 | tf_op jit(solution)/shard_map/ppermute | solution.py:283
  59.5 9.7 %collective-permute-start.19 = (bf16[896,128]{1,0:T(8,128)(2,1)S(1)}, bf16[896,128]{1,0:T(8,128)(2,1)S(1)}, u32[]{:S(2)}, u32[]{:S(2)}) collective-permute-start(bf16[896,128]{1,0:T(8,128)(2,1)S(1)} %add_convert_fusion.own_a), channel_id=1, source_target_pairs={{0,4},{1,3},{2,6},{3,1},{4,0},{5,7},{6,2},{7,5},{8,12},{9,11},{10,... | collective-permute-start | bytes 688136 | tf_op jit(solution)/shard_map/ppermute | solution.py:283
  65.0 4.9 %collective-permute-start.15 = (bf16[896,128]{1,0:T(8,128)(2,1)S(1)}, bf16[896,128]{1,0:T(8,128)(2,1)S(1)}, u32[]{:S(2)}, u32[]{:S(2)}) collective-permute-start(bf16[896,128]{1,0:T(8,128)(2,1)S(1)} %add_convert_fusion.1.own_a), channel_id=1, source_target_pairs={{0,4},{1,3},{2,6},{3,1},{4,0},{5,7},{6,2},{7,5},{8,12},{9,11},{10,... | collective-permute-start | bytes 688136 | tf_op jit(solution)/shard_map/ppermute | solution.py:283
  66.2 7.2 %collective-permute-start.20 = (bf16[896,128]{1,0:T(8,128)(2,1)S(1)}, bf16[896,128]{1,0:T(8,128)(2,1)S(1)}, u32[]{:S(2)}, u32[]{:S(2)}) collective-permute-start(bf16[896,128]{1,0:T(8,128)(2,1)S(1)} %add_convert_fusion.own_a), channel_id=1, source_target_pairs={{0,1},{1,0},{2,3},{3,2},{4,5},{5,4},{6,7},{7,6},{8,9},{9,8},{10,11... | collective-permute-start | bytes 688136 | tf_op jit(solution)/shard_map/ppermute | solution.py:278
  69.2 4.2 %collective-permute-start.21 = (bf16[896,128]{1,0:T(8,128)(2,1)S(1)}, bf16[896,128]{1,0:T(8,128)(2,1)S(1)}, u32[]{:S(2)}, u32[]{:S(2)}) collective-permute-start(bf16[896,128]{1,0:T(8,128)(2,1)S(1)} %collective-permute-done.19.own_b), channel_id=1, source_target_pairs={{0,1},{1,0},{2,3},{3,2},{4,5},{5,4},{6,7},{7,6},{8,9},{9,8},{10,11... | collective-permute-start | bytes 688136 | tf_op jit(solution)/shard_map/ppermute | solution.py:278
  69.2 5.8 %collective-permute-start.16 = (bf16[896,128]{1,0:T(8,128)(2,1)S(1)}, bf16[896,128]{1,0:T(8,128)(2,1)S(1)}, u32[]{:S(2)}, u32[]{:S(2)}) collective-permute-start(bf16[896,128]{1,0:T(8,128)(2,1)S(1)} %add_convert_fusion.1.own_a), channel_id=1, source_target_pairs={{0,1},{1,0},{2,3},{3,2},{4,5},{5,4},{6,7},{7,6},{8,9},{9,8},{10,11... | collective-permute-start | bytes 688136 | tf_op jit(solution)/shard_map/ppermute | solution.py:278
  69.9 5.1 %collective-permute-start.17 = (bf16[896,128]{1,0:T(8,128)(2,1)S(1)}, bf16[896,128]{1,0:T(8,128)(2,1)S(1)}, u32[]{:S(2)}, u32[]{:S(2)}) collective-permute-start(bf16[896,128]{1,0:T(8,128)(2,1)S(1)} %collective-permute-done.15.own_b), channel_id=1, source_target_pairs={{0,1},{1,0},{2,3},{3,2},{4,5},{5,4},{6,7},{7,6},{8,9},{9,8},{10,11... | collective-permute-start | bytes 688136 | tf_op jit(solution)/shard_map/ppermute | solution.py:278

commit v4 on v3

--- a/solution.py
+++ b/solution.py
@@ -14,6 +14,10 @@
 NN = (((1,), (0,)), ((), ()))
 TN = (((0,), (0,)), ((), ()))
 MIB = 1024 * 1024
+SHARES = (
+    (0, 3, 6, 1, 4, 7, 2, 5, 8, 9, 12, 15, 10, 13),
+    (16, 11, 14, 17, 18, 21, 24, 19, 22, 25, 20, 23, 26, 27),
+)
 
 
 def dot(a, b, dims):
@@ -63,36 +67,51 @@
     keep_h[slot] = hidden
 
 
-def term_rows(conv, mix, terms):
-    def block(at, y, other):
-        return conv[at + 64 * y : at + 64 * y + 64, 128 * other : 128 * other + 128]
-
-    for dx in range(3):
-        for dz in range(3):
-            row = 64 * (9 * dx + 3 + dz)
-            at = 128 * (3 * dx + dz)
-            terms[row : row + 64] = (block(at, 0, 0) + block(at, 1, 1)).astype(BF)
-            terms[row - 192 : row - 128] = block(at, 0, 1).astype(BF)
-            terms[row + 192 : row + 256] = block(at, 1, 0).astype(BF)
-    terms[1728:1792] = (mix[:64, :128] + mix[64:, 128:]).astype(BF)
-
-
-def backward_layer(layer, owned, up, wide, folded, slope, keep_a, keep_h, terms, spread_if):
+def term_rows(blocks, base, conv, mix, terms):
+    for number, tap in enumerate(blocks):
+        at = 128 * (3 * (tap // 9) + tap % 3 - base)
+        if tap == 27:
+            value = mix[:64, :128] + mix[64:, 128:]
+        elif tap // 3 % 3 == 1:
+            value = conv[at : at + 64, :128] + conv[at + 64 : at + 128, 128:]
+        elif tap // 3 % 3 == 0:
+            value = conv[at : at + 64, 128:]
+        else:
+            value = conv[at + 64 : at + 128, :128]
+        terms[64 * number : 64 * number + 64] = value.astype(BF)
+
+
+def some_columns(padded, groups):
+    planes = padded.shape[0] - 2
+    parts = []
+    for d in range(3):
+        inside = [g - 3 * d for g in groups if g // 3 == d]
+        if inside:
+            parts.append(padded[d : d + planes, :, 128 * inside[0] : 128 * inside[-1] + 128])
+    return jnp.concatenate(parts, axis=2).reshape(planes * padded.shape[1], 128 * len(groups))
+
+
+def backward_layer(shares, mine, layer, owned, up, grad, wide, folded, slope, keep_a, keep_h, terms, spread_if):
     planes = wide.shape[0] - 2
     length = wide.shape[1]
     now = up[...]
-    up_low = now.astype(BF)
-    grad = (dot(up_low, folded[layer, 1152:], NN) * slope[layer]).astype(BF)
-
-    @pl.when(owned)
-    def _():
-        conv = dot(columns_of(keep_a.at[0]), grad, TN)
-        term_rows(conv, dot(up_low, keep_h[0], TN), terms)
-
-    @pl.when(spread_if)
-    def _():
-        wide[1 : planes + 1] = dot(grad, folded[layer, :1152], NT).reshape(planes, length, 1152)
-        total = now
+    half = now.shape[0] // 2
+    for rows in (slice(0, half), slice(half, 2 * half)):
+        hid_grad = dot(now[rows].astype(BF), folded[layer, 1152:], NN)
+        grad[rows] = (hid_grad * slope[layer, rows]).astype(BF)
+
+    for replica, blocks in enumerate(shares):
+        groups = sorted({3 * (tap // 9) + tap % 3 for tap in blocks if tap < 27})
+
+        @pl.when(owned & (mine == replica) if len(shares) > 1 else owned)
+        def _(blocks=blocks, groups=groups):
+            conv = dot(some_columns(keep_a.at[0], groups), grad[...], TN)
+            mix = dot(up[...].astype(BF), keep_h[0], TN) if 27 in blocks else None
+            term_rows(blocks, groups[0], conv, mix, terms)
+
+    def spread():
+        wide[1 : planes + 1] = dot(grad[...], folded[layer, :1152], NT).reshape(planes, length, 1152)
+        total = up[...]
         for dz in range(3):
             part = 0.0
             for dx in range(3):
@@ -101,6 +120,11 @@
             part = part.reshape(planes * length, 128)
             total = total + (part if dz == 1 else shifted(part, dz - 1, length))
         up[...] = total
+
+    if spread_if is None:
+        spread()
+    else:
+        pl.when(spread_if)(spread)
 
 
 def clear_edges(ref):
@@ -181,24 +205,28 @@
     lax.fori_loop(0, folded.shape[0], step, 0)
 
 
-def all_back(section, last, up, wide, folded, slope, keep_a, keep_h, terms, replica, out):
+def all_back(shares, me_ref, last, up, grad, wide, folded, slope, keep_a, keep_h, terms, out):
+    section, replica = me_ref[0], me_ref[2]
     sections = folded.shape[0]
+    target = out if len(shares) > 1 else terms
 
     def back(i, carry):
         layer = sections - 1 - i
+        spread_if = None if last else layer > 0
         backward_layer(
-            layer, layer == section, up, wide, folded, slope, keep_a, keep_h, terms, (layer >= 0) if last else layer > 0
+            shares, replica, layer, layer == section, up, grad, wide, folded, slope, keep_a, keep_h, target, spread_if
         )
         return carry
 
     lax.fori_loop(0, sections, back, 0)
-    rows = out.shape[0]
-    out[...] = terms[pl.ds(pl.multiple_of(replica * rows, rows), rows)]
-
-
-def second_kernel(plan, piece_count, me_ref, conv, mix, *refs):
+    if len(shares) == 1:
+        rows = out.shape[0]
+        out[...] = terms[pl.ds(pl.multiple_of(replica * rows, rows), rows)]
+
+
+def second_kernel(shares, plan, piece_count, me_ref, conv, mix, *refs):
     pieces, refs = refs[:piece_count], refs[piece_count:]
-    act_in, up, out, folded, slope, keep_a, keep_h, act, wide, terms = refs
+    act_in, up, out, folded, slope, keep_a, keep_h, act, wide, terms, grad = refs
     section = me_ref[0]
     act[...] = act_in[...]
     take(plan, me_ref, 1, 1, conv, mix, pieces, folded, up)
@@ -211,41 +239,54 @@
         return carry
 
     lax.fori_loop(0, folded.shape[0], step, 0)
-    all_back(section, True, up, wide, folded, slope, keep_a, keep_h, terms, me_ref[2], out)
-
-
-def third_kernel(me_ref, up_in, folded, slope, keep_a, keep_h, out, up, wide, terms):
+    all_back(shares, me_ref, True, up, grad, wide, folded, slope, keep_a, keep_h, terms, out)
+
+
+def third_kernel(shares, me_ref, up_in, folded, slope, keep_a, keep_h, out, up, wide, terms, grad):
     up[...] = up_in[...]
     clear_edges(wide)
-    all_back(me_ref[0], False, up, wide, folded, slope, keep_a, keep_h, terms, me_ref[2], out)
-
-
-def send_grads(whole, conv, mix, group, start, stop, sems):
-    taps = conv.shape[2]
-    count = min(stop, taps) - start
-    copies = [(whole.at[pl.ds(start, count)], conv.at[group, 0, pl.ds(start, count)])]
-    if stop > taps:
-        copies.append((whole.at[pl.ds(taps, stop - taps)], mix.at[group, 0]))
-    return begin(copies, sems, 1 if start else 0)
-
-
-def pair_kernel(group, factor, me_ref, own_a, own_b, far_a, far_b, *refs):
+    all_back(shares, me_ref, False, up, grad, wide, folded, slope, keep_a, keep_h, terms, out)
+
+
+def send_taps(taps, factor, value, conv, mix, group, whole, sems):
+    for number, tap in enumerate(taps):
+        whole[64 * tap : 64 * tap + 64] = value[64 * number : 64 * number + 64] * factor
+    runs = []
+    for tap in sorted(taps):
+        if runs and tap < 27 and tap == runs[-1][1]:
+            runs[-1][1] += 1
+        else:
+            runs.append([tap, tap + 1])
+    copies = []
+    for start, stop in runs:
+        rows = pl.ds(64 * start, 64 * (stop - start))
+        copies.append((whole.at[rows], mix.at[group, 0] if start == 27 else conv.at[group, 0, rows]))
+    return begin(copies, sems, 0)
+
+
+def pair_kernel(group, factor, swapped, me_ref, a, b, *refs):
+    conv, mix, whole, sems = refs[-4:]
+    for core in range(2):
+
+        @pl.when((me_ref[2] ^ swapped) == core)
+        def _(core=core):
+            value = a[...].astype(F32) + b[...].astype(F32)
+            finish(send_taps(SHARES[core], factor, value, conv, mix, group, whole, sems))
+
+
+def both_kernel(group, factor, me_ref, own_a, own_b, far_a, far_b, *refs):
     conv, mix, whole, sems = refs[-4:]
     first = me_ref[2] == 0
-    rows = own_a.shape[0]
     own = own_a[...].astype(F32) + own_b[...].astype(F32)
     far = far_a[...].astype(F32) + far_b[...].astype(F32)
-    whole[:rows] = jnp.where(first, own, far) * factor
-    started = send_grads(whole, conv, mix, group, 0, rows, sems)
-    whole[rows:] = jnp.where(first, far, own) * factor
-    started += send_grads(whole, conv, mix, group, rows, 2 * rows, sems)
+    started = send_taps(SHARES[0], factor, jnp.where(first, own, far), conv, mix, group, whole, sems.at[0])
+    started += send_taps(SHARES[1], factor, jnp.where(first, far, own), conv, mix, group, whole, sems.at[1])
     finish(started)
 
 
 def plain_kernel(group, factor, me_ref, terms, *refs):
     conv, mix, whole, sems = refs[-4:]
-    whole[...] = terms[...].astype(F32) * factor
-    finish(send_grads(whole, conv, mix, group, 0, whole.shape[0], sems))
+    finish(send_taps(range(28), factor, terms[...].astype(F32), conv, mix, group, whole, sems.at[0]))
 
 
 def size_of(x):
@@ -265,7 +306,7 @@
         kernel,
         out_shape=outs,
         in_specs=specs,
-        out_specs=[far if kernel.func in (pair_kernel, plain_kernel) else vmem] * len(outs),
+        out_specs=[far if kernel.func in (pair_kernel, both_kernel, plain_kernel) else vmem] * len(outs),
         scratch_shapes=scratch,
         input_output_aliases={len(args) + i: i for i in range(len(into))},
         compiler_params=pltpu.CompilerParams(vmem_limit_bytes=limit),
@@ -429,20 +470,22 @@
         pieces[7] = exchange(after(pieces[5], act), 1)
     late = [pieces[i] for i in needed(plan, 1, 1)]
     terms = jax.ShapeDtypeStruct((width // replicas, hidden), BF)
+    shares = SHARES if paired else (tuple(range(28)),)
     wide = pltpu.VMEM((total_x + 2, extent_z, 9 * lanes), F32)
     whole = pltpu.VMEM((width, hidden), BF)
+    grad = pltpu.VMEM((cells, 2 * hidden), BF)
     up, late_terms = call(
-        functools.partial(second_kernel, plan, len(late)),
+        functools.partial(second_kernel, shares, plan, len(late)),
         [act, terms],
-        [pltpu.VMEM(x.shape, x.dtype) for x in kept] + [pltpu.VMEM((cells, lanes), F32), wide, whole],
+        [pltpu.VMEM(x.shape, x.dtype) for x in kept] + [pltpu.VMEM((cells, lanes), F32), wide, whole, grad],
         40 * MIB,
         me, conv_rows, mix_weight, *late, act,
     )
     traded = cross(late_terms, 2, 4) if paired else None
     (early_terms,) = call(
-        functools.partial(third_kernel),
+        functools.partial(third_kernel, shares),
         [terms],
-        [pltpu.VMEM((cells, lanes), F32), wide, whole],
+        [pltpu.VMEM((cells, lanes), F32), wide, whole, grad],
         20 * MIB,
         me, up, *saved,
     )
@@ -452,7 +495,7 @@
         jax.ShapeDtypeStruct((groups, 1, taps, hidden), F32),
         jax.ShapeDtypeStruct((groups, 1, channels, hidden), F32),
     ]
-    scratch = [pltpu.VMEM((width, hidden), F32), pltpu.SemaphoreType.DMA((3,))]
+    scratch = [pltpu.VMEM((width, hidden), F32), pltpu.SemaphoreType.DMA((2, 8))]
     grads = ()
     for group in (1, 0):
         own = late_terms if group else early_terms
@@ -460,7 +503,7 @@
             met = after(traded, early_terms) if group else cross(own, 2, 4)
             half = (own.astype(F32) + met.astype(F32)).astype(BF)
             other = cross(half, 4, 2)
-            kernel, parts = pair_kernel, (half, other, exchange(half, 1), exchange(other, 1))
+            kernel, parts = both_kernel, (half, other, exchange(half, 1), exchange(other, 1))
         else:
             level = [own] + [exchange(own, k * replicas) for k in range(1, micro_count)]
             level = [x.astype(F32) for x in level]

time: 76.8 us -> 76.2 us (level)
  starting transfers between devices: 25.4 us -> 24.3 us
  waiting for transfers between devices: 21.6 us -> 22.5 us
    ppermute x12, starting transfers between devices: 11.4 us -> 10.3 us  [exchange(): return lax.ppermute(block, 'space', [(i, i ^ mask) for i in range(count)])]
    ppermute x6, waiting for transfers between devices: 5 us -> 5.82 us  [cross(): lax.ppermute(block, 'space', [(i, i ^ (second if i % 2 else first)) for i...]
where the time goes in v4:
time: 76.2 us; the launch traced here: 76 us
  Pallas kernels  26.7 us (35%)
  starting transfers between devices  24.3 us (32%)
  waiting for transfers between devices  22.5 us (30%)
  other arithmetic  1.58 us (2%)
  between operations  0.86 us (1%)
    pallas_call x6, Pallas kernels, call(): pl.pallas_call(kernel, out_shape=outs, in_specs=specs, out_specs=[far if...  26.7 us
    ppermute x2, waiting for transfers between devices, gather_paired(): lax.ppermute(after(part[group], *near[:group]), 'section', across)  12.7 us
    ppermute x12, starting transfers between devices, exchange(): return lax.ppermute(block, 'space', [(i, i ^ mask) for i in range(count)])  10.3 us
    ppermute x2, starting transfers between devices, gather_paired(): lax.ppermute(after(mine[group], *near), ('section', 'space'), route)  7.28 us
    ppermute x6, starting transfers between devices, cross(): lax.ppermute(block, 'space', [(i, i ^ (second if i % 2 else first)) for i...  6.08 us
    ppermute x6, waiting for transfers between devices, cross(): lax.ppermute(block, 'space', [(i, i ^ (second if i % 2 else first)) for i...  5.82 us
    ppermute x12, waiting for transfers between devices, exchange(): return lax.ppermute(block, 'space', [(i, i ^ mask) for i in range(count)])  3.98 us
  transfers between devices with their start and end apart: 22, of which 8 were waited for; matrix products, arithmetic and copies ran while one was open for 0% of the time, Pallas kernels for 18%

profile of v4, /device:TPU:1, one launch (start us, length us, event | category | flops | bytes accessed | tf_op | source)
XLA Modules:
  0.0 76.0 jit_solution(2532562018116268568)
XLA Ops:
  0.7 1.3 %fusion = bf16[2,896,128]{2,1,0:T(8,128)(2,1)S(1)} fusion(bf16[2,64,128]{2,1,0:T(8,128)(2,1)} %bitcast.27, bf16[2,1728,128]{2,1,0:T(8,128)(2,1)} %bitcast.24, pred[]{:T(512)S(6)} %eq.7), kind=kLoop, calls=%fused_computation.2 | loop fusion | flops 1146880 | bytes 1835009 | tf_op jit(solution)/shard_map/jit(_where)/select_n | solution.py:337
  2.2 4.8 %collective-permute-start = (bf16[896,128]{1,0:T(8,128)(2,1)S(1)}, bf16[896,128]{1,0:T(8,128)(2,1)S(1)}, u32[]{:S(2)}, u32[]{:S(2)}) collective-permute-start(bf16[896,128]{1,0:T(8,128)(2,1)S(1)} %get-tuple-element.45), channel_id=1, source_target_pairs={{0,8},{1,25},{2,10},{3,27},{4,12},{5,29},{6,14},{7,31},{8,16},{9,1... | collective-permute-start | bytes 688136 | tf_op jit(solution)/shard_map/ppermute | solution.py:355
  7.1 0.8 %shard_map.59 = (bf16[256,128]{1,0:T(8,128)(2,1)S(1)}, bf16[256,128]{1,0:T(8,128)(2,1)S(1)}, bf16[256,128]{1,0:T(8,128)(2,1)S(1)}, bf16[512,128]{1,0:T(8,128)(2,1)S(1)}) custom-call(s32[3]{0:T(128)S(1)} %pad_add_fusion.me_ref, bf16[4,128,128]{2,1,0:T(8,128)(2,1)S(1)} %bitcast.28, bf16[4,128,128]{2,1,0:T(8,128)(2,1)S(1)} %bitcast.29, ...), custom_call_target="tpu_custom_call" | custom-call | flops 104857600 | bytes 1048576 | tf_op jit(solution)/shard_map/pallas_call | solution.py:305
  8.1 0.6 collective-permute-start.1
  8.7 0.7 collective-permute-done.3.refs_5_.refs_7_
  9.4 7.7 %collective-permute-done.1 = bf16[448,128]{1,0:T(8,128)(2,1)S(1)} collective-permute-done((bf16[448,128]{1,0:T(8,128)(2,1)S(1)}, bf16[448,128]{1,0:T(8,128)(2,1)S(1)}, u32[]{:S(2)}, u32[]{:S(2)}) %collective-permute-start.1) | collective-permute-done | bytes 114720 | tf_op jit(solution)/shard_map/ppermute | solution.py:356
  17.1 1.4 %collective-permute-start.4 = (bf16[1856,128]{1,0:T(8,128)(2,1)S(1)}, bf16[1856,128]{1,0:T(8,128)(2,1)S(1)}, u32[]{:S(2)}, u32[]{:S(2)}) collective-permute-start(bf16[1856,128]{1,0:T(8,128)(2,1)S(1)} %pad_maximum_fusion.refs_0_), channel_id=1, source_target_pairs={{0,2},{1,5},{2,0},{3,7},{4,6},{5,1},{6,4},{7,3},{8,10},{9,13},{10,... | collective-permute-start | bytes 1425416 | tf_op jit(solution)/shard_map/ppermute | solution.py:324
  18.5 2.5 %collective-permute-start.6 = (bf16[896,128]{1,0:T(8,128)(2,1)S(1)}, bf16[896,128]{1,0:T(8,128)(2,1)S(1)}, u32[]{:S(2)}, u32[]{:S(2)}) collective-permute-start(bf16[896,128]{1,0:T(8,128)(2,1)S(1)} %get-tuple-element.25), channel_id=1, source_target_pairs={{0,8},{1,25},{2,10},{3,27},{4,12},{5,29},{6,14},{7,31},{8,16},{9,1... | collective-permute-start | bytes 688136 | tf_op jit(solution)/shard_map/ppermute | solution.py:355
  21.0 1.2 %collective-permute-start.5 = (bf16[256,128]{1,0:T(8,128)(2,1)S(1)}, bf16[256,128]{1,0:T(8,128)(2,1)S(1)}, u32[]{:S(2)}, u32[]{:S(2)}) collective-permute-start(bf16[256,128]{1,0:T(8,128)(2,1)S(1)} %get-tuple-element.24), channel_id=1, source_target_pairs={{0,6},{1,7},{2,4},{3,5},{4,2},{5,3},{6,0},{7,1},{8,14},{9,15},{10,... | collective-permute-start | bytes 196616 | tf_op jit(solution)/shard_map/ppermute | solution.py:319
  22.1 2.2 %collective-permute-start.11 = (bf16[1856,128]{1,0:T(8,128)(2,1)S(1)}, bf16[1856,128]{1,0:T(8,128)(2,1)S(1)}, u32[]{:S(2)}, u32[]{:S(2)}) collective-permute-start(bf16[1856,128]{1,0:T(8,128)(2,1)S(1)} %pad_maximum_fusion.refs_0_), channel_id=1, source_target_pairs={{0,1},{1,0},{2,3},{3,2},{4,5},{5,4},{6,7},{7,6},{8,9},{9,8},{10,11... | collective-permute-start | bytes 1425416 | tf_op jit(solution)/shard_map/ppermute | solution.py:319
  24.3 1.7 %collective-permute-done.5.refs_6_.refs_8_ = bf16[256,128]{1,0:T(8,128)(2,1)S(1)} collective-permute-done((bf16[256,128]{1,0:T(8,128)(2,1)S(1)}, bf16[256,128]{1,0:T(8,128)(2,1)S(1)}, u32[]{:S(2)}, u32[]{:S(2)}) %collective-permute-start.5) | collective-permute-done | bytes 65568 | tf_op jit(solution)/shard_map/ppermute | solution.py:319
  26.0 5.0 %collective-permute-done.7 = bf16[448,128]{1,0:T(8,128)(2,1)S(1)} collective-permute-done((bf16[448,128]{1,0:T(8,128)(2,1)S(1)}, bf16[448,128]{1,0:T(8,128)(2,1)S(1)}, u32[]{:S(2)}, u32[]{:S(2)}) %collective-permute-start.7) | collective-permute-done | bytes 114720 | tf_op jit(solution)/shard_map/ppermute | solution.py:356
  31.0 0.1 collective-permute-start.8
  31.2 0.4 collective-permute-start.12
  31.6 1.2 %collective-permute-start.9 = (bf16[1344,128]{1,0:T(8,128)(2,1)S(1)}, bf16[1344,128]{1,0:T(8,128)(2,1)S(1)}, u32[]{:S(2)}, u32[]{:S(2)}) collective-permute-start(bf16[1344,128]{1,0:T(8,128)(2,1)S(1)} %constant_dynamic-update-slice_fusion.refs_2_), channel_id=1, source_target_pairs={{0,2},{1,5},{2,0},{3,7},{4,6},{5,1},{6,4},{7,3},{8,10},{9,13},{10,... | collective-permute-start | bytes 1032200 | tf_op jit(solution)/shard_map/ppermute | solution.py:324
  32.8 0.2 collective-permute-done.12.refs_7_.refs_9_
  33.0 6.1 %shard_map.60 = (f32[1024,128]{1,0:T(8,128)S(1)}, bf16[4,1280,256]{2,1,0:T(8,128)(2,1)S(1)}, bf16[4,1024,256]{2,1,0:T(8,128)(2,1)S(1)}, bf16[2,10,128,384]{3,2,1,0:T(8,128)(2,1)S(1)}, bf16[2,1024,256]{2,1,0:T(8,128)(2,1)S(1)}) custom-call(s32[3]{0:T(128)S(1)} %pad_add_fusion.me_ref, bf16[2,1,1728,128]{3,2,1,0:T(8,128)(2,1)S(1)} %bitcast.25, ...), custom_call_target="tpu_custom_call" | custom-call | flops 3145728000 | bytes 31457280 | tf_op jit(solution)/shard_map/pallas_call | solution.py:305
  39.1 0.4 collective-permute-start.13
  39.5 1.3 %collective-permute-done.13.refs_5_ = bf16[1344,128]{1,0:T(8,128)(2,1)S(1)} collective-permute-done((bf16[1344,128]{1,0:T(8,128)(2,1)S(1)}, bf16[1344,128]{1,0:T(8,128)(2,1)S(1)}, u32[]{:S(2)}, u32[]{:S(2)}) %collective-permute-start.13) | collective-permute-done | bytes 344096 | tf_op jit(solution)/shard_map/ppermute | solution.py:319
  40.8 11.4 %shard_map.61 = (f32[1024,128]{1,0:T(8,128)S(1)}, bf16[896,128]{1,0:T(8,128)(2,1)S(1)}) custom-call(s32[3]{0:T(128)S(1)} %pad_add_fusion.me_ref, bf16[2,1,1728,128]{3,2,1,0:T(8,128)(2,1)S(1)} %bitcast.26, bf16[2,1,64,128]{3,2,1,0:T(8,128)(2,1)S(1)} %copy-done.1, bf16[1856,128]{1,0:T(8,128)(2,1)S(1)} %collective-permute-done.4.refs_1_.refs_0_, ...), custom_call_target="tpu_custom_call" | custom-call | flops 4194304000 | bytes 41943040 | tf_op jit(solution)/shard_map/pallas_call | solution.py:305
  52.2 1.2 %collective-permute-start.18 = (bf16[896,128]{1,0:T(8,128)(2,1)S(1)}, bf16[896,128]{1,0:T(8,128)(2,1)S(1)}, u32[]{:S(2)}, u32[]{:S(2)}) collective-permute-start(bf16[896,128]{1,0:T(8,128)(2,1)S(1)} %get-tuple-element.36), channel_id=1, source_target_pairs={{0,2},{1,5},{2,0},{3,7},{4,6},{5,1},{6,4},{7,3},{8,10},{9,13},{10,... | collective-permute-start | bytes 688136 | tf_op jit(solution)/shard_map/ppermute | solution.py:324
  53.4 5.0 %shard_map.62 = bf16[896,128]{1,0:T(8,128)(2,1)S(1)} custom-call(s32[3]{0:T(128)S(1)} %pad_add_fusion.me_ref, f32[1024,128]{1,0:T(8,128)S(1)} %get-tuple-element.31.up_in, bf16[4,1280,256]{2,1,0:T(8,128)(2,1)S(1)} %get-tuple-element.32.folded, bf16[4,1024,256]{2,1,0:T(8,128)(2,1)S(1)} %get-tuple-element.33.slope, ...), custom_call_target="tpu_custom_call" | custom-call | flops 2097152000 | bytes 20971520 | tf_op jit(solution)/shard_map/pallas_call | solution.py:305
  58.5 0.4 collective-permute-start.14
  58.9 0.6 collective-permute-start.19
  59.5 4.9 %collective-permute-done.14 = bf16[896,128]{1,0:T(8,128)(2,1)S(1)} collective-permute-done((bf16[896,128]{1,0:T(8,128)(2,1)S(1)}, bf16[896,128]{1,0:T(8,128)(2,1)S(1)}, u32[]{:S(2)}, u32[]{:S(2)}) %collective-permute-start.14) | collective-permute-done | bytes 229408 | tf_op jit(solution)/shard_map/ppermute | solution.py:324
  64.5 1.3 %collective-permute-start.15 = (bf16[896,128]{1,0:T(8,128)(2,1)S(1)}, bf16[896,128]{1,0:T(8,128)(2,1)S(1)}, u32[]{:S(2)}, u32[]{:S(2)}) collective-permute-start(bf16[896,128]{1,0:T(8,128)(2,1)S(1)} %add_convert_fusion.1.own_a), channel_id=1, source_target_pairs={{0,4},{1,3},{2,6},{3,1},{4,0},{5,7},{6,2},{7,5},{8,12},{9,11},{10,... | collective-permute-start | bytes 688136 | tf_op jit(solution)/shard_map/ppermute | solution.py:324
  65.8 2.6 %collective-permute-start.20 = (bf16[896,128]{1,0:T(8,128)(2,1)S(1)}, bf16[896,128]{1,0:T(8,128)(2,1)S(1)}, u32[]{:S(2)}, u32[]{:S(2)}) collective-permute-start(bf16[896,128]{1,0:T(8,128)(2,1)S(1)} %add_convert_fusion.own_a), channel_id=1, source_target_pairs={{0,1},{1,0},{2,3},{3,2},{4,5},{5,4},{6,7},{7,6},{8,9},{9,8},{10,11... | collective-permute-start | bytes 688136 | tf_op jit(solution)/shard_map/ppermute | solution.py:319
  68.4 0.5 collective-permute-start.16
  68.9 0.9 %collective-permute-done.15.own_b = bf16[896,128]{1,0:T(8,128)(2,1)S(1)} collective-permute-done((bf16[896,128]{1,0:T(8,128)(2,1)S(1)}, bf16[896,128]{1,0:T(8,128)(2,1)S(1)}, u32[]{:S(2)}, u32[]{:S(2)}) %collective-permute-start.15) | collective-permute-done | bytes 229408 | tf_op jit(solution)/shard_map/ppermute | solution.py:324
  69.8 2.8 %collective-permute-start.17 = (bf16[896,128]{1,0:T(8,128)(2,1)S(1)}, bf16[896,128]{1,0:T(8,128)(2,1)S(1)}, u32[]{:S(2)}, u32[]{:S(2)}) collective-permute-start(bf16[896,128]{1,0:T(8,128)(2,1)S(1)} %collective-permute-done.15.own_b), channel_id=1, source_target_pairs={{0,1},{1,0},{2,3},{3,2},{4,5},{5,4},{6,7},{7,6},{8,9},{9,8},{10,11... | collective-permute-start | bytes 688136 | tf_op jit(solution)/shard_map/ppermute | solution.py:319
  72.6 1.7 %shard_map.63 = (f32[2,1,1728,128]{3,2,1,0:T(8,128)}, f32[2,1,64,128]{3,2,1,0:T(8,128)}) custom-call(s32[3]{0:T(128)S(1)} %pad_add_fusion.me_ref, bf16[896,128]{1,0:T(8,128)(2,1)S(1)} %add_convert_fusion.own_a, bf16[896,128]{1,0:T(8,128)(2,1)S(1)} %collective-permute-done.19.own_b, bf16[896,128]{1,0:T(8,128)(2,1)S(1)} %collective-permute-done.20.far_a, ...), custom_call_target="tpu_custom_call" | custom-call | flops 6553600 | bytes 65536 | tf_op jit(solution)/shard_map/pallas_call | solution.py:305
  74.3 1.7 %shard_map.64 = (f32[2,1,1728,128]{3,2,1,0:T(8,128)}, f32[2,1,64,128]{3,2,1,0:T(8,128)}) custom-call(s32[3]{0:T(128)S(1)} %pad_add_fusion.me_ref, bf16[896,128]{1,0:T(8,128)(2,1)S(1)} %add_convert_fusion.1.own_a, bf16[896,128]{1,0:T(8,128)(2,1)S(1)} %collective-permute-done.15.own_b, ...), custom_call_target="tpu_custom_call", output_to_operand_aliasing={{0}: (5, {}), {1}: (6, {})} | custom-call | flops 6553600 | bytes 65536 | tf_op jit(solution)/shard_map/pallas_call | solution.py:305
  (37 shorter events, 0.6 us)
Async XLA Ops:
  0.6 6.5 %copy-start.3 = (bf16[4,64,1,2,128]{4,3,2,1,0:T(2,128)(2,1)S(1)}, bf16[4,64,1,2,128]{4,3,2,1,0:T(2,128)(2,1)}, u32[]{:S(2)}) copy-start(bf16[4,64,1,2,128]{4,3,2,1,0:T(2,128)(2,1)} %param.5) | copy-start | bytes 393220
  0.6 6.5 %copy-start.2 = (bf16[4,64,1,2,128]{4,3,2,1,0:T(2,128)(2,1)S(1)}, bf16[4,64,1,2,128]{4,3,2,1,0:T(2,128)(2,1)}, u32[]{:S(2)}) copy-start(bf16[4,64,1,2,128]{4,3,2,1,0:T(2,128)(2,1)} %param.4) | copy-start | bytes 393220
  2.0 30.9 %copy-start = (bf16[2,1,128,1728]{2,3,1,0:T(8,128)(2,1)S(1)}, bf16[2,1,128,1728]{2,3,1,0:T(8,128)(2,1)}, u32[]{:S(2)}) copy-start(bf16[2,1,128,1728]{2,3,1,0:T(8,128)(2,1)} %param.6) | copy-start | bytes 2654212
  2.1 30.9 %copy-start.1 = (bf16[2,1,64,128]{3,2,1,0:T(8,128)(2,1)S(1)}, bf16[2,1,64,128]{3,2,1,0:T(8,128)(2,1)}, u32[]{:S(2)}) copy-start(bf16[2,1,64,128]{3,2,1,0:T(8,128)(2,1)} %mix.3) | copy-start | bytes 98308
  2.1 5.1 %collective-permute-start.2 = (bf16[16,128]{1,0:T(8,128)(2,1)S(1)}, bf16[16,128]{1,0:T(8,128)(2,1)S(1)}, u32[]{:S(2)}, u32[]{:S(2)}) collective-permute-start(bf16[16,128]{1,0:T(8,128)(2,1)S(1)} %slice_bitcast_fusion.2), channel_id=1, source_target_pairs={{0,1},{1,0},{2,3},{3,2},{4,5},{5,4},{6,7},{7,6},{8,9},{9,8},{10,11... | collective-permute-start | bytes 12296 | tf_op jit(solution)/shard_map/ppermute | solution.py:319
  2.2 14.8 %collective-permute-start = (bf16[896,128]{1,0:T(8,128)(2,1)S(1)}, bf16[896,128]{1,0:T(8,128)(2,1)S(1)}, u32[]{:S(2)}, u32[]{:S(2)}) collective-permute-start(bf16[896,128]{1,0:T(8,128)(2,1)S(1)} %get-tuple-element.45), channel_id=1, source_target_pairs={{0,8},{1,25},{2,10},{3,27},{4,12},{5,29},{6,14},{7,31},{8,16},{9,1... | collective-permute-start | bytes 688136 | tf_op jit(solution)/shard_map/ppermute | solution.py:355
  8.0 1.4 %collective-permute-start.3 = (bf16[512,128]{1,0:T(8,128)(2,1)S(1)}, bf16[512,128]{1,0:T(8,128)(2,1)S(1)}, u32[]{:S(2)}, u32[]{:S(2)}) collective-permute-start(bf16[512,128]{1,0:T(8,128)(2,1)S(1)} %get-tuple-element.23), channel_id=1, source_target_pairs={{0,1},{1,0},{2,3},{3,2},{4,5},{5,4},{6,7},{7,6},{8,9},{9,8},{10,11... | collective-permute-start | bytes 393224 | tf_op jit(solution)/shard_map/ppermute | solution.py:319
  8.1 9.0 %collective-permute-start.1 = (bf16[448,128]{1,0:T(8,128)(2,1)S(1)}, bf16[448,128]{1,0:T(8,128)(2,1)S(1)}, u32[]{:S(2)}, u32[]{:S(2)}) collective-permute-start(bf16[448,128]{1,0:T(8,128)(2,1)S(1)} %get-tuple-element.43), channel_id=1, source_target_pairs={{0,16},{8,24},{16,0},{24,8},{1,17},{9,25},{17,1},{25,9},{2,18},{10... | collective-permute-start | bytes 344072 | tf_op jit(solution)/shard_map/ppermute | solution.py:356
  17.1 13.9 %collective-permute-start.4 = (bf16[1856,128]{1,0:T(8,128)(2,1)S(1)}, bf16[1856,128]{1,0:T(8,128)(2,1)S(1)}, u32[]{:S(2)}, u32[]{:S(2)}) collective-permute-start(bf16[1856,128]{1,0:T(8,128)(2,1)S(1)} %pad_maximum_fusion.refs_0_), channel_id=1, source_target_pairs={{0,2},{1,5},{2,0},{3,7},{4,6},{5,1},{6,4},{7,3},{8,10},{9,13},{10,... | collective-permute-start | bytes 1425416 | tf_op jit(solution)/shard_map/ppermute | solution.py:324
  18.5 12.5 %collective-permute-start.6 = (bf16[896,128]{1,0:T(8,128)(2,1)S(1)}, bf16[896,128]{1,0:T(8,128)(2,1)S(1)}, u32[]{:S(2)}, u32[]{:S(2)}) collective-permute-start(bf16[896,128]{1,0:T(8,128)(2,1)S(1)} %get-tuple-element.25), channel_id=1, source_target_pairs={{0,8},{1,25},{2,10},{3,27},{4,12},{5,29},{6,14},{7,31},{8,16},{9,1... | collective-permute-start | bytes 688136 | tf_op jit(solution)/shard_map/ppermute | solution.py:355
  21.0 10.1 %collective-permute-start.7 = (bf16[448,128]{1,0:T(8,128)(2,1)S(1)}, bf16[448,128]{1,0:T(8,128)(2,1)S(1)}, u32[]{:S(2)}, u32[]{:S(2)}) collective-permute-start(bf16[448,128]{1,0:T(8,128)(2,1)S(1)} %get-tuple-element.26), channel_id=1, source_target_pairs={{0,16},{8,24},{16,0},{24,8},{1,17},{9,25},{17,1},{25,9},{2,18},{10... | collective-permute-start | bytes 344072 | tf_op jit(solution)/shard_map/ppermute | solution.py:356
  21.0 5.1 %collective-permute-start.5 = (bf16[256,128]{1,0:T(8,128)(2,1)S(1)}, bf16[256,128]{1,0:T(8,128)(2,1)S(1)}, u32[]{:S(2)}, u32[]{:S(2)}) collective-permute-start(bf16[256,128]{1,0:T(8,128)(2,1)S(1)} %get-tuple-element.24), channel_id=1, source_target_pairs={{0,6},{1,7},{2,4},{3,5},{4,2},{5,3},{6,0},{7,1},{8,14},{9,15},{10,... | collective-permute-start | bytes 196616 | tf_op jit(solution)/shard_map/ppermute | solution.py:319
  22.1 10.9 %collective-permute-start.11 = (bf16[1856,128]{1,0:T(8,128)(2,1)S(1)}, bf16[1856,128]{1,0:T(8,128)(2,1)S(1)}, u32[]{:S(2)}, u32[]{:S(2)}) collective-permute-start(bf16[1856,128]{1,0:T(8,128)(2,1)S(1)} %pad_maximum_fusion.refs_0_), channel_id=1, source_target_pairs={{0,1},{1,0},{2,3},{3,2},{4,5},{5,4},{6,7},{7,6},{8,9},{9,8},{10,11... | collective-permute-start | bytes 1425416 | tf_op jit(solution)/shard_map/ppermute | solution.py:319
  31.0 1.9 %collective-permute-start.8 = (bf16[1856,128]{1,0:T(8,128)(2,1)S(1)}, bf16[1856,128]{1,0:T(8,128)(2,1)S(1)}, u32[]{:S(2)}, u32[]{:S(2)}) collective-permute-start(bf16[1856,128]{1,0:T(8,128)(2,1)S(1)} %collective-permute-done.4.refs_1_.refs_0_), channel_id=1, source_target_pairs={{0,1},{1,0},{2,3},{3,2},{4,5},{5,4},{6,7},{7,6},{8,9},{9,8},{10,11... | collective-permute-start | bytes 1425416 | tf_op jit(solution)/shard_map/ppermute | solution.py:319
  31.2 1.8 %collective-permute-start.12 = (bf16[256,128]{1,0:T(8,128)(2,1)S(1)}, bf16[256,128]{1,0:T(8,128)(2,1)S(1)}, u32[]{:S(2)}, u32[]{:S(2)}) collective-permute-start(bf16[256,128]{1,0:T(8,128)(2,1)S(1)} %collective-permute-done.5.refs_6_.refs_8_), channel_id=1, source_target_pairs={{0,1},{1,0},{2,3},{3,2},{4,5},{5,4},{6,7},{7,6},{8,9},{9,8},{10,11... | collective-permute-start | bytes 196616 | tf_op jit(solution)/shard_map/ppermute | solution.py:319
  31.6 7.5 %collective-permute-start.9 = (bf16[1344,128]{1,0:T(8,128)(2,1)S(1)}, bf16[1344,128]{1,0:T(8,128)(2,1)S(1)}, u32[]{:S(2)}, u32[]{:S(2)}) collective-permute-start(bf16[1344,128]{1,0:T(8,128)(2,1)S(1)} %constant_dynamic-update-slice_fusion.refs_2_), channel_id=1, source_target_pairs={{0,2},{1,5},{2,0},{3,7},{4,6},{5,1},{6,4},{7,3},{8,10},{9,13},{10,... | collective-permute-start | bytes 1032200 | tf_op jit(solution)/shard_map/ppermute | solution.py:324
  32.7 6.7 %collective-permute-start.10 = (bf16[1344,128]{1,0:T(8,128)(2,1)S(1)}, bf16[1344,128]{1,0:T(8,128)(2,1)S(1)}, u32[]{:S(2)}, u32[]{:S(2)}) collective-permute-start(bf16[1344,128]{1,0:T(8,128)(2,1)S(1)} %constant_dynamic-update-slice_fusion.refs_2_), channel_id=1, source_target_pairs={{0,1},{1,0},{2,3},{3,2},{4,5},{5,4},{6,7},{7,6},{8,9},{9,8},{10,11... | collective-permute-start | bytes 1032200 | tf_op jit(solution)/shard_map/ppermute | solution.py:319
  39.1 1.7 %collective-permute-start.13 = (bf16[1344,128]{1,0:T(8,128)(2,1)S(1)}, bf16[1344,128]{1,0:T(8,128)(2,1)S(1)}, u32[]{:S(2)}, u32[]{:S(2)}) collective-permute-start(bf16[1344,128]{1,0:T(8,128)(2,1)S(1)} %collective-permute-done.9.refs_3_), channel_id=1, source_target_pairs={{0,1},{1,0},{2,3},{3,2},{4,5},{5,4},{6,7},{7,6},{8,9},{9,8},{10,11... | collective-permute-start | bytes 1032200 | tf_op jit(solution)/shard_map/ppermute | solution.py:319
  52.2 6.7 %collective-permute-start.18 = (bf16[896,128]{1,0:T(8,128)(2,1)S(1)}, bf16[896,128]{1,0:T(8,128)(2,1)S(1)}, u32[]{:S(2)}, u32[]{:S(2)}) collective-permute-start(bf16[896,128]{1,0:T(8,128)(2,1)S(1)} %get-tuple-element.36), channel_id=1, source_target_pairs={{0,2},{1,5},{2,0},{3,7},{4,6},{5,1},{6,4},{7,3},{8,10},{9,13},{10,... | collective-permute-start | bytes 688136 | tf_op jit(solution)/shard_map/ppermute | solution.py:324
  58.5 6.0 %collective-permute-start.14 = (bf16[896,128]{1,0:T(8,128)(2,1)S(1)}, bf16[896,128]{1,0:T(8,128)(2,1)S(1)}, u32[]{:S(2)}, u32[]{:S(2)}) collective-permute-start(bf16[896,128]{1,0:T(8,128)(2,1)S(1)} %shard_map.62), channel_id=1, source_target_pairs={{0,2},{1,5},{2,0},{3,7},{4,6},{5,1},{6,4},{7,3},{8,10},{9,13},{10,... | collective-permute-start | bytes 688136 | tf_op jit(solution)/shard_map/ppermute | solution.py:324
  58.9 9.5 %collective-permute-start.19 = (bf16[896,128]{1,0:T(8,128)(2,1)S(1)}, bf16[896,128]{1,0:T(8,128)(2,1)S(1)}, u32[]{:S(2)}, u32[]{:S(2)}) collective-permute-start(bf16[896,128]{1,0:T(8,128)(2,1)S(1)} %add_convert_fusion.own_a), channel_id=1, source_target_pairs={{0,4},{1,3},{2,6},{3,1},{4,0},{5,7},{6,2},{7,5},{8,12},{9,11},{10,... | collective-permute-start | bytes 688136 | tf_op jit(solution)/shard_map/ppermute | solution.py:324
  64.5 5.2 %collective-permute-start.15 = (bf16[896,128]{1,0:T(8,128)(2,1)S(1)}, bf16[896,128]{1,0:T(8,128)(2,1)S(1)}, u32[]{:S(2)}, u32[]{:S(2)}) collective-permute-start(bf16[896,128]{1,0:T(8,128)(2,1)S(1)} %add_convert_fusion.1.own_a), channel_id=1, source_target_pairs={{0,4},{1,3},{2,6},{3,1},{4,0},{5,7},{6,2},{7,5},{8,12},{9,11},{10,... | collective-permute-start | bytes 688136 | tf_op jit(solution)/shard_map/ppermute | solution.py:324
  65.8 6.7 %collective-permute-start.20 = (bf16[896,128]{1,0:T(8,128)(2,1)S(1)}, bf16[896,128]{1,0:T(8,128)(2,1)S(1)}, u32[]{:S(2)}, u32[]{:S(2)}) collective-permute-start(bf16[896,128]{1,0:T(8,128)(2,1)S(1)} %add_convert_fusion.own_a), channel_id=1, source_target_pairs={{0,1},{1,0},{2,3},{3,2},{4,5},{5,4},{6,7},{7,6},{8,9},{9,8},{10,11... | collective-permute-start | bytes 688136 | tf_op jit(solution)/shard_map/ppermute | solution.py:319
  68.4 4.2 %collective-permute-start.21 = (bf16[896,128]{1,0:T(8,128)(2,1)S(1)}, bf16[896,128]{1,0:T(8,128)(2,1)S(1)}, u32[]{:S(2)}, u32[]{:S(2)}) collective-permute-start(bf16[896,128]{1,0:T(8,128)(2,1)S(1)} %collective-permute-done.19.own_b), channel_id=1, source_target_pairs={{0,1},{1,0},{2,3},{3,2},{4,5},{5,4},{6,7},{7,6},{8,9},{9,8},{10,11... | collective-permute-start | bytes 688136 | tf_op jit(solution)/shard_map/ppermute | solution.py:319
  68.4 5.9 %collective-permute-start.16 = (bf16[896,128]{1,0:T(8,128)(2,1)S(1)}, bf16[896,128]{1,0:T(8,128)(2,1)S(1)}, u32[]{:S(2)}, u32[]{:S(2)}) collective-permute-start(bf16[896,128]{1,0:T(8,128)(2,1)S(1)} %add_convert_fusion.1.own_a), channel_id=1, source_target_pairs={{0,1},{1,0},{2,3},{3,2},{4,5},{5,4},{6,7},{7,6},{8,9},{9,8},{10,11... | collective-permute-start | bytes 688136 | tf_op jit(solution)/shard_map/ppermute | solution.py:319
  69.8 4.5 %collective-permute-start.17 = (bf16[896,128]{1,0:T(8,128)(2,1)S(1)}, bf16[896,128]{1,0:T(8,128)(2,1)S(1)}, u32[]{:S(2)}, u32[]{:S(2)}) collective-permute-start(bf16[896,128]{1,0:T(8,128)(2,1)S(1)} %collective-permute-done.15.own_b), channel_id=1, source_target_pairs={{0,1},{1,0},{2,3},{3,2},{4,5},{5,4},{6,7},{7,6},{8,9},{9,8},{10,11... | collective-permute-start | bytes 688136 | tf_op jit(solution)/shard_map/ppermute | solution.py:319

commit v5 on v4

--- a/solution.py
+++ b/solution.py
@@ -192,17 +192,24 @@
 
 def first_kernel(plan, piece_count, me_ref, conv, mix, *refs):
     pieces, refs = refs[:piece_count], refs[piece_count:]
-    act, folded, slope, keep_a, keep_h = refs
+    act, folded, slope, keep_a, keep_h, mark = refs
     section = me_ref[0]
     take(plan, me_ref, 0, 0, conv, mix, pieces, folded, act)
     for slot in range(2):
         clear_edges(keep_a.at[slot])
+    mark[...] = jnp.zeros_like(mark)
 
     def step(layer, carry):
         forward_layer(layer, jnp.where(layer == section, 0, 1), act, folded, slope, keep_a, keep_h)
         return carry
 
-    lax.fori_loop(0, folded.shape[0], step, 0)
+    lax.fori_loop(0, folded.shape[0] - 1, step, 0)
+
+
+def next_kernel(me_ref, mark, folded, *refs):
+    act, slope, keep_a, keep_h = refs[-4:]
+    layer = folded.shape[0] - 1
+    forward_layer(layer, jnp.where(layer == me_ref[0], 0, 1), act, folded, slope, keep_a, keep_h)
 
 
 def all_back(shares, me_ref, last, up, grad, wide, folded, slope, keep_a, keep_h, terms, out):
@@ -296,7 +303,7 @@
 def call(kernel, outs, scratch, traffic, *args, into=()):
     vmem = pl.BlockSpec(memory_space=pltpu.VMEM)
     far = pl.BlockSpec(memory_space=pl.ANY)
-    specs = [pl.BlockSpec(memory_space=pltpu.SMEM)] + [vmem] * (len(args) - 1) + [far] * len(into)
+    specs = [pl.BlockSpec(memory_space=pltpu.SMEM)] + [vmem] * (len(args) - 1) + [vmem if kernel.func is next_kernel else far] * len(into)
     held = sum(size_of(x) for x in scratch if x.memory_space == pltpu.VMEM)
     passed = sum(size_of(x) for x in args) + sum(size_of(x) for x in outs)
     limit = held + held // 4 + 10 * MIB
@@ -356,17 +363,22 @@
         far.append(lax.ppermute(after(part[group], *near[:group]), "section", across))
     sent = [beside, other[256:]]
     diagonal_far = exchange(diagonal, 1)
-    pieces = []
-    for group in range(2):
-        here = jnp.concatenate([near[group], far[group]] + (sent if group == 0 else []), axis=0)
-        there = cross(here, 2, 4)
-        pieces += [here, there, exchange(here, 1), None if group else exchange(after(there, diagonal, near[1], far[1]), 1)]
-    planes = [own, other, diagonal, diagonal_far]
+    here = [jnp.concatenate([near[g], far[g]] + (sent if g == 0 else []), axis=0) for g in range(2)]
+    here[0] = after(here[0], diagonal)
+    there = [cross(x, 2, 4) for x in here]
+    late = exchange(here[1], 1)
+    ready = after(there[0], late)
+    pieces = [here[0], there[0], exchange(here[0], 1), exchange(ready[:half], 1), here[1], there[1], late, None]
+    planes = [own, other, diagonal, diagonal_far, exchange(ready[half:], 1)]
     plane_rows = 128
 
     def plan(section, place, field):
         chip, core = place // 2, place % 2
         side = (chip // 2) ^ (chip % 2)
+
+        def where(piece, row):
+            return (12, row - half) if piece == 3 and row >= half else (piece, row)
+
         weight_steps = []
         for group in range(2):
             steps = []
@@ -378,7 +390,7 @@
                     piece = 4 * group + 2 * swapped + other
                     first = (side ^ other) * 14
                     steps.append((piece, 0, 14, beside, first, (0, 14)))
-                    steps.append((piece, half, 7, across, first + source * 7, (0, 7, 14, 21)))
+                    steps.append((*where(piece, half), 7, across, first + source * 7, (0, 7, 14, 21)))
             weight_steps.append(steps)
         plane_steps = []
         start = field * plane_rows
@@ -387,8 +399,8 @@
         for swapped in range(2):
             rel = swapped ^ (2 + 2 * (core ^ swapped))
             start = half + quarter + field * plane_rows
-            plane_steps.append((1 + 2 * swapped, start, plane_rows, rel))
-            plane_steps.append((1 + 2 * swapped, start + 2 * plane_rows, plane_rows, rel ^ 1))
+            plane_steps.append((*where(1 + 2 * swapped, start), plane_rows, rel))
+            plane_steps.append((*where(1 + 2 * swapped, start + 2 * plane_rows), plane_rows, rel ^ 1))
         return weight_steps, plane_steps
 
     return pieces + planes, plan
@@ -460,14 +472,18 @@
         jax.ShapeDtypeStruct((2, cells, 2 * hidden), BF),
     ]
     early = [pieces[i] for i in needed(plan, 0, 0)]
-    act, *saved = call(
+    act, folded, *state, mark = call(
         functools.partial(first_kernel, plan, len(early)),
-        [act] + kept,
-        [], 30 * MIB,
+        [act] + kept + [jax.ShapeDtypeStruct((8, 128), F32)],
+        [], 2 * MIB,
         me, conv_rows, mix_weight, *early,
     )
+    act, *state = call(
+        functools.partial(next_kernel), [act] + kept[1:], [], 2 * MIB, me, mark, folded, into=(act, *state)
+    )
+    saved = (folded, *state)
     if paired:
-        pieces[7] = exchange(after(pieces[5], act), 1)
+        pieces[7] = exchange(after(pieces[5], mark), 1)
     late = [pieces[i] for i in needed(plan, 1, 1)]
     terms = jax.ShapeDtypeStruct((width // replicas, hidden), BF)
     shares = SHARES if paired else (tuple(range(28)),)

time: 76.2 us -> 74.4 us (0.976)
  waiting for transfers between devices: 22.5 us -> 18.1 us
  starting transfers between devices: 24.3 us -> 25.9 us
    ppermute x2, waiting for transfers between devices: 12.7 us -> 9.72 us  [gather_paired(): lax.ppermute(after(part[group], *near[:group]), 'section', across)]
    ppermute x12 -> x13, waiting for transfers between devices: 3.98 us -> 2.19 us  [exchange(): return lax.ppermute(block, 'space', [(i, i ^ mask) for i in range(count)])]
    ppermute x2, waiting for transfers between devices: 0.01 us -> 1.43 us  [gather_paired(): lax.ppermute(after(mine[group], *near), ('section', 'space'), route)]
    ppermute x12 -> x13, starting transfers between devices: 10.3 us -> 11.5 us  [exchange(): return lax.ppermute(block, 'space', [(i, i ^ mask) for i in range(count)])]
    ppermute x6, waiting for transfers between devices: 5.82 us -> 4.78 us  [cross(): lax.ppermute(block, 'space', [(i, i ^ (second if i % 2 else first)) for i...]
    pallas_call x6 -> x7, Pallas kernels: 26.7 us -> 27.4 us  [call(): pl.pallas_call(kernel, out_shape=outs, in_specs=specs, out_specs=[far if...]
  transfers between devices with their start and end apart: 22 -> 23, of which waited for: 8 -> 7; matrix products, arithmetic and copies ran while one was open for 0% -> 0% of each run, Pallas kernels for 18% -> 19%
where the time goes in v5:
time: 74.4 us; the launch traced here: 74.2 us
  Pallas kernels  27.4 us (37%)
  starting transfers between devices  25.9 us (35%)
  waiting for transfers between devices  18.1 us (24%)
  other arithmetic  1.58 us (2%)
  between operations  1.05 us (1%)
    pallas_call x7, Pallas kernels, call(): pl.pallas_call(kernel, out_shape=outs, in_specs=specs, out_specs=[far if...  27.4 us
    ppermute x13, starting transfers between devices, exchange(): return lax.ppermute(block, 'space', [(i, i ^ mask) for i in range(count)])  11.5 us
    ppermute x2, waiting for transfers between devices, gather_paired(): lax.ppermute(after(part[group], *near[:group]), 'section', across)  9.72 us
    ppermute x2, starting transfers between devices, gather_paired(): lax.ppermute(after(mine[group], *near), ('section', 'space'), route)  6.94 us
    ppermute x6, starting transfers between devices, cross(): lax.ppermute(block, 'space', [(i, i ^ (second if i % 2 else first)) for i...  6.35 us
    ppermute x6, waiting for transfers between devices, cross(): lax.ppermute(block, 'space', [(i, i ^ (second if i % 2 else first)) for i...  4.78 us
    ppermute x13, waiting for transfers between devices, exchange(): return lax.ppermute(block, 'space', [(i, i ^ mask) for i in range(count)])  2.19 us
  transfers between devices with their start and end apart: 23, of which 7 were waited for; matrix products, arithmetic and copies ran while one was open for 0% of the time, Pallas kernels for 19%

profile of v5, /device:TPU:1, one launch (start us, length us, event | category | flops | bytes accessed | tf_op | source)
XLA Modules:
  0.0 74.2 jit_solution(10398340225473422785)
XLA Ops:
  0.7 1.3 %fusion = bf16[2,896,128]{2,1,0:T(8,128)(2,1)S(1)} fusion(bf16[2,64,128]{2,1,0:T(8,128)(2,1)} %bitcast.27, bf16[2,1728,128]{2,1,0:T(8,128)(2,1)} %bitcast.24, pred[]{:T(512)S(6)} %eq.7), kind=kLoop, calls=%fused_computation.2 | loop fusion | flops 1146880 | bytes 1835009 | tf_op jit(solution)/shard_map/jit(_where)/select_n | solution.py:344
  2.1 4.2 %collective-permute-start = (bf16[896,128]{1,0:T(8,128)(2,1)S(1)}, bf16[896,128]{1,0:T(8,128)(2,1)S(1)}, u32[]{:S(2)}, u32[]{:S(2)}) collective-permute-start(bf16[896,128]{1,0:T(8,128)(2,1)S(1)} %get-tuple-element.57), channel_id=1, source_target_pairs={{0,8},{1,25},{2,10},{3,27},{4,12},{5,29},{6,14},{7,31},{8,16},{9,1... | collective-permute-start | bytes 688136 | tf_op jit(solution)/shard_map/ppermute | solution.py:362
  6.4 1.1 %collective-permute-done.2.token = bf16[16,128]{1,0:T(8,128)(2,1)S(1)} collective-permute-done((bf16[16,128]{1,0:T(8,128)(2,1)S(1)}, bf16[16,128]{1,0:T(8,128)(2,1)S(1)}, u32[]{:S(2)}, u32[]{:S(2)}) %collective-permute-start.2) | collective-permute-done | bytes 4128 | tf_op jit(solution)/shard_map/ppermute | solution.py:326
  7.5 0.8 %shard_map.59 = (bf16[256,128]{1,0:T(8,128)(2,1)S(1)}, bf16[256,128]{1,0:T(8,128)(2,1)S(1)}, bf16[256,128]{1,0:T(8,128)(2,1)S(1)}, bf16[512,128]{1,0:T(8,128)(2,1)S(1)}) custom-call(s32[3]{0:T(128)S(1)} %pad_add_fusion.me_ref, bf16[4,128,128]{2,1,0:T(8,128)(2,1)S(1)} %bitcast.28, bf16[4,128,128]{2,1,0:T(8,128)(2,1)S(1)} %bitcast.29, ...), custom_call_target="tpu_custom_call" | custom-call | flops 104857600 | bytes 1048576 | tf_op jit(solution)/shard_map/pallas_call | solution.py:312
  8.6 1.1 %collective-permute-start.1 = (bf16[448,128]{1,0:T(8,128)(2,1)S(1)}, bf16[448,128]{1,0:T(8,128)(2,1)S(1)}, u32[]{:S(2)}, u32[]{:S(2)}) collective-permute-start(bf16[448,128]{1,0:T(8,128)(2,1)S(1)} %get-tuple-element.55), channel_id=1, source_target_pairs={{0,16},{8,24},{16,0},{24,8},{1,17},{9,25},{17,1},{25,9},{2,18},{10... | collective-permute-start | bytes 344072 | tf_op jit(solution)/shard_map/ppermute | solution.py:363
  9.7 2.2 %collective-permute-start.4 = (bf16[256,128]{1,0:T(8,128)(2,1)S(1)}, bf16[256,128]{1,0:T(8,128)(2,1)S(1)}, u32[]{:S(2)}, u32[]{:S(2)}) collective-permute-start(bf16[256,128]{1,0:T(8,128)(2,1)S(1)} %get-tuple-element.30), channel_id=1, source_target_pairs={{0,6},{1,7},{2,4},{3,5},{4,2},{5,3},{6,0},{7,1},{8,14},{9,15},{10,... | collective-permute-start | bytes 196616 | tf_op jit(solution)/shard_map/ppermute | solution.py:326
  11.9 2.7 %collective-permute-start.6 = (bf16[896,128]{1,0:T(8,128)(2,1)S(1)}, bf16[896,128]{1,0:T(8,128)(2,1)S(1)}, u32[]{:S(2)}, u32[]{:S(2)}) collective-permute-start(bf16[896,128]{1,0:T(8,128)(2,1)S(1)} %get-tuple-element.32), channel_id=1, source_target_pairs={{0,8},{1,25},{2,10},{3,27},{4,12},{5,29},{6,14},{7,31},{8,16},{9,1... | collective-permute-start | bytes 688136 | tf_op jit(solution)/shard_map/ppermute | solution.py:362
  14.6 3.0 %collective-permute-done.1 = bf16[448,128]{1,0:T(8,128)(2,1)S(1)} collective-permute-done((bf16[448,128]{1,0:T(8,128)(2,1)S(1)}, bf16[448,128]{1,0:T(8,128)(2,1)S(1)}, u32[]{:S(2)}, u32[]{:S(2)}) %collective-permute-start.1) | collective-permute-done | bytes 114720 | tf_op jit(solution)/shard_map/ppermute | solution.py:363
  17.6 1.3 %collective-permute-start.5 = (bf16[1856,128]{1,0:T(8,128)(2,1)S(1)}, bf16[1856,128]{1,0:T(8,128)(2,1)S(1)}, u32[]{:S(2)}, u32[]{:S(2)}) collective-permute-start(bf16[1856,128]{1,0:T(8,128)(2,1)S(1)} %pad_maximum_fusion.refs_0_), channel_id=1, source_target_pairs={{0,2},{1,5},{2,0},{3,7},{4,6},{5,1},{6,4},{7,3},{8,10},{9,13},{10,... | collective-permute-start | bytes 1425416 | tf_op jit(solution)/shard_map/ppermute | solution.py:331
  18.9 1.4 %collective-permute-done.6 = bf16[896,128]{1,0:T(8,128)(2,1)S(1)} collective-permute-done((bf16[896,128]{1,0:T(8,128)(2,1)S(1)}, bf16[896,128]{1,0:T(8,128)(2,1)S(1)}, u32[]{:S(2)}, u32[]{:S(2)}) %collective-permute-start.6) | collective-permute-done | bytes 229408 | tf_op jit(solution)/shard_map/ppermute | solution.py:362
  20.4 6.7 %collective-permute-done.7 = bf16[448,128]{1,0:T(8,128)(2,1)S(1)} collective-permute-done((bf16[448,128]{1,0:T(8,128)(2,1)S(1)}, bf16[448,128]{1,0:T(8,128)(2,1)S(1)}, u32[]{:S(2)}, u32[]{:S(2)}) %collective-permute-start.7) | collective-permute-done | bytes 114720 | tf_op jit(solution)/shard_map/ppermute | solution.py:363
  27.2 0.5 collective-permute-start.10
  27.7 1.2 %collective-permute-start.8 = (bf16[1344,128]{1,0:T(8,128)(2,1)S(1)}, bf16[1344,128]{1,0:T(8,128)(2,1)S(1)}, u32[]{:S(2)}, u32[]{:S(2)}) collective-permute-start(bf16[1344,128]{1,0:T(8,128)(2,1)S(1)} %constant_dynamic-update-slice_fusion.refs_1_), channel_id=1, source_target_pairs={{0,2},{1,5},{2,0},{3,7},{4,6},{5,1},{6,4},{7,3},{8,10},{9,13},{10,... | collective-permute-start | bytes 1032200 | tf_op jit(solution)/shard_map/ppermute | solution.py:331
  29.0 0.4 collective-permute-start.13
  29.4 0.2 collective-permute-start.11
  29.7 0.3 collective-permute-start.12
  30.0 1.1 %collective-permute-done.12.refs_7_.refs_8_ = bf16[256,128]{1,0:T(8,128)(2,1)S(1)} collective-permute-done((bf16[256,128]{1,0:T(8,128)(2,1)S(1)}, bf16[256,128]{1,0:T(8,128)(2,1)S(1)}, u32[]{:S(2)}, u32[]{:S(2)}) %collective-permute-start.12) | collective-permute-done | bytes 65568 | tf_op jit(solution)/shard_map/ppermute | solution.py:326
  31.1 4.9 %shard_map.60 = (f32[1024,128]{1,0:T(8,128)S(1)}, bf16[4,1280,256]{2,1,0:T(8,128)(2,1)S(1)}, bf16[4,1024,256]{2,1,0:T(8,128)(2,1)S(1)}, bf16[2,10,128,384]{3,2,1...) custom-call(s32[3]{0:T(128)S(1)} %pad_add_fusion.me_ref, ...), custom_call_target="tpu_custom_call" | custom-call | flops 209715200 | bytes 2097152 | tf_op jit(solution)/shard_map/pallas_call | solution.py:312
  36.0 0.3 collective-permute-start.14
  36.3 1.8 %shard_map.61 = (f32[1024,128]{1,0:T(8,128)S(1)}, bf16[4,1024,256]{2,1,0:T(8,128)(2,1)S(1)}, bf16[2,10,128,384]{3,2,1,0:T(8,128)(2,1)S(1)}, bf16[2,1024,256]{2,1,0:T(8,128)(2,1)S(1)}) custom-call(s32[3]{0:T(128)S(1)} %pad_add_fusion.me_ref, ...), custom_call_target="tpu_custom_call", output_to_operand_aliasing={{0}: (3, {}), {1}: (4, {}), {2}: (5, {}), {3}: (6, {})} | custom-call | flops 209715200 | bytes 2097152 | tf_op jit(solution)/shard_map/pallas_call | solution.py:312
  38.1 11.5 %shard_map.62 = (f32[1024,128]{1,0:T(8,128)S(1)}, bf16[896,128]{1,0:T(8,128)(2,1)S(1)}) custom-call(s32[3]{0:T(128)S(1)} %pad_add_fusion.me_ref, bf16[2,1,1728,128]{3,2,1,0:T(8,128)(2,1)S(1)} %bitcast.26, bf16[2,1,64,128]{3,2,1,0:T(8,128)(2,1)S(1)} %copy-done.1, bf16[1856,128]{1,0:T(8,128)(2,1)S(1)} %collective-permute-done.5.refs_1_.refs_0_, ...), custom_call_target="tpu_custom_call" | custom-call | flops 4194304000 | bytes 41943040 | tf_op jit(solution)/shard_map/pallas_call | solution.py:312
  49.6 1.3 %collective-permute-start.19 = (bf16[896,128]{1,0:T(8,128)(2,1)S(1)}, bf16[896,128]{1,0:T(8,128)(2,1)S(1)}, u32[]{:S(2)}, u32[]{:S(2)}) collective-permute-start(bf16[896,128]{1,0:T(8,128)(2,1)S(1)} %get-tuple-element.48), channel_id=1, source_target_pairs={{0,2},{1,5},{2,0},{3,7},{4,6},{5,1},{6,4},{7,3},{8,10},{9,13},{10,... | collective-permute-start | bytes 688136 | tf_op jit(solution)/shard_map/ppermute | solution.py:331
  50.9 5.0 %shard_map.63 = bf16[896,128]{1,0:T(8,128)(2,1)S(1)} custom-call(s32[3]{0:T(128)S(1)} %pad_add_fusion.me_ref, f32[1024,128]{1,0:T(8,128)S(1)} %get-tuple-element.44.up_in, bf16[4,1280,256]{2,1,0:T(8,128)(2,1)S(1)} %get-tuple-element.38.folded, bf16[4,1024,256]{2,1,0:T(8,128)(2,1)S(1)} %get-tuple-element.45.slope, ...), custom_call_target="tpu_custom_call" | custom-call | flops 2097152000 | bytes 20971520 | tf_op jit(solution)/shard_map/pallas_call | solution.py:312
  56.0 0.3 collective-permute-start.15
  56.3 1.2 %collective-permute-start.20 = (bf16[896,128]{1,0:T(8,128)(2,1)S(1)}, bf16[896,128]{1,0:T(8,128)(2,1)S(1)}, u32[]{:S(2)}, u32[]{:S(2)}) collective-permute-start(bf16[896,128]{1,0:T(8,128)(2,1)S(1)} %add_convert_fusion.own_a), channel_id=1, source_target_pairs={{0,4},{1,3},{2,6},{3,1},{4,0},{5,7},{6,2},{7,5},{8,12},{9,11},{10,... | collective-permute-start | bytes 688136 | tf_op jit(solution)/shard_map/ppermute | solution.py:331
  57.6 4.6 %collective-permute-done.15 = bf16[896,128]{1,0:T(8,128)(2,1)S(1)} collective-permute-done((bf16[896,128]{1,0:T(8,128)(2,1)S(1)}, bf16[896,128]{1,0:T(8,128)(2,1)S(1)}, u32[]{:S(2)}, u32[]{:S(2)}) %collective-permute-start.15) | collective-permute-done | bytes 229408 | tf_op jit(solution)/shard_map/ppermute | solution.py:331
  62.2 1.0 %collective-permute-start.16 = (bf16[896,128]{1,0:T(8,128)(2,1)S(1)}, bf16[896,128]{1,0:T(8,128)(2,1)S(1)}, u32[]{:S(2)}, u32[]{:S(2)}) collective-permute-start(bf16[896,128]{1,0:T(8,128)(2,1)S(1)} %add_convert_fusion.1.own_a), channel_id=1, source_target_pairs={{0,4},{1,3},{2,6},{3,1},{4,0},{5,7},{6,2},{7,5},{8,12},{9,11},{10,... | collective-permute-start | bytes 688136 | tf_op jit(solution)/shard_map/ppermute | solution.py:331
  63.2 3.2 %collective-permute-start.21 = (bf16[896,128]{1,0:T(8,128)(2,1)S(1)}, bf16[896,128]{1,0:T(8,128)(2,1)S(1)}, u32[]{:S(2)}, u32[]{:S(2)}) collective-permute-start(bf16[896,128]{1,0:T(8,128)(2,1)S(1)} %add_convert_fusion.own_a), channel_id=1, source_target_pairs={{0,1},{1,0},{2,3},{3,2},{4,5},{5,4},{6,7},{7,6},{8,9},{9,8},{10,11... | collective-permute-start | bytes 688136 | tf_op jit(solution)/shard_map/ppermute | solution.py:326
  66.4 0.5 collective-permute-start.17
  67.1 3.5 %collective-permute-start.18 = (bf16[896,128]{1,0:T(8,128)(2,1)S(1)}, bf16[896,128]{1,0:T(8,128)(2,1)S(1)}, u32[]{:S(2)}, u32[]{:S(2)}) collective-permute-start(bf16[896,128]{1,0:T(8,128)(2,1)S(1)} %collective-permute-done.16.own_b), channel_id=1, source_target_pairs={{0,1},{1,0},{2,3},{3,2},{4,5},{5,4},{6,7},{7,6},{8,9},{9,8},{10,11... | collective-permute-start | bytes 688136 | tf_op jit(solution)/shard_map/ppermute | solution.py:326
  70.6 1.7 %shard_map.64 = (f32[2,1,1728,128]{3,2,1,0:T(8,128)}, f32[2,1,64,128]{3,2,1,0:T(8,128)}) custom-call(s32[3]{0:T(128)S(1)} %pad_add_fusion.me_ref, bf16[896,128]{1,0:T(8,128)(2,1)S(1)} %add_convert_fusion.own_a, bf16[896,128]{1,0:T(8,128)(2,1)S(1)} %collective-permute-done.20.own_b, bf16[896,128]{1,0:T(8,128)(2,1)S(1)} %collective-permute-done.21.far_a, ...), custom_call_target="tpu_custom_call" | custom-call | flops 6553600 | bytes 65536 | tf_op jit(solution)/shard_map/pallas_call | solution.py:312
  72.3 1.7 %shard_map.65 = (f32[2,1,1728,128]{3,2,1,0:T(8,128)}, f32[2,1,64,128]{3,2,1,0:T(8,128)}) custom-call(s32[3]{0:T(128)S(1)} %pad_add_fusion.me_ref, bf16[896,128]{1,0:T(8,128)(2,1)S(1)} %add_convert_fusion.1.own_a, bf16[896,128]{1,0:T(8,128)(2,1)S(1)} %collective-permute-done.16.own_b, ...), custom_call_target="tpu_custom_call", output_to_operand_aliasing={{0}: (5, {}), {1}: (6, {})} | custom-call | flops 6553600 | bytes 65536 | tf_op jit(solution)/shard_map/pallas_call | solution.py:312
  (42 shorter events, 0.9 us)
Async XLA Ops:
  0.6 6.9 %copy-start.2 = (bf16[4,64,1,2,128]{4,3,2,1,0:T(2,128)(2,1)S(1)}, bf16[4,64,1,2,128]{4,3,2,1,0:T(2,128)(2,1)}, u32[]{:S(2)}) copy-start(bf16[4,64,1,2,128]{4,3,2,1,0:T(2,128)(2,1)} %param.4) | copy-start | bytes 393220
  0.6 6.8 %copy-start.3 = (bf16[4,64,1,2,128]{4,3,2,1,0:T(2,128)(2,1)S(1)}, bf16[4,64,1,2,128]{4,3,2,1,0:T(2,128)(2,1)}, u32[]{:S(2)}) copy-start(bf16[4,64,1,2,128]{4,3,2,1,0:T(2,128)(2,1)} %param.5) | copy-start | bytes 393220
  2.1 29.0 %copy-start = (bf16[2,1,128,1728]{2,3,1,0:T(8,128)(2,1)S(1)}, bf16[2,1,128,1728]{2,3,1,0:T(8,128)(2,1)}, u32[]{:S(2)}) copy-start(bf16[2,1,128,1728]{2,3,1,0:T(8,128)(2,1)} %param.6) | copy-start | bytes 2654212
  2.1 29.0 %copy-start.1 = (bf16[2,1,64,128]{3,2,1,0:T(8,128)(2,1)S(1)}, bf16[2,1,64,128]{3,2,1,0:T(8,128)(2,1)}, u32[]{:S(2)}) copy-start(bf16[2,1,64,128]{3,2,1,0:T(8,128)(2,1)} %mix.3) | copy-start | bytes 98308
  2.1 9.8 %collective-permute-start = (bf16[896,128]{1,0:T(8,128)(2,1)S(1)}, bf16[896,128]{1,0:T(8,128)(2,1)S(1)}, u32[]{:S(2)}, u32[]{:S(2)}) collective-permute-start(bf16[896,128]{1,0:T(8,128)(2,1)S(1)} %get-tuple-element.57), channel_id=1, source_target_pairs={{0,8},{1,25},{2,10},{3,27},{4,12},{5,29},{6,14},{7,31},{8,16},{9,1... | collective-permute-start | bytes 688136 | tf_op jit(solution)/shard_map/ppermute | solution.py:362
  6.3 1.2 %collective-permute-start.2 = (bf16[16,128]{1,0:T(8,128)(2,1)S(1)}, bf16[16,128]{1,0:T(8,128)(2,1)S(1)}, u32[]{:S(2)}, u32[]{:S(2)}) collective-permute-start(bf16[16,128]{1,0:T(8,128)(2,1)S(1)} %slice_bitcast_fusion.2), channel_id=1, source_target_pairs={{0,1},{1,0},{2,3},{3,2},{4,5},{5,4},{6,7},{7,6},{8,9},{9,8},{10,11... | collective-permute-start | bytes 12296 | tf_op jit(solution)/shard_map/ppermute | solution.py:326
  8.3 3.6 %collective-permute-start.3 = (bf16[512,128]{1,0:T(8,128)(2,1)S(1)}, bf16[512,128]{1,0:T(8,128)(2,1)S(1)}, u32[]{:S(2)}, u32[]{:S(2)}) collective-permute-start(bf16[512,128]{1,0:T(8,128)(2,1)S(1)} %get-tuple-element.29), channel_id=1, source_target_pairs={{0,1},{1,0},{2,3},{3,2},{4,5},{5,4},{6,7},{7,6},{8,9},{9,8},{10,11... | collective-permute-start | bytes 393224 | tf_op jit(solution)/shard_map/ppermute | solution.py:326
  8.6 9.0 %collective-permute-start.1 = (bf16[448,128]{1,0:T(8,128)(2,1)S(1)}, bf16[448,128]{1,0:T(8,128)(2,1)S(1)}, u32[]{:S(2)}, u32[]{:S(2)}) collective-permute-start(bf16[448,128]{1,0:T(8,128)(2,1)S(1)} %get-tuple-element.55), channel_id=1, source_target_pairs={{0,16},{8,24},{16,0},{24,8},{1,17},{9,25},{17,1},{25,9},{2,18},{10... | collective-permute-start | bytes 344072 | tf_op jit(solution)/shard_map/ppermute | solution.py:363
  9.7 7.9 %collective-permute-start.4 = (bf16[256,128]{1,0:T(8,128)(2,1)S(1)}, bf16[256,128]{1,0:T(8,128)(2,1)S(1)}, u32[]{:S(2)}, u32[]{:S(2)}) collective-permute-start(bf16[256,128]{1,0:T(8,128)(2,1)S(1)} %get-tuple-element.30), channel_id=1, source_target_pairs={{0,6},{1,7},{2,4},{3,5},{4,2},{5,3},{6,0},{7,1},{8,14},{9,15},{10,... | collective-permute-start | bytes 196616 | tf_op jit(solution)/shard_map/ppermute | solution.py:326
  11.9 8.5 %collective-permute-start.6 = (bf16[896,128]{1,0:T(8,128)(2,1)S(1)}, bf16[896,128]{1,0:T(8,128)(2,1)S(1)}, u32[]{:S(2)}, u32[]{:S(2)}) collective-permute-start(bf16[896,128]{1,0:T(8,128)(2,1)S(1)} %get-tuple-element.32), channel_id=1, source_target_pairs={{0,8},{1,25},{2,10},{3,27},{4,12},{5,29},{6,14},{7,31},{8,16},{9,1... | collective-permute-start | bytes 688136 | tf_op jit(solution)/shard_map/ppermute | solution.py:362
  14.6 12.5 %collective-permute-start.7 = (bf16[448,128]{1,0:T(8,128)(2,1)S(1)}, bf16[448,128]{1,0:T(8,128)(2,1)S(1)}, u32[]{:S(2)}, u32[]{:S(2)}) collective-permute-start(bf16[448,128]{1,0:T(8,128)(2,1)S(1)} %get-tuple-element.33), channel_id=1, source_target_pairs={{0,16},{8,24},{16,0},{24,8},{1,17},{9,25},{17,1},{25,9},{2,18},{10... | collective-permute-start | bytes 344072 | tf_op jit(solution)/shard_map/ppermute | solution.py:363
  17.6 11.3 %collective-permute-start.5 = (bf16[1856,128]{1,0:T(8,128)(2,1)S(1)}, bf16[1856,128]{1,0:T(8,128)(2,1)S(1)}, u32[]{:S(2)}, u32[]{:S(2)}) collective-permute-start(bf16[1856,128]{1,0:T(8,128)(2,1)S(1)} %pad_maximum_fusion.refs_0_), channel_id=1, source_target_pairs={{0,2},{1,5},{2,0},{3,7},{4,6},{5,1},{6,4},{7,3},{8,10},{9,13},{10,... | collective-permute-start | bytes 1425416 | tf_op jit(solution)/shard_map/ppermute | solution.py:331
  27.2 1.8 %collective-permute-start.9 = (bf16[1344,128]{1,0:T(8,128)(2,1)S(1)}, bf16[1344,128]{1,0:T(8,128)(2,1)S(1)}, u32[]{:S(2)}, u32[]{:S(2)}) collective-permute-start(bf16[1344,128]{1,0:T(8,128)(2,1)S(1)} %constant_dynamic-update-slice_fusion.refs_1_), channel_id=1, source_target_pairs={{0,1},{1,0},{2,3},{3,2},{4,5},{5,4},{6,7},{7,6},{8,9},{9,8},{10,11... | collective-permute-start | bytes 1032200 | tf_op jit(solution)/shard_map/ppermute | solution.py:326
  27.2 3.8 %collective-permute-start.10 = (bf16[1856,128]{1,0:T(8,128)(2,1)S(1)}, bf16[1856,128]{1,0:T(8,128)(2,1)S(1)}, u32[]{:S(2)}, u32[]{:S(2)}) collective-permute-start(bf16[1856,128]{1,0:T(8,128)(2,1)S(1)} %pad_maximum_fusion.refs_0_), channel_id=1, source_target_pairs={{0,1},{1,0},{2,3},{3,2},{4,5},{5,4},{6,7},{7,6},{8,9},{9,8},{10,11... | collective-permute-start | bytes 1425416 | tf_op jit(solution)/shard_map/ppermute | solution.py:326
  27.7 8.2 %collective-permute-start.8 = (bf16[1344,128]{1,0:T(8,128)(2,1)S(1)}, bf16[1344,128]{1,0:T(8,128)(2,1)S(1)}, u32[]{:S(2)}, u32[]{:S(2)}) collective-permute-start(bf16[1344,128]{1,0:T(8,128)(2,1)S(1)} %constant_dynamic-update-slice_fusion.refs_1_), channel_id=1, source_target_pairs={{0,2},{1,5},{2,0},{3,7},{4,6},{5,1},{6,4},{7,3},{8,10},{9,13},{10,... | collective-permute-start | bytes 1032200 | tf_op jit(solution)/shard_map/ppermute | solution.py:331
  29.0 2.1 %collective-permute-start.13 = (bf16[960,128]{1,0:T(8,128)(2,1)S(1)}, bf16[960,128]{1,0:T(8,128)(2,1)S(1)}, u32[]{:S(2)}, u32[]{:S(2)}) collective-permute-start(bf16[960,128]{1,0:T(8,128)(2,1)S(1)} %slice.39), channel_id=1, source_target_pairs={{0,1},{1,0},{2,3},{3,2},{4,5},{5,4},{6,7},{7,6},{8,9},{9,8},{10,11... | collective-permute-start | bytes 737288 | tf_op jit(solution)/shard_map/ppermute | solution.py:326
  29.4 1.7 %collective-permute-start.11 = (bf16[896,128]{1,0:T(8,128)(2,1)S(1)}, bf16[896,128]{1,0:T(8,128)(2,1)S(1)}, u32[]{:S(2)}, u32[]{:S(2)}) collective-permute-start(bf16[896,128]{1,0:T(8,128)(2,1)S(1)} %slice.38), channel_id=1, source_target_pairs={{0,1},{1,0},{2,3},{3,2},{4,5},{5,4},{6,7},{7,6},{8,9},{9,8},{10,11... | collective-permute-start | bytes 688136 | tf_op jit(solution)/shard_map/ppermute | solution.py:326
  29.7 1.4 %collective-permute-start.12 = (bf16[256,128]{1,0:T(8,128)(2,1)S(1)}, bf16[256,128]{1,0:T(8,128)(2,1)S(1)}, u32[]{:S(2)}, u32[]{:S(2)}) collective-permute-start(bf16[256,128]{1,0:T(8,128)(2,1)S(1)} %collective-permute-done.4.refs_6_.refs_7_), channel_id=1, source_target_pairs={{0,1},{1,0},{2,3},{3,2},{4,5},{5,4},{6,7},{7,6},{8,9},{9,8},{10,11... | collective-permute-start | bytes 196616 | tf_op jit(solution)/shard_map/ppermute | solution.py:326
  36.0 2.1 %collective-permute-start.14 = (bf16[1344,128]{1,0:T(8,128)(2,1)S(1)}, bf16[1344,128]{1,0:T(8,128)(2,1)S(1)}, u32[]{:S(2)}, u32[]{:S(2)}) collective-permute-start(bf16[1344,128]{1,0:T(8,128)(2,1)S(1)} %collective-permute-done.8.refs_2_), channel_id=1, source_target_pairs={{0,1},{1,0},{2,3},{3,2},{4,5},{5,4},{6,7},{7,6},{8,9},{9,8},{10,11... | collective-permute-start | bytes 1032200 | tf_op jit(solution)/shard_map/ppermute | solution.py:326
  49.6 6.7 %collective-permute-start.19 = (bf16[896,128]{1,0:T(8,128)(2,1)S(1)}, bf16[896,128]{1,0:T(8,128)(2,1)S(1)}, u32[]{:S(2)}, u32[]{:S(2)}) collective-permute-start(bf16[896,128]{1,0:T(8,128)(2,1)S(1)} %get-tuple-element.48), channel_id=1, source_target_pairs={{0,2},{1,5},{2,0},{3,7},{4,6},{5,1},{6,4},{7,3},{8,10},{9,13},{10,... | collective-permute-start | bytes 688136 | tf_op jit(solution)/shard_map/ppermute | solution.py:331
  56.0 6.1 %collective-permute-start.15 = (bf16[896,128]{1,0:T(8,128)(2,1)S(1)}, bf16[896,128]{1,0:T(8,128)(2,1)S(1)}, u32[]{:S(2)}, u32[]{:S(2)}) collective-permute-start(bf16[896,128]{1,0:T(8,128)(2,1)S(1)} %shard_map.63), channel_id=1, source_target_pairs={{0,2},{1,5},{2,0},{3,7},{4,6},{5,1},{6,4},{7,3},{8,10},{9,13},{10,... | collective-permute-start | bytes 688136 | tf_op jit(solution)/shard_map/ppermute | solution.py:331
  56.3 10.0 %collective-permute-start.20 = (bf16[896,128]{1,0:T(8,128)(2,1)S(1)}, bf16[896,128]{1,0:T(8,128)(2,1)S(1)}, u32[]{:S(2)}, u32[]{:S(2)}) collective-permute-start(bf16[896,128]{1,0:T(8,128)(2,1)S(1)} %add_convert_fusion.own_a), channel_id=1, source_target_pairs={{0,4},{1,3},{2,6},{3,1},{4,0},{5,7},{6,2},{7,5},{8,12},{9,11},{10,... | collective-permute-start | bytes 688136 | tf_op jit(solution)/shard_map/ppermute | solution.py:331
  62.2 4.9 %collective-permute-start.16 = (bf16[896,128]{1,0:T(8,128)(2,1)S(1)}, bf16[896,128]{1,0:T(8,128)(2,1)S(1)}, u32[]{:S(2)}, u32[]{:S(2)}) collective-permute-start(bf16[896,128]{1,0:T(8,128)(2,1)S(1)} %add_convert_fusion.1.own_a), channel_id=1, source_target_pairs={{0,4},{1,3},{2,6},{3,1},{4,0},{5,7},{6,2},{7,5},{8,12},{9,11},{10,... | collective-permute-start | bytes 688136 | tf_op jit(solution)/shard_map/ppermute | solution.py:331
  63.2 7.4 %collective-permute-start.21 = (bf16[896,128]{1,0:T(8,128)(2,1)S(1)}, bf16[896,128]{1,0:T(8,128)(2,1)S(1)}, u32[]{:S(2)}, u32[]{:S(2)}) collective-permute-start(bf16[896,128]{1,0:T(8,128)(2,1)S(1)} %add_convert_fusion.own_a), channel_id=1, source_target_pairs={{0,1},{1,0},{2,3},{3,2},{4,5},{5,4},{6,7},{7,6},{8,9},{9,8},{10,11... | collective-permute-start | bytes 688136 | tf_op jit(solution)/shard_map/ppermute | solution.py:326
  66.4 4.2 %collective-permute-start.22 = (bf16[896,128]{1,0:T(8,128)(2,1)S(1)}, bf16[896,128]{1,0:T(8,128)(2,1)S(1)}, u32[]{:S(2)}, u32[]{:S(2)}) collective-permute-start(bf16[896,128]{1,0:T(8,128)(2,1)S(1)} %collective-permute-done.20.own_b), channel_id=1, source_target_pairs={{0,1},{1,0},{2,3},{3,2},{4,5},{5,4},{6,7},{7,6},{8,9},{9,8},{10,11... | collective-permute-start | bytes 688136 | tf_op jit(solution)/shard_map/ppermute | solution.py:326
  66.4 5.9 %collective-permute-start.17 = (bf16[896,128]{1,0:T(8,128)(2,1)S(1)}, bf16[896,128]{1,0:T(8,128)(2,1)S(1)}, u32[]{:S(2)}, u32[]{:S(2)}) collective-permute-start(bf16[896,128]{1,0:T(8,128)(2,1)S(1)} %add_convert_fusion.1.own_a), channel_id=1, source_target_pairs={{0,1},{1,0},{2,3},{3,2},{4,5},{5,4},{6,7},{7,6},{8,9},{9,8},{10,11... | collective-permute-start | bytes 688136 | tf_op jit(solution)/shard_map/ppermute | solution.py:326
  67.1 5.2 %collective-permute-start.18 = (bf16[896,128]{1,0:T(8,128)(2,1)S(1)}, bf16[896,128]{1,0:T(8,128)(2,1)S(1)}, u32[]{:S(2)}, u32[]{:S(2)}) collective-permute-start(bf16[896,128]{1,0:T(8,128)(2,1)S(1)} %collective-permute-done.16.own_b), channel_id=1, source_target_pairs={{0,1},{1,0},{2,3},{3,2},{4,5},{5,4},{6,7},{7,6},{8,9},{9,8},{10,11... | collective-permute-start | bytes 688136 | tf_op jit(solution)/shard_map/ppermute | solution.py:326

commit v6 on v5

--- a/solution.py
+++ b/solution.py
@@ -255,30 +255,15 @@
     all_back(shares, me_ref, False, up, grad, wide, folded, slope, keep_a, keep_h, terms, out)
 
 
-def send_taps(taps, factor, value, conv, mix, group, whole, sems):
+def place_taps(taps, factor, value, whole):
     for number, tap in enumerate(taps):
         whole[64 * tap : 64 * tap + 64] = value[64 * number : 64 * number + 64] * factor
-    runs = []
-    for tap in sorted(taps):
-        if runs and tap < 27 and tap == runs[-1][1]:
-            runs[-1][1] += 1
-        else:
-            runs.append([tap, tap + 1])
-    copies = []
-    for start, stop in runs:
-        rows = pl.ds(64 * start, 64 * (stop - start))
-        copies.append((whole.at[rows], mix.at[group, 0] if start == 27 else conv.at[group, 0, rows]))
-    return begin(copies, sems, 0)
-
-
-def pair_kernel(group, factor, swapped, me_ref, a, b, *refs):
-    conv, mix, whole, sems = refs[-4:]
-    for core in range(2):
-
-        @pl.when((me_ref[2] ^ swapped) == core)
-        def _(core=core):
-            value = a[...].astype(F32) + b[...].astype(F32)
-            finish(send_taps(SHARES[core], factor, value, conv, mix, group, whole, sems))
+
+
+def send_whole(whole, conv, mix, group, sems):
+    taps = conv.shape[2]
+    copies = [(whole.at[pl.ds(row, taps // 3)], conv.at[group, 0, pl.ds(row, taps // 3)]) for row in range(0, taps, taps // 3)]
+    finish(begin(copies + [(whole.at[pl.ds(taps, whole.shape[0] - taps)], mix.at[group, 0])], sems, 0))
 
 
 def both_kernel(group, factor, me_ref, own_a, own_b, far_a, far_b, *refs):
@@ -286,14 +271,15 @@
     first = me_ref[2] == 0
     own = own_a[...].astype(F32) + own_b[...].astype(F32)
     far = far_a[...].astype(F32) + far_b[...].astype(F32)
-    started = send_taps(SHARES[0], factor, jnp.where(first, own, far), conv, mix, group, whole, sems.at[0])
-    started += send_taps(SHARES[1], factor, jnp.where(first, far, own), conv, mix, group, whole, sems.at[1])
-    finish(started)
+    place_taps(SHARES[0], factor, jnp.where(first, own, far), whole)
+    place_taps(SHARES[1], factor, jnp.where(first, far, own), whole)
+    send_whole(whole, conv, mix, group, sems)
 
 
 def plain_kernel(group, factor, me_ref, terms, *refs):
     conv, mix, whole, sems = refs[-4:]
-    finish(send_taps(range(28), factor, terms[...].astype(F32), conv, mix, group, whole, sems.at[0]))
+    place_taps(range(28), factor, terms[...].astype(F32), whole)
+    send_whole(whole, conv, mix, group, sems)
 
 
 def size_of(x):
@@ -313,7 +299,7 @@
         kernel,
         out_shape=outs,
         in_specs=specs,
-        out_specs=[far if kernel.func in (pair_kernel, both_kernel, plain_kernel) else vmem] * len(outs),
+        out_specs=[far if kernel.func in (both_kernel, plain_kernel) else vmem] * len(outs),
         scratch_shapes=scratch,
         input_output_aliases={len(args) + i: i for i in range(len(into))},
         compiler_params=pltpu.CompilerParams(vmem_limit_bytes=limit),
@@ -511,7 +497,7 @@
         jax.ShapeDtypeStruct((groups, 1, taps, hidden), F32),
         jax.ShapeDtypeStruct((groups, 1, channels, hidden), F32),
     ]
-    scratch = [pltpu.VMEM((width, hidden), F32), pltpu.SemaphoreType.DMA((2, 8))]
+    scratch = [pltpu.VMEM((width, hidden), F32), pltpu.SemaphoreType.DMA((4,))]
     grads = ()
     for group in (1, 0):
         own = late_terms if group else early_terms

time: 74.4 us -> 74.2 us (level)
  no operation moved by 1% of the time
where the time goes in v6:
time: 74.2 us; the launch traced here: 74.1 us
  Pallas kernels  27.3 us (37%)
  starting transfers between devices  25.9 us (35%)
  waiting for transfers between devices  18.1 us (24%)
  other arithmetic  1.58 us (2%)
  between operations  1.05 us (1%)
    pallas_call x7, Pallas kernels, call(): pl.pallas_call(kernel, out_shape=outs, in_specs=specs, out_specs=[far if...  27.3 us
    ppermute x13, starting transfers between devices, exchange(): return lax.ppermute(block, 'space', [(i, i ^ mask) for i in range(count)])  11.5 us
    ppermute x2, waiting for transfers between devices, gather_paired(): lax.ppermute(after(part[group], *near[:group]), 'section', across)  9.72 us
    ppermute x2, starting transfers between devices, gather_paired(): lax.ppermute(after(mine[group], *near), ('section', 'space'), route)  6.94 us
    ppermute x6, starting transfers between devices, cross(): lax.ppermute(block, 'space', [(i, i ^ (second if i % 2 else first)) for i...  6.35 us
    ppermute x6, waiting for transfers between devices, cross(): lax.ppermute(block, 'space', [(i, i ^ (second if i % 2 else first)) for i...  4.78 us
    ppermute x13, waiting for transfers between devices, exchange(): return lax.ppermute(block, 'space', [(i, i ^ mask) for i in range(count)])  2.19 us
  transfers between devices with their start and end apart: 23, of which 7 were waited for; matrix products, arithmetic and copies ran while one was open for 0% of the time, Pallas kernels for 19%

profile of v6, /device:TPU:1, one launch (start us, length us, event | category | flops | bytes accessed | tf_op | source)
XLA Modules:
  0.0 74.1 jit_solution(14388201999246386607)
XLA Ops:
  0.7 1.3 %fusion = bf16[2,896,128]{2,1,0:T(8,128)(2,1)S(1)} fusion(bf16[2,64,128]{2,1,0:T(8,128)(2,1)} %bitcast.27, bf16[2,1728,128]{2,1,0:T(8,128)(2,1)} %bitcast.24, pred[]{:T(512)S(6)} %eq.7), kind=kLoop, calls=%fused_computation.2 | loop fusion | flops 1146880 | bytes 1835009 | tf_op jit(solution)/shard_map/jit(_where)/select_n | solution.py:330
  2.1 4.2 %collective-permute-start = (bf16[896,128]{1,0:T(8,128)(2,1)S(1)}, bf16[896,128]{1,0:T(8,128)(2,1)S(1)}, u32[]{:S(2)}, u32[]{:S(2)}) collective-permute-start(bf16[896,128]{1,0:T(8,128)(2,1)S(1)} %get-tuple-element.57), channel_id=1, source_target_pairs={{0,8},{1,25},{2,10},{3,27},{4,12},{5,29},{6,14},{7,31},{8,16},{9,1... | collective-permute-start | bytes 688136 | tf_op jit(solution)/shard_map/ppermute | solution.py:348
  6.4 1.1 %collective-permute-done.2.token = bf16[16,128]{1,0:T(8,128)(2,1)S(1)} collective-permute-done((bf16[16,128]{1,0:T(8,128)(2,1)S(1)}, bf16[16,128]{1,0:T(8,128)(2,1)S(1)}, u32[]{:S(2)}, u32[]{:S(2)}) %collective-permute-start.2) | collective-permute-done | bytes 4128 | tf_op jit(solution)/shard_map/ppermute | solution.py:312
  7.5 0.8 %shard_map.59 = (bf16[256,128]{1,0:T(8,128)(2,1)S(1)}, bf16[256,128]{1,0:T(8,128)(2,1)S(1)}, bf16[256,128]{1,0:T(8,128)(2,1)S(1)}, bf16[512,128]{1,0:T(8,128)(2,1)S(1)}) custom-call(s32[3]{0:T(128)S(1)} %pad_add_fusion.me_ref, bf16[4,128,128]{2,1,0:T(8,128)(2,1)S(1)} %bitcast.28, bf16[4,128,128]{2,1,0:T(8,128)(2,1)S(1)} %bitcast.29, ...), custom_call_target="tpu_custom_call" | custom-call | flops 104857600 | bytes 1048576 | tf_op jit(solution)/shard_map/pallas_call | solution.py:298
  8.6 1.1 %collective-permute-start.1 = (bf16[448,128]{1,0:T(8,128)(2,1)S(1)}, bf16[448,128]{1,0:T(8,128)(2,1)S(1)}, u32[]{:S(2)}, u32[]{:S(2)}) collective-permute-start(bf16[448,128]{1,0:T(8,128)(2,1)S(1)} %get-tuple-element.55), channel_id=1, source_target_pairs={{0,16},{8,24},{16,0},{24,8},{1,17},{9,25},{17,1},{25,9},{2,18},{10... | collective-permute-start | bytes 344072 | tf_op jit(solution)/shard_map/ppermute | solution.py:349
  9.7 2.2 %collective-permute-start.4 = (bf16[256,128]{1,0:T(8,128)(2,1)S(1)}, bf16[256,128]{1,0:T(8,128)(2,1)S(1)}, u32[]{:S(2)}, u32[]{:S(2)}) collective-permute-start(bf16[256,128]{1,0:T(8,128)(2,1)S(1)} %get-tuple-element.30), channel_id=1, source_target_pairs={{0,6},{1,7},{2,4},{3,5},{4,2},{5,3},{6,0},{7,1},{8,14},{9,15},{10,... | collective-permute-start | bytes 196616 | tf_op jit(solution)/shard_map/ppermute | solution.py:312
  11.9 2.7 %collective-permute-start.6 = (bf16[896,128]{1,0:T(8,128)(2,1)S(1)}, bf16[896,128]{1,0:T(8,128)(2,1)S(1)}, u32[]{:S(2)}, u32[]{:S(2)}) collective-permute-start(bf16[896,128]{1,0:T(8,128)(2,1)S(1)} %get-tuple-element.32), channel_id=1, source_target_pairs={{0,8},{1,25},{2,10},{3,27},{4,12},{5,29},{6,14},{7,31},{8,16},{9,1... | collective-permute-start | bytes 688136 | tf_op jit(solution)/shard_map/ppermute | solution.py:348
  14.6 3.0 %collective-permute-done.1 = bf16[448,128]{1,0:T(8,128)(2,1)S(1)} collective-permute-done((bf16[448,128]{1,0:T(8,128)(2,1)S(1)}, bf16[448,128]{1,0:T(8,128)(2,1)S(1)}, u32[]{:S(2)}, u32[]{:S(2)}) %collective-permute-start.1) | collective-permute-done | bytes 114720 | tf_op jit(solution)/shard_map/ppermute | solution.py:349
  17.6 1.3 %collective-permute-start.5 = (bf16[1856,128]{1,0:T(8,128)(2,1)S(1)}, bf16[1856,128]{1,0:T(8,128)(2,1)S(1)}, u32[]{:S(2)}, u32[]{:S(2)}) collective-permute-start(bf16[1856,128]{1,0:T(8,128)(2,1)S(1)} %pad_maximum_fusion.refs_0_), channel_id=1, source_target_pairs={{0,2},{1,5},{2,0},{3,7},{4,6},{5,1},{6,4},{7,3},{8,10},{9,13},{10,... | collective-permute-start | bytes 1425416 | tf_op jit(solution)/shard_map/ppermute | solution.py:317
  18.9 1.4 %collective-permute-done.6 = bf16[896,128]{1,0:T(8,128)(2,1)S(1)} collective-permute-done((bf16[896,128]{1,0:T(8,128)(2,1)S(1)}, bf16[896,128]{1,0:T(8,128)(2,1)S(1)}, u32[]{:S(2)}, u32[]{:S(2)}) %collective-permute-start.6) | collective-permute-done | bytes 229408 | tf_op jit(solution)/shard_map/ppermute | solution.py:348
  20.4 6.7 %collective-permute-done.7 = bf16[448,128]{1,0:T(8,128)(2,1)S(1)} collective-permute-done((bf16[448,128]{1,0:T(8,128)(2,1)S(1)}, bf16[448,128]{1,0:T(8,128)(2,1)S(1)}, u32[]{:S(2)}, u32[]{:S(2)}) %collective-permute-start.7) | collective-permute-done | bytes 114720 | tf_op jit(solution)/shard_map/ppermute | solution.py:349
  27.2 0.5 collective-permute-start.10
  27.7 1.2 %collective-permute-start.8 = (bf16[1344,128]{1,0:T(8,128)(2,1)S(1)}, bf16[1344,128]{1,0:T(8,128)(2,1)S(1)}, u32[]{:S(2)}, u32[]{:S(2)}) collective-permute-start(bf16[1344,128]{1,0:T(8,128)(2,1)S(1)} %constant_dynamic-update-slice_fusion.refs_1_), channel_id=1, source_target_pairs={{0,2},{1,5},{2,0},{3,7},{4,6},{5,1},{6,4},{7,3},{8,10},{9,13},{10,... | collective-permute-start | bytes 1032200 | tf_op jit(solution)/shard_map/ppermute | solution.py:317
  29.0 0.4 collective-permute-start.13
  29.4 0.2 collective-permute-start.11
  29.7 0.3 collective-permute-start.12
  30.0 1.1 %collective-permute-done.12.refs_7_.refs_8_ = bf16[256,128]{1,0:T(8,128)(2,1)S(1)} collective-permute-done((bf16[256,128]{1,0:T(8,128)(2,1)S(1)}, bf16[256,128]{1,0:T(8,128)(2,1)S(1)}, u32[]{:S(2)}, u32[]{:S(2)}) %collective-permute-start.12) | collective-permute-done | bytes 65568 | tf_op jit(solution)/shard_map/ppermute | solution.py:312
  31.1 4.9 %shard_map.60 = (f32[1024,128]{1,0:T(8,128)S(1)}, bf16[4,1280,256]{2,1,0:T(8,128)(2,1)S(1)}, bf16[4,1024,256]{2,1,0:T(8,128)(2,1)S(1)}, bf16[2,10,128,384]{3,2,1...) custom-call(s32[3]{0:T(128)S(1)} %pad_add_fusion.me_ref, ...), custom_call_target="tpu_custom_call" | custom-call | flops 209715200 | bytes 2097152 | tf_op jit(solution)/shard_map/pallas_call | solution.py:298
  36.0 0.3 collective-permute-start.14
  36.3 1.8 %shard_map.61 = (f32[1024,128]{1,0:T(8,128)S(1)}, bf16[4,1024,256]{2,1,0:T(8,128)(2,1)S(1)}, bf16[2,10,128,384]{3,2,1,0:T(8,128)(2,1)S(1)}, bf16[2,1024,256]{2,1,0:T(8,128)(2,1)S(1)}) custom-call(s32[3]{0:T(128)S(1)} %pad_add_fusion.me_ref, ...), custom_call_target="tpu_custom_call", output_to_operand_aliasing={{0}: (3, {}), {1}: (4, {}), {2}: (5, {}), {3}: (6, {})} | custom-call | flops 209715200 | bytes 2097152 | tf_op jit(solution)/shard_map/pallas_call | solution.py:298
  38.1 11.5 %shard_map.62 = (f32[1024,128]{1,0:T(8,128)S(1)}, bf16[896,128]{1,0:T(8,128)(2,1)S(1)}) custom-call(s32[3]{0:T(128)S(1)} %pad_add_fusion.me_ref, bf16[2,1,1728,128]{3,2,1,0:T(8,128)(2,1)S(1)} %bitcast.26, bf16[2,1,64,128]{3,2,1,0:T(8,128)(2,1)S(1)} %copy-done.1, bf16[1856,128]{1,0:T(8,128)(2,1)S(1)} %collective-permute-done.5.refs_1_.refs_0_, ...), custom_call_target="tpu_custom_call" | custom-call | flops 4194304000 | bytes 41943040 | tf_op jit(solution)/shard_map/pallas_call | solution.py:298
  49.6 1.3 %collective-permute-start.19 = (bf16[896,128]{1,0:T(8,128)(2,1)S(1)}, bf16[896,128]{1,0:T(8,128)(2,1)S(1)}, u32[]{:S(2)}, u32[]{:S(2)}) collective-permute-start(bf16[896,128]{1,0:T(8,128)(2,1)S(1)} %get-tuple-element.48), channel_id=1, source_target_pairs={{0,2},{1,5},{2,0},{3,7},{4,6},{5,1},{6,4},{7,3},{8,10},{9,13},{10,... | collective-permute-start | bytes 688136 | tf_op jit(solution)/shard_map/ppermute | solution.py:317
  50.9 5.0 %shard_map.63 = bf16[896,128]{1,0:T(8,128)(2,1)S(1)} custom-call(s32[3]{0:T(128)S(1)} %pad_add_fusion.me_ref, f32[1024,128]{1,0:T(8,128)S(1)} %get-tuple-element.44.up_in, bf16[4,1280,256]{2,1,0:T(8,128)(2,1)S(1)} %get-tuple-element.38.folded, bf16[4,1024,256]{2,1,0:T(8,128)(2,1)S(1)} %get-tuple-element.45.slope, ...), custom_call_target="tpu_custom_call" | custom-call | flops 2097152000 | bytes 20971520 | tf_op jit(solution)/shard_map/pallas_call | solution.py:298
  56.0 0.3 collective-permute-start.15
  56.3 1.2 %collective-permute-start.20 = (bf16[896,128]{1,0:T(8,128)(2,1)S(1)}, bf16[896,128]{1,0:T(8,128)(2,1)S(1)}, u32[]{:S(2)}, u32[]{:S(2)}) collective-permute-start(bf16[896,128]{1,0:T(8,128)(2,1)S(1)} %add_convert_fusion.own_a), channel_id=1, source_target_pairs={{0,4},{1,3},{2,6},{3,1},{4,0},{5,7},{6,2},{7,5},{8,12},{9,11},{10,... | collective-permute-start | bytes 688136 | tf_op jit(solution)/shard_map/ppermute | solution.py:317
  57.6 4.6 %collective-permute-done.15 = bf16[896,128]{1,0:T(8,128)(2,1)S(1)} collective-permute-done((bf16[896,128]{1,0:T(8,128)(2,1)S(1)}, bf16[896,128]{1,0:T(8,128)(2,1)S(1)}, u32[]{:S(2)}, u32[]{:S(2)}) %collective-permute-start.15) | collective-permute-done | bytes 229408 | tf_op jit(solution)/shard_map/ppermute | solution.py:317
  62.2 1.0 %collective-permute-start.16 = (bf16[896,128]{1,0:T(8,128)(2,1)S(1)}, bf16[896,128]{1,0:T(8,128)(2,1)S(1)}, u32[]{:S(2)}, u32[]{:S(2)}) collective-permute-start(bf16[896,128]{1,0:T(8,128)(2,1)S(1)} %add_convert_fusion.1.own_a), channel_id=1, source_target_pairs={{0,4},{1,3},{2,6},{3,1},{4,0},{5,7},{6,2},{7,5},{8,12},{9,11},{10,... | collective-permute-start | bytes 688136 | tf_op jit(solution)/shard_map/ppermute | solution.py:317
  63.2 3.2 %collective-permute-start.21 = (bf16[896,128]{1,0:T(8,128)(2,1)S(1)}, bf16[896,128]{1,0:T(8,128)(2,1)S(1)}, u32[]{:S(2)}, u32[]{:S(2)}) collective-permute-start(bf16[896,128]{1,0:T(8,128)(2,1)S(1)} %add_convert_fusion.own_a), channel_id=1, source_target_pairs={{0,1},{1,0},{2,3},{3,2},{4,5},{5,4},{6,7},{7,6},{8,9},{9,8},{10,11... | collective-permute-start | bytes 688136 | tf_op jit(solution)/shard_map/ppermute | solution.py:312
  66.4 0.5 collective-permute-start.17
  67.1 3.5 %collective-permute-start.18 = (bf16[896,128]{1,0:T(8,128)(2,1)S(1)}, bf16[896,128]{1,0:T(8,128)(2,1)S(1)}, u32[]{:S(2)}, u32[]{:S(2)}) collective-permute-start(bf16[896,128]{1,0:T(8,128)(2,1)S(1)} %collective-permute-done.16.own_b), channel_id=1, source_target_pairs={{0,1},{1,0},{2,3},{3,2},{4,5},{5,4},{6,7},{7,6},{8,9},{9,8},{10,11... | collective-permute-start | bytes 688136 | tf_op jit(solution)/shard_map/ppermute | solution.py:312
  70.6 1.6 %shard_map.64 = (f32[2,1,1728,128]{3,2,1,0:T(8,128)}, f32[2,1,64,128]{3,2,1,0:T(8,128)}) custom-call(s32[3]{0:T(128)S(1)} %pad_add_fusion.me_ref, bf16[896,128]{1,0:T(8,128)(2,1)S(1)} %add_convert_fusion.own_a, bf16[896,128]{1,0:T(8,128)(2,1)S(1)} %collective-permute-done.20.own_b, bf16[896,128]{1,0:T(8,128)(2,1)S(1)} %collective-permute-done.21.far_a, ...), custom_call_target="tpu_custom_call" | custom-call | flops 6553600 | bytes 65536 | tf_op jit(solution)/shard_map/pallas_call | solution.py:298
  72.3 1.7 %shard_map.65 = (f32[2,1,1728,128]{3,2,1,0:T(8,128)}, f32[2,1,64,128]{3,2,1,0:T(8,128)}) custom-call(s32[3]{0:T(128)S(1)} %pad_add_fusion.me_ref, bf16[896,128]{1,0:T(8,128)(2,1)S(1)} %add_convert_fusion.1.own_a, bf16[896,128]{1,0:T(8,128)(2,1)S(1)} %collective-permute-done.16.own_b, ...), custom_call_target="tpu_custom_call", output_to_operand_aliasing={{0}: (5, {}), {1}: (6, {})} | custom-call | flops 6553600 | bytes 65536 | tf_op jit(solution)/shard_map/pallas_call | solution.py:298
  (42 shorter events, 0.9 us)
Async XLA Ops:
  0.6 6.9 %copy-start.2 = (bf16[4,64,1,2,128]{4,3,2,1,0:T(2,128)(2,1)S(1)}, bf16[4,64,1,2,128]{4,3,2,1,0:T(2,128)(2,1)}, u32[]{:S(2)}) copy-start(bf16[4,64,1,2,128]{4,3,2,1,0:T(2,128)(2,1)} %param.4) | copy-start | bytes 393220
  0.6 6.8 %copy-start.3 = (bf16[4,64,1,2,128]{4,3,2,1,0:T(2,128)(2,1)S(1)}, bf16[4,64,1,2,128]{4,3,2,1,0:T(2,128)(2,1)}, u32[]{:S(2)}) copy-start(bf16[4,64,1,2,128]{4,3,2,1,0:T(2,128)(2,1)} %param.5) | copy-start | bytes 393220
  2.1 29.0 %copy-start = (bf16[2,1,128,1728]{2,3,1,0:T(8,128)(2,1)S(1)}, bf16[2,1,128,1728]{2,3,1,0:T(8,128)(2,1)}, u32[]{:S(2)}) copy-start(bf16[2,1,128,1728]{2,3,1,0:T(8,128)(2,1)} %param.6) | copy-start | bytes 2654212
  2.1 29.0 %copy-start.1 = (bf16[2,1,64,128]{3,2,1,0:T(8,128)(2,1)S(1)}, bf16[2,1,64,128]{3,2,1,0:T(8,128)(2,1)}, u32[]{:S(2)}) copy-start(bf16[2,1,64,128]{3,2,1,0:T(8,128)(2,1)} %mix.3) | copy-start | bytes 98308
  2.1 9.8 %collective-permute-start = (bf16[896,128]{1,0:T(8,128)(2,1)S(1)}, bf16[896,128]{1,0:T(8,128)(2,1)S(1)}, u32[]{:S(2)}, u32[]{:S(2)}) collective-permute-start(bf16[896,128]{1,0:T(8,128)(2,1)S(1)} %get-tuple-element.57), channel_id=1, source_target_pairs={{0,8},{1,25},{2,10},{3,27},{4,12},{5,29},{6,14},{7,31},{8,16},{9,1... | collective-permute-start | bytes 688136 | tf_op jit(solution)/shard_map/ppermute | solution.py:348
  6.3 1.2 %collective-permute-start.2 = (bf16[16,128]{1,0:T(8,128)(2,1)S(1)}, bf16[16,128]{1,0:T(8,128)(2,1)S(1)}, u32[]{:S(2)}, u32[]{:S(2)}) collective-permute-start(bf16[16,128]{1,0:T(8,128)(2,1)S(1)} %slice_bitcast_fusion.2), channel_id=1, source_target_pairs={{0,1},{1,0},{2,3},{3,2},{4,5},{5,4},{6,7},{7,6},{8,9},{9,8},{10,11... | collective-permute-start | bytes 12296 | tf_op jit(solution)/shard_map/ppermute | solution.py:312
  8.3 3.6 %collective-permute-start.3 = (bf16[512,128]{1,0:T(8,128)(2,1)S(1)}, bf16[512,128]{1,0:T(8,128)(2,1)S(1)}, u32[]{:S(2)}, u32[]{:S(2)}) collective-permute-start(bf16[512,128]{1,0:T(8,128)(2,1)S(1)} %get-tuple-element.29), channel_id=1, source_target_pairs={{0,1},{1,0},{2,3},{3,2},{4,5},{5,4},{6,7},{7,6},{8,9},{9,8},{10,11... | collective-permute-start | bytes 393224 | tf_op jit(solution)/shard_map/ppermute | solution.py:312
  8.6 9.0 %collective-permute-start.1 = (bf16[448,128]{1,0:T(8,128)(2,1)S(1)}, bf16[448,128]{1,0:T(8,128)(2,1)S(1)}, u32[]{:S(2)}, u32[]{:S(2)}) collective-permute-start(bf16[448,128]{1,0:T(8,128)(2,1)S(1)} %get-tuple-element.55), channel_id=1, source_target_pairs={{0,16},{8,24},{16,0},{24,8},{1,17},{9,25},{17,1},{25,9},{2,18},{10... | collective-permute-start | bytes 344072 | tf_op jit(solution)/shard_map/ppermute | solution.py:349
  9.7 7.9 %collective-permute-start.4 = (bf16[256,128]{1,0:T(8,128)(2,1)S(1)}, bf16[256,128]{1,0:T(8,128)(2,1)S(1)}, u32[]{:S(2)}, u32[]{:S(2)}) collective-permute-start(bf16[256,128]{1,0:T(8,128)(2,1)S(1)} %get-tuple-element.30), channel_id=1, source_target_pairs={{0,6},{1,7},{2,4},{3,5},{4,2},{5,3},{6,0},{7,1},{8,14},{9,15},{10,... | collective-permute-start | bytes 196616 | tf_op jit(solution)/shard_map/ppermute | solution.py:312
  11.9 8.5 %collective-permute-start.6 = (bf16[896,128]{1,0:T(8,128)(2,1)S(1)}, bf16[896,128]{1,0:T(8,128)(2,1)S(1)}, u32[]{:S(2)}, u32[]{:S(2)}) collective-permute-start(bf16[896,128]{1,0:T(8,128)(2,1)S(1)} %get-tuple-element.32), channel_id=1, source_target_pairs={{0,8},{1,25},{2,10},{3,27},{4,12},{5,29},{6,14},{7,31},{8,16},{9,1... | collective-permute-start | bytes 688136 | tf_op jit(solution)/shard_map/ppermute | solution.py:348
  14.6 12.5 %collective-permute-start.7 = (bf16[448,128]{1,0:T(8,128)(2,1)S(1)}, bf16[448,128]{1,0:T(8,128)(2,1)S(1)}, u32[]{:S(2)}, u32[]{:S(2)}) collective-permute-start(bf16[448,128]{1,0:T(8,128)(2,1)S(1)} %get-tuple-element.33), channel_id=1, source_target_pairs={{0,16},{8,24},{16,0},{24,8},{1,17},{9,25},{17,1},{25,9},{2,18},{10... | collective-permute-start | bytes 344072 | tf_op jit(solution)/shard_map/ppermute | solution.py:349
  17.6 11.3 %collective-permute-start.5 = (bf16[1856,128]{1,0:T(8,128)(2,1)S(1)}, bf16[1856,128]{1,0:T(8,128)(2,1)S(1)}, u32[]{:S(2)}, u32[]{:S(2)}) collective-permute-start(bf16[1856,128]{1,0:T(8,128)(2,1)S(1)} %pad_maximum_fusion.refs_0_), channel_id=1, source_target_pairs={{0,2},{1,5},{2,0},{3,7},{4,6},{5,1},{6,4},{7,3},{8,10},{9,13},{10,... | collective-permute-start | bytes 1425416 | tf_op jit(solution)/shard_map/ppermute | solution.py:317
  27.2 1.8 %collective-permute-start.9 = (bf16[1344,128]{1,0:T(8,128)(2,1)S(1)}, bf16[1344,128]{1,0:T(8,128)(2,1)S(1)}, u32[]{:S(2)}, u32[]{:S(2)}) collective-permute-start(bf16[1344,128]{1,0:T(8,128)(2,1)S(1)} %constant_dynamic-update-slice_fusion.refs_1_), channel_id=1, source_target_pairs={{0,1},{1,0},{2,3},{3,2},{4,5},{5,4},{6,7},{7,6},{8,9},{9,8},{10,11... | collective-permute-start | bytes 1032200 | tf_op jit(solution)/shard_map/ppermute | solution.py:312
  27.2 3.8 %collective-permute-start.10 = (bf16[1856,128]{1,0:T(8,128)(2,1)S(1)}, bf16[1856,128]{1,0:T(8,128)(2,1)S(1)}, u32[]{:S(2)}, u32[]{:S(2)}) collective-permute-start(bf16[1856,128]{1,0:T(8,128)(2,1)S(1)} %pad_maximum_fusion.refs_0_), channel_id=1, source_target_pairs={{0,1},{1,0},{2,3},{3,2},{4,5},{5,4},{6,7},{7,6},{8,9},{9,8},{10,11... | collective-permute-start | bytes 1425416 | tf_op jit(solution)/shard_map/ppermute | solution.py:312
  27.7 8.2 %collective-permute-start.8 = (bf16[1344,128]{1,0:T(8,128)(2,1)S(1)}, bf16[1344,128]{1,0:T(8,128)(2,1)S(1)}, u32[]{:S(2)}, u32[]{:S(2)}) collective-permute-start(bf16[1344,128]{1,0:T(8,128)(2,1)S(1)} %constant_dynamic-update-slice_fusion.refs_1_), channel_id=1, source_target_pairs={{0,2},{1,5},{2,0},{3,7},{4,6},{5,1},{6,4},{7,3},{8,10},{9,13},{10,... | collective-permute-start | bytes 1032200 | tf_op jit(solution)/shard_map/ppermute | solution.py:317
  29.0 2.1 %collective-permute-start.13 = (bf16[960,128]{1,0:T(8,128)(2,1)S(1)}, bf16[960,128]{1,0:T(8,128)(2,1)S(1)}, u32[]{:S(2)}, u32[]{:S(2)}) collective-permute-start(bf16[960,128]{1,0:T(8,128)(2,1)S(1)} %slice.39), channel_id=1, source_target_pairs={{0,1},{1,0},{2,3},{3,2},{4,5},{5,4},{6,7},{7,6},{8,9},{9,8},{10,11... | collective-permute-start | bytes 737288 | tf_op jit(solution)/shard_map/ppermute | solution.py:312
  29.4 1.7 %collective-permute-start.11 = (bf16[896,128]{1,0:T(8,128)(2,1)S(1)}, bf16[896,128]{1,0:T(8,128)(2,1)S(1)}, u32[]{:S(2)}, u32[]{:S(2)}) collective-permute-start(bf16[896,128]{1,0:T(8,128)(2,1)S(1)} %slice.38), channel_id=1, source_target_pairs={{0,1},{1,0},{2,3},{3,2},{4,5},{5,4},{6,7},{7,6},{8,9},{9,8},{10,11... | collective-permute-start | bytes 688136 | tf_op jit(solution)/shard_map/ppermute | solution.py:312
  29.7 1.4 %collective-permute-start.12 = (bf16[256,128]{1,0:T(8,128)(2,1)S(1)}, bf16[256,128]{1,0:T(8,128)(2,1)S(1)}, u32[]{:S(2)}, u32[]{:S(2)}) collective-permute-start(bf16[256,128]{1,0:T(8,128)(2,1)S(1)} %collective-permute-done.4.refs_6_.refs_7_), channel_id=1, source_target_pairs={{0,1},{1,0},{2,3},{3,2},{4,5},{5,4},{6,7},{7,6},{8,9},{9,8},{10,11... | collective-permute-start | bytes 196616 | tf_op jit(solution)/shard_map/ppermute | solution.py:312
  36.0 2.1 %collective-permute-start.14 = (bf16[1344,128]{1,0:T(8,128)(2,1)S(1)}, bf16[1344,128]{1,0:T(8,128)(2,1)S(1)}, u32[]{:S(2)}, u32[]{:S(2)}) collective-permute-start(bf16[1344,128]{1,0:T(8,128)(2,1)S(1)} %collective-permute-done.8.refs_2_), channel_id=1, source_target_pairs={{0,1},{1,0},{2,3},{3,2},{4,5},{5,4},{6,7},{7,6},{8,9},{9,8},{10,11... | collective-permute-start | bytes 1032200 | tf_op jit(solution)/shard_map/ppermute | solution.py:312
  49.6 6.7 %collective-permute-start.19 = (bf16[896,128]{1,0:T(8,128)(2,1)S(1)}, bf16[896,128]{1,0:T(8,128)(2,1)S(1)}, u32[]{:S(2)}, u32[]{:S(2)}) collective-permute-start(bf16[896,128]{1,0:T(8,128)(2,1)S(1)} %get-tuple-element.48), channel_id=1, source_target_pairs={{0,2},{1,5},{2,0},{3,7},{4,6},{5,1},{6,4},{7,3},{8,10},{9,13},{10,... | collective-permute-start | bytes 688136 | tf_op jit(solution)/shard_map/ppermute | solution.py:317
  56.0 6.1 %collective-permute-start.15 = (bf16[896,128]{1,0:T(8,128)(2,1)S(1)}, bf16[896,128]{1,0:T(8,128)(2,1)S(1)}, u32[]{:S(2)}, u32[]{:S(2)}) collective-permute-start(bf16[896,128]{1,0:T(8,128)(2,1)S(1)} %shard_map.63), channel_id=1, source_target_pairs={{0,2},{1,5},{2,0},{3,7},{4,6},{5,1},{6,4},{7,3},{8,10},{9,13},{10,... | collective-permute-start | bytes 688136 | tf_op jit(solution)/shard_map/ppermute | solution.py:317
  56.3 10.0 %collective-permute-start.20 = (bf16[896,128]{1,0:T(8,128)(2,1)S(1)}, bf16[896,128]{1,0:T(8,128)(2,1)S(1)}, u32[]{:S(2)}, u32[]{:S(2)}) collective-permute-start(bf16[896,128]{1,0:T(8,128)(2,1)S(1)} %add_convert_fusion.own_a), channel_id=1, source_target_pairs={{0,4},{1,3},{2,6},{3,1},{4,0},{5,7},{6,2},{7,5},{8,12},{9,11},{10,... | collective-permute-start | bytes 688136 | tf_op jit(solution)/shard_map/ppermute | solution.py:317
  62.2 4.9 %collective-permute-start.16 = (bf16[896,128]{1,0:T(8,128)(2,1)S(1)}, bf16[896,128]{1,0:T(8,128)(2,1)S(1)}, u32[]{:S(2)}, u32[]{:S(2)}) collective-permute-start(bf16[896,128]{1,0:T(8,128)(2,1)S(1)} %add_convert_fusion.1.own_a), channel_id=1, source_target_pairs={{0,4},{1,3},{2,6},{3,1},{4,0},{5,7},{6,2},{7,5},{8,12},{9,11},{10,... | collective-permute-start | bytes 688136 | tf_op jit(solution)/shard_map/ppermute | solution.py:317
  63.2 7.4 %collective-permute-start.21 = (bf16[896,128]{1,0:T(8,128)(2,1)S(1)}, bf16[896,128]{1,0:T(8,128)(2,1)S(1)}, u32[]{:S(2)}, u32[]{:S(2)}) collective-permute-start(bf16[896,128]{1,0:T(8,128)(2,1)S(1)} %add_convert_fusion.own_a), channel_id=1, source_target_pairs={{0,1},{1,0},{2,3},{3,2},{4,5},{5,4},{6,7},{7,6},{8,9},{9,8},{10,11... | collective-permute-start | bytes 688136 | tf_op jit(solution)/shard_map/ppermute | solution.py:312
  66.4 4.2 %collective-permute-start.22 = (bf16[896,128]{1,0:T(8,128)(2,1)S(1)}, bf16[896,128]{1,0:T(8,128)(2,1)S(1)}, u32[]{:S(2)}, u32[]{:S(2)}) collective-permute-start(bf16[896,128]{1,0:T(8,128)(2,1)S(1)} %collective-permute-done.20.own_b), channel_id=1, source_target_pairs={{0,1},{1,0},{2,3},{3,2},{4,5},{5,4},{6,7},{7,6},{8,9},{9,8},{10,11... | collective-permute-start | bytes 688136 | tf_op jit(solution)/shard_map/ppermute | solution.py:312
  66.4 5.9 %collective-permute-start.17 = (bf16[896,128]{1,0:T(8,128)(2,1)S(1)}, bf16[896,128]{1,0:T(8,128)(2,1)S(1)}, u32[]{:S(2)}, u32[]{:S(2)}) collective-permute-start(bf16[896,128]{1,0:T(8,128)(2,1)S(1)} %add_convert_fusion.1.own_a), channel_id=1, source_target_pairs={{0,1},{1,0},{2,3},{3,2},{4,5},{5,4},{6,7},{7,6},{8,9},{9,8},{10,11... | collective-permute-start | bytes 688136 | tf_op jit(solution)/shard_map/ppermute | solution.py:312
  67.1 5.2 %collective-permute-start.18 = (bf16[896,128]{1,0:T(8,128)(2,1)S(1)}, bf16[896,128]{1,0:T(8,128)(2,1)S(1)}, u32[]{:S(2)}, u32[]{:S(2)}) collective-permute-start(bf16[896,128]{1,0:T(8,128)(2,1)S(1)} %collective-permute-done.16.own_b), channel_id=1, source_target_pairs={{0,1},{1,0},{2,3},{3,2},{4,5},{5,4},{6,7},{7,6},{8,9},{9,8},{10,11... | collective-permute-start | bytes 688136 | tf_op jit(solution)/shard_map/ppermute | solution.py:312

commit v7 on v6

--- a/solution.py
+++ b/solution.py
@@ -51,7 +51,7 @@
     return jnp.concatenate(parts, axis=2).reshape(planes * padded.shape[1], 3 * padded.shape[2])
 
 
-def forward_layer(layer, slot, act, folded, slope, keep_a, keep_h):
+def forward_layer(layer, slot, act, folded, slope, keep_a, keep_h, mix_if=None):
     padded = keep_a.at[slot]
     planes = padded.shape[0] - 2
     length = padded.shape[1]
@@ -63,8 +63,15 @@
     wide = pre * gate
     hidden = wide.astype(BF)
     slope[layer] = (gate + wide * (1.0 - gate)).astype(slope.dtype)
-    act[...] = now + dot(hidden, folded[layer, 1152:], NT)
     keep_h[slot] = hidden
+
+    def mix():
+        act[...] = now + dot(hidden, folded[layer, 1152:], NT)
+
+    if mix_if is None:
+        mix()
+    else:
+        pl.when(mix_if)(mix)
 
 
 def term_rows(blocks, base, conv, mix, terms):
@@ -242,7 +249,7 @@
     clear_edges(wide)
 
     def step(layer, carry):
-        forward_layer(layer, jnp.where(layer == section, 0, 1), act, folded, slope, keep_a, keep_h)
+        forward_layer(layer, jnp.where(layer == section, 0, 1), act, folded, slope, keep_a, keep_h, layer < folded.shape[0] - 1)
         return carry
 
     lax.fori_loop(0, folded.shape[0], step, 0)

time: 74.2 us -> 74.1 us (level)
  no operation moved by 1% of the time
where the time goes in v7:
time: 74.1 us; the launch traced here: 73.9 us
  Pallas kernels  27.2 us (37%)
  starting transfers between devices  25.8 us (35%)
  waiting for transfers between devices  18.2 us (25%)
  other arithmetic  1.58 us (2%)
  between operations  1.05 us (1%)
    pallas_call x7, Pallas kernels, call(): pl.pallas_call(kernel, out_shape=outs, in_specs=specs, out_specs=[far if...  27.2 us
    ppermute x13, starting transfers between devices, exchange(): return lax.ppermute(block, 'space', [(i, i ^ mask) for i in range(count)])  11.5 us
    ppermute x2, waiting for transfers between devices, gather_paired(): lax.ppermute(after(part[group], *near[:group]), 'section', across)  9.72 us
    ppermute x2, starting transfers between devices, gather_paired(): lax.ppermute(after(mine[group], *near), ('section', 'space'), route)  6.94 us
    ppermute x6, starting transfers between devices, cross(): lax.ppermute(block, 'space', [(i, i ^ (second if i % 2 else first)) for i...  6.27 us
    ppermute x6, waiting for transfers between devices, cross(): lax.ppermute(block, 'space', [(i, i ^ (second if i % 2 else first)) for i...  4.83 us
    ppermute x13, waiting for transfers between devices, exchange(): return lax.ppermute(block, 'space', [(i, i ^ mask) for i in range(count)])  2.19 us
  transfers between devices with their start and end apart: 23, of which 7 were waited for; matrix products, arithmetic and copies ran while one was open for 0% of the time, Pallas kernels for 19%

profile of v7, /device:TPU:1, one launch (start us, length us, event | category | flops | bytes accessed | tf_op | source)
XLA Modules:
  0.0 73.9 jit_solution(13484204826133327885)
XLA Ops:
  0.7 1.3 %fusion = bf16[2,896,128]{2,1,0:T(8,128)(2,1)S(1)} fusion(bf16[2,64,128]{2,1,0:T(8,128)(2,1)} %bitcast.27, bf16[2,1728,128]{2,1,0:T(8,128)(2,1)} %bitcast.24, pred[]{:T(512)S(6)} %eq.7), kind=kLoop, calls=%fused_computation.2 | loop fusion | flops 1146880 | bytes 1835009 | tf_op jit(solution)/shard_map/jit(_where)/select_n | solution.py:337
  2.1 4.2 %collective-permute-start = (bf16[896,128]{1,0:T(8,128)(2,1)S(1)}, bf16[896,128]{1,0:T(8,128)(2,1)S(1)}, u32[]{:S(2)}, u32[]{:S(2)}) collective-permute-start(bf16[896,128]{1,0:T(8,128)(2,1)S(1)} %get-tuple-element.57), channel_id=1, source_target_pairs={{0,8},{1,25},{2,10},{3,27},{4,12},{5,29},{6,14},{7,31},{8,16},{9,1... | collective-permute-start | bytes 688136 | tf_op jit(solution)/shard_map/ppermute | solution.py:355
  6.4 1.1 %collective-permute-done.2.token = bf16[16,128]{1,0:T(8,128)(2,1)S(1)} collective-permute-done((bf16[16,128]{1,0:T(8,128)(2,1)S(1)}, bf16[16,128]{1,0:T(8,128)(2,1)S(1)}, u32[]{:S(2)}, u32[]{:S(2)}) %collective-permute-start.2) | collective-permute-done | bytes 4128 | tf_op jit(solution)/shard_map/ppermute | solution.py:319
  7.5 0.8 %shard_map.59 = (bf16[256,128]{1,0:T(8,128)(2,1)S(1)}, bf16[256,128]{1,0:T(8,128)(2,1)S(1)}, bf16[256,128]{1,0:T(8,128)(2,1)S(1)}, bf16[512,128]{1,0:T(8,128)(2,1)S(1)}) custom-call(s32[3]{0:T(128)S(1)} %pad_add_fusion.me_ref, bf16[4,128,128]{2,1,0:T(8,128)(2,1)S(1)} %bitcast.28, bf16[4,128,128]{2,1,0:T(8,128)(2,1)S(1)} %bitcast.29, ...), custom_call_target="tpu_custom_call" | custom-call | flops 104857600 | bytes 1048576 | tf_op jit(solution)/shard_map/pallas_call | solution.py:305
  8.6 1.1 %collective-permute-start.1 = (bf16[448,128]{1,0:T(8,128)(2,1)S(1)}, bf16[448,128]{1,0:T(8,128)(2,1)S(1)}, u32[]{:S(2)}, u32[]{:S(2)}) collective-permute-start(bf16[448,128]{1,0:T(8,128)(2,1)S(1)} %get-tuple-element.55), channel_id=1, source_target_pairs={{0,16},{8,24},{16,0},{24,8},{1,17},{9,25},{17,1},{25,9},{2,18},{10... | collective-permute-start | bytes 344072 | tf_op jit(solution)/shard_map/ppermute | solution.py:356
  9.7 2.2 %collective-permute-start.4 = (bf16[256,128]{1,0:T(8,128)(2,1)S(1)}, bf16[256,128]{1,0:T(8,128)(2,1)S(1)}, u32[]{:S(2)}, u32[]{:S(2)}) collective-permute-start(bf16[256,128]{1,0:T(8,128)(2,1)S(1)} %get-tuple-element.30), channel_id=1, source_target_pairs={{0,6},{1,7},{2,4},{3,5},{4,2},{5,3},{6,0},{7,1},{8,14},{9,15},{10,... | collective-permute-start | bytes 196616 | tf_op jit(solution)/shard_map/ppermute | solution.py:319
  11.9 2.7 %collective-permute-start.6 = (bf16[896,128]{1,0:T(8,128)(2,1)S(1)}, bf16[896,128]{1,0:T(8,128)(2,1)S(1)}, u32[]{:S(2)}, u32[]{:S(2)}) collective-permute-start(bf16[896,128]{1,0:T(8,128)(2,1)S(1)} %get-tuple-element.32), channel_id=1, source_target_pairs={{0,8},{1,25},{2,10},{3,27},{4,12},{5,29},{6,14},{7,31},{8,16},{9,1... | collective-permute-start | bytes 688136 | tf_op jit(solution)/shard_map/ppermute | solution.py:355
  14.6 3.0 %collective-permute-done.1 = bf16[448,128]{1,0:T(8,128)(2,1)S(1)} collective-permute-done((bf16[448,128]{1,0:T(8,128)(2,1)S(1)}, bf16[448,128]{1,0:T(8,128)(2,1)S(1)}, u32[]{:S(2)}, u32[]{:S(2)}) %collective-permute-start.1) | collective-permute-done | bytes 114720 | tf_op jit(solution)/shard_map/ppermute | solution.py:356
  17.6 1.3 %collective-permute-start.5 = (bf16[1856,128]{1,0:T(8,128)(2,1)S(1)}, bf16[1856,128]{1,0:T(8,128)(2,1)S(1)}, u32[]{:S(2)}, u32[]{:S(2)}) collective-permute-start(bf16[1856,128]{1,0:T(8,128)(2,1)S(1)} %pad_maximum_fusion.refs_0_), channel_id=1, source_target_pairs={{0,2},{1,5},{2,0},{3,7},{4,6},{5,1},{6,4},{7,3},{8,10},{9,13},{10,... | collective-permute-start | bytes 1425416 | tf_op jit(solution)/shard_map/ppermute | solution.py:324
  18.9 1.4 %collective-permute-done.6 = bf16[896,128]{1,0:T(8,128)(2,1)S(1)} collective-permute-done((bf16[896,128]{1,0:T(8,128)(2,1)S(1)}, bf16[896,128]{1,0:T(8,128)(2,1)S(1)}, u32[]{:S(2)}, u32[]{:S(2)}) %collective-permute-start.6) | collective-permute-done | bytes 229408 | tf_op jit(solution)/shard_map/ppermute | solution.py:355
  20.4 6.7 %collective-permute-done.7 = bf16[448,128]{1,0:T(8,128)(2,1)S(1)} collective-permute-done((bf16[448,128]{1,0:T(8,128)(2,1)S(1)}, bf16[448,128]{1,0:T(8,128)(2,1)S(1)}, u32[]{:S(2)}, u32[]{:S(2)}) %collective-permute-start.7) | collective-permute-done | bytes 114720 | tf_op jit(solution)/shard_map/ppermute | solution.py:356
  27.2 0.5 collective-permute-start.10
  27.7 1.2 %collective-permute-start.8 = (bf16[1344,128]{1,0:T(8,128)(2,1)S(1)}, bf16[1344,128]{1,0:T(8,128)(2,1)S(1)}, u32[]{:S(2)}, u32[]{:S(2)}) collective-permute-start(bf16[1344,128]{1,0:T(8,128)(2,1)S(1)} %constant_dynamic-update-slice_fusion.refs_1_), channel_id=1, source_target_pairs={{0,2},{1,5},{2,0},{3,7},{4,6},{5,1},{6,4},{7,3},{8,10},{9,13},{10,... | collective-permute-start | bytes 1032200 | tf_op jit(solution)/shard_map/ppermute | solution.py:324
  29.0 0.4 collective-permute-start.13
  29.4 0.2 collective-permute-start.11
  29.7 0.3 collective-permute-start.12
  30.0 1.1 %collective-permute-done.12.refs_7_.refs_8_ = bf16[256,128]{1,0:T(8,128)(2,1)S(1)} collective-permute-done((bf16[256,128]{1,0:T(8,128)(2,1)S(1)}, bf16[256,128]{1,0:T(8,128)(2,1)S(1)}, u32[]{:S(2)}, u32[]{:S(2)}) %collective-permute-start.12) | collective-permute-done | bytes 65568 | tf_op jit(solution)/shard_map/ppermute | solution.py:319
  31.1 4.9 %shard_map.60 = (f32[1024,128]{1,0:T(8,128)S(1)}, bf16[4,1280,256]{2,1,0:T(8,128)(2,1)S(1)}, bf16[4,1024,256]{2,1,0:T(8,128)(2,1)S(1)}, bf16[2,10,128,384]{3,2,1...) custom-call(s32[3]{0:T(128)S(1)} %pad_add_fusion.me_ref, ...), custom_call_target="tpu_custom_call" | custom-call | flops 209715200 | bytes 2097152 | tf_op jit(solution)/shard_map/pallas_call | solution.py:305
  36.0 0.3 collective-permute-start.14
  36.3 1.8 %shard_map.61 = (f32[1024,128]{1,0:T(8,128)S(1)}, bf16[4,1024,256]{2,1,0:T(8,128)(2,1)S(1)}, bf16[2,10,128,384]{3,2,1,0:T(8,128)(2,1)S(1)}, bf16[2,1024,256]{2,1,0:T(8,128)(2,1)S(1)}) custom-call(s32[3]{0:T(128)S(1)} %pad_add_fusion.me_ref, ...), custom_call_target="tpu_custom_call", output_to_operand_aliasing={{0}: (3, {}), {1}: (4, {}), {2}: (5, {}), {3}: (6, {})} | custom-call | flops 209715200 | bytes 2097152 | tf_op jit(solution)/shard_map/pallas_call | solution.py:305
  38.1 11.4 %shard_map.62 = (f32[1024,128]{1,0:T(8,128)S(1)}, bf16[896,128]{1,0:T(8,128)(2,1)S(1)}) custom-call(s32[3]{0:T(128)S(1)} %pad_add_fusion.me_ref, bf16[2,1,1728,128]{3,2,1,0:T(8,128)(2,1)S(1)} %bitcast.26, bf16[2,1,64,128]{3,2,1,0:T(8,128)(2,1)S(1)} %copy-done.1, bf16[1856,128]{1,0:T(8,128)(2,1)S(1)} %collective-permute-done.5.refs_1_.refs_0_, ...), custom_call_target="tpu_custom_call" | custom-call | flops 4194304000 | bytes 41943040 | tf_op jit(solution)/shard_map/pallas_call | solution.py:305
  49.5 1.3 %collective-permute-start.19 = (bf16[896,128]{1,0:T(8,128)(2,1)S(1)}, bf16[896,128]{1,0:T(8,128)(2,1)S(1)}, u32[]{:S(2)}, u32[]{:S(2)}) collective-permute-start(bf16[896,128]{1,0:T(8,128)(2,1)S(1)} %get-tuple-element.48), channel_id=1, source_target_pairs={{0,2},{1,5},{2,0},{3,7},{4,6},{5,1},{6,4},{7,3},{8,10},{9,13},{10,... | collective-permute-start | bytes 688136 | tf_op jit(solution)/shard_map/ppermute | solution.py:324
  50.8 5.0 %shard_map.63 = bf16[896,128]{1,0:T(8,128)(2,1)S(1)} custom-call(s32[3]{0:T(128)S(1)} %pad_add_fusion.me_ref, f32[1024,128]{1,0:T(8,128)S(1)} %get-tuple-element.44.up_in, bf16[4,1280,256]{2,1,0:T(8,128)(2,1)S(1)} %get-tuple-element.38.folded, bf16[4,1024,256]{2,1,0:T(8,128)(2,1)S(1)} %get-tuple-element.45.slope, ...), custom_call_target="tpu_custom_call" | custom-call | flops 2097152000 | bytes 20971520 | tf_op jit(solution)/shard_map/pallas_call | solution.py:305
  55.9 0.3 collective-permute-start.15
  56.2 1.2 %collective-permute-start.20 = (bf16[896,128]{1,0:T(8,128)(2,1)S(1)}, bf16[896,128]{1,0:T(8,128)(2,1)S(1)}, u32[]{:S(2)}, u32[]{:S(2)}) collective-permute-start(bf16[896,128]{1,0:T(8,128)(2,1)S(1)} %add_convert_fusion.own_a), channel_id=1, source_target_pairs={{0,4},{1,3},{2,6},{3,1},{4,0},{5,7},{6,2},{7,5},{8,12},{9,11},{10,... | collective-permute-start | bytes 688136 | tf_op jit(solution)/shard_map/ppermute | solution.py:324
  57.4 4.6 %collective-permute-done.15 = bf16[896,128]{1,0:T(8,128)(2,1)S(1)} collective-permute-done((bf16[896,128]{1,0:T(8,128)(2,1)S(1)}, bf16[896,128]{1,0:T(8,128)(2,1)S(1)}, u32[]{:S(2)}, u32[]{:S(2)}) %collective-permute-start.15) | collective-permute-done | bytes 229408 | tf_op jit(solution)/shard_map/ppermute | solution.py:324
  62.1 0.9 %collective-permute-start.16 = (bf16[896,128]{1,0:T(8,128)(2,1)S(1)}, bf16[896,128]{1,0:T(8,128)(2,1)S(1)}, u32[]{:S(2)}, u32[]{:S(2)}) collective-permute-start(bf16[896,128]{1,0:T(8,128)(2,1)S(1)} %add_convert_fusion.1.own_a), channel_id=1, source_target_pairs={{0,4},{1,3},{2,6},{3,1},{4,0},{5,7},{6,2},{7,5},{8,12},{9,11},{10,... | collective-permute-start | bytes 688136 | tf_op jit(solution)/shard_map/ppermute | solution.py:324
  63.0 3.3 %collective-permute-start.21 = (bf16[896,128]{1,0:T(8,128)(2,1)S(1)}, bf16[896,128]{1,0:T(8,128)(2,1)S(1)}, u32[]{:S(2)}, u32[]{:S(2)}) collective-permute-start(bf16[896,128]{1,0:T(8,128)(2,1)S(1)} %add_convert_fusion.own_a), channel_id=1, source_target_pairs={{0,1},{1,0},{2,3},{3,2},{4,5},{5,4},{6,7},{7,6},{8,9},{9,8},{10,11... | collective-permute-start | bytes 688136 | tf_op jit(solution)/shard_map/ppermute | solution.py:319
  66.3 0.5 collective-permute-start.17
  67.0 3.4 %collective-permute-start.18 = (bf16[896,128]{1,0:T(8,128)(2,1)S(1)}, bf16[896,128]{1,0:T(8,128)(2,1)S(1)}, u32[]{:S(2)}, u32[]{:S(2)}) collective-permute-start(bf16[896,128]{1,0:T(8,128)(2,1)S(1)} %collective-permute-done.16.own_b), channel_id=1, source_target_pairs={{0,1},{1,0},{2,3},{3,2},{4,5},{5,4},{6,7},{7,6},{8,9},{9,8},{10,11... | collective-permute-start | bytes 688136 | tf_op jit(solution)/shard_map/ppermute | solution.py:319
  70.5 1.6 %shard_map.64 = (f32[2,1,1728,128]{3,2,1,0:T(8,128)}, f32[2,1,64,128]{3,2,1,0:T(8,128)}) custom-call(s32[3]{0:T(128)S(1)} %pad_add_fusion.me_ref, bf16[896,128]{1,0:T(8,128)(2,1)S(1)} %add_convert_fusion.own_a, bf16[896,128]{1,0:T(8,128)(2,1)S(1)} %collective-permute-done.20.own_b, bf16[896,128]{1,0:T(8,128)(2,1)S(1)} %collective-permute-done.21.far_a, ...), custom_call_target="tpu_custom_call" | custom-call | flops 6553600 | bytes 65536 | tf_op jit(solution)/shard_map/pallas_call | solution.py:305
  72.1 1.7 %shard_map.65 = (f32[2,1,1728,128]{3,2,1,0:T(8,128)}, f32[2,1,64,128]{3,2,1,0:T(8,128)}) custom-call(s32[3]{0:T(128)S(1)} %pad_add_fusion.me_ref, bf16[896,128]{1,0:T(8,128)(2,1)S(1)} %add_convert_fusion.1.own_a, bf16[896,128]{1,0:T(8,128)(2,1)S(1)} %collective-permute-done.16.own_b, ...), custom_call_target="tpu_custom_call", output_to_operand_aliasing={{0}: (5, {}), {1}: (6, {})} | custom-call | flops 6553600 | bytes 65536 | tf_op jit(solution)/shard_map/pallas_call | solution.py:305
  (42 shorter events, 1.0 us)
Async XLA Ops:
  0.6 6.9 %copy-start.2 = (bf16[4,64,1,2,128]{4,3,2,1,0:T(2,128)(2,1)S(1)}, bf16[4,64,1,2,128]{4,3,2,1,0:T(2,128)(2,1)}, u32[]{:S(2)}) copy-start(bf16[4,64,1,2,128]{4,3,2,1,0:T(2,128)(2,1)} %param.4) | copy-start | bytes 393220
  0.6 6.8 %copy-start.3 = (bf16[4,64,1,2,128]{4,3,2,1,0:T(2,128)(2,1)S(1)}, bf16[4,64,1,2,128]{4,3,2,1,0:T(2,128)(2,1)}, u32[]{:S(2)}) copy-start(bf16[4,64,1,2,128]{4,3,2,1,0:T(2,128)(2,1)} %param.5) | copy-start | bytes 393220
  2.1 29.0 %copy-start = (bf16[2,1,128,1728]{2,3,1,0:T(8,128)(2,1)S(1)}, bf16[2,1,128,1728]{2,3,1,0:T(8,128)(2,1)}, u32[]{:S(2)}) copy-start(bf16[2,1,128,1728]{2,3,1,0:T(8,128)(2,1)} %param.6) | copy-start | bytes 2654212
  2.1 29.0 %copy-start.1 = (bf16[2,1,64,128]{3,2,1,0:T(8,128)(2,1)S(1)}, bf16[2,1,64,128]{3,2,1,0:T(8,128)(2,1)}, u32[]{:S(2)}) copy-start(bf16[2,1,64,128]{3,2,1,0:T(8,128)(2,1)} %mix.3) | copy-start | bytes 98308
  2.1 9.8 %collective-permute-start = (bf16[896,128]{1,0:T(8,128)(2,1)S(1)}, bf16[896,128]{1,0:T(8,128)(2,1)S(1)}, u32[]{:S(2)}, u32[]{:S(2)}) collective-permute-start(bf16[896,128]{1,0:T(8,128)(2,1)S(1)} %get-tuple-element.57), channel_id=1, source_target_pairs={{0,8},{1,25},{2,10},{3,27},{4,12},{5,29},{6,14},{7,31},{8,16},{9,1... | collective-permute-start | bytes 688136 | tf_op jit(solution)/shard_map/ppermute | solution.py:355
  6.3 1.2 %collective-permute-start.2 = (bf16[16,128]{1,0:T(8,128)(2,1)S(1)}, bf16[16,128]{1,0:T(8,128)(2,1)S(1)}, u32[]{:S(2)}, u32[]{:S(2)}) collective-permute-start(bf16[16,128]{1,0:T(8,128)(2,1)S(1)} %slice_bitcast_fusion.2), channel_id=1, source_target_pairs={{0,1},{1,0},{2,3},{3,2},{4,5},{5,4},{6,7},{7,6},{8,9},{9,8},{10,11... | collective-permute-start | bytes 12296 | tf_op jit(solution)/shard_map/ppermute | solution.py:319
  8.3 3.6 %collective-permute-start.3 = (bf16[512,128]{1,0:T(8,128)(2,1)S(1)}, bf16[512,128]{1,0:T(8,128)(2,1)S(1)}, u32[]{:S(2)}, u32[]{:S(2)}) collective-permute-start(bf16[512,128]{1,0:T(8,128)(2,1)S(1)} %get-tuple-element.29), channel_id=1, source_target_pairs={{0,1},{1,0},{2,3},{3,2},{4,5},{5,4},{6,7},{7,6},{8,9},{9,8},{10,11... | collective-permute-start | bytes 393224 | tf_op jit(solution)/shard_map/ppermute | solution.py:319
  8.6 9.0 %collective-permute-start.1 = (bf16[448,128]{1,0:T(8,128)(2,1)S(1)}, bf16[448,128]{1,0:T(8,128)(2,1)S(1)}, u32[]{:S(2)}, u32[]{:S(2)}) collective-permute-start(bf16[448,128]{1,0:T(8,128)(2,1)S(1)} %get-tuple-element.55), channel_id=1, source_target_pairs={{0,16},{8,24},{16,0},{24,8},{1,17},{9,25},{17,1},{25,9},{2,18},{10... | collective-permute-start | bytes 344072 | tf_op jit(solution)/shard_map/ppermute | solution.py:356
  9.7 7.9 %collective-permute-start.4 = (bf16[256,128]{1,0:T(8,128)(2,1)S(1)}, bf16[256,128]{1,0:T(8,128)(2,1)S(1)}, u32[]{:S(2)}, u32[]{:S(2)}) collective-permute-start(bf16[256,128]{1,0:T(8,128)(2,1)S(1)} %get-tuple-element.30), channel_id=1, source_target_pairs={{0,6},{1,7},{2,4},{3,5},{4,2},{5,3},{6,0},{7,1},{8,14},{9,15},{10,... | collective-permute-start | bytes 196616 | tf_op jit(solution)/shard_map/ppermute | solution.py:319
  11.9 8.5 %collective-permute-start.6 = (bf16[896,128]{1,0:T(8,128)(2,1)S(1)}, bf16[896,128]{1,0:T(8,128)(2,1)S(1)}, u32[]{:S(2)}, u32[]{:S(2)}) collective-permute-start(bf16[896,128]{1,0:T(8,128)(2,1)S(1)} %get-tuple-element.32), channel_id=1, source_target_pairs={{0,8},{1,25},{2,10},{3,27},{4,12},{5,29},{6,14},{7,31},{8,16},{9,1... | collective-permute-start | bytes 688136 | tf_op jit(solution)/shard_map/ppermute | solution.py:355
  14.6 12.5 %collective-permute-start.7 = (bf16[448,128]{1,0:T(8,128)(2,1)S(1)}, bf16[448,128]{1,0:T(8,128)(2,1)S(1)}, u32[]{:S(2)}, u32[]{:S(2)}) collective-permute-start(bf16[448,128]{1,0:T(8,128)(2,1)S(1)} %get-tuple-element.33), channel_id=1, source_target_pairs={{0,16},{8,24},{16,0},{24,8},{1,17},{9,25},{17,1},{25,9},{2,18},{10... | collective-permute-start | bytes 344072 | tf_op jit(solution)/shard_map/ppermute | solution.py:356
  17.6 11.3 %collective-permute-start.5 = (bf16[1856,128]{1,0:T(8,128)(2,1)S(1)}, bf16[1856,128]{1,0:T(8,128)(2,1)S(1)}, u32[]{:S(2)}, u32[]{:S(2)}) collective-permute-start(bf16[1856,128]{1,0:T(8,128)(2,1)S(1)} %pad_maximum_fusion.refs_0_), channel_id=1, source_target_pairs={{0,2},{1,5},{2,0},{3,7},{4,6},{5,1},{6,4},{7,3},{8,10},{9,13},{10,... | collective-permute-start | bytes 1425416 | tf_op jit(solution)/shard_map/ppermute | solution.py:324
  27.2 1.8 %collective-permute-start.9 = (bf16[1344,128]{1,0:T(8,128)(2,1)S(1)}, bf16[1344,128]{1,0:T(8,128)(2,1)S(1)}, u32[]{:S(2)}, u32[]{:S(2)}) collective-permute-start(bf16[1344,128]{1,0:T(8,128)(2,1)S(1)} %constant_dynamic-update-slice_fusion.refs_1_), channel_id=1, source_target_pairs={{0,1},{1,0},{2,3},{3,2},{4,5},{5,4},{6,7},{7,6},{8,9},{9,8},{10,11... | collective-permute-start | bytes 1032200 | tf_op jit(solution)/shard_map/ppermute | solution.py:319
  27.2 3.8 %collective-permute-start.10 = (bf16[1856,128]{1,0:T(8,128)(2,1)S(1)}, bf16[1856,128]{1,0:T(8,128)(2,1)S(1)}, u32[]{:S(2)}, u32[]{:S(2)}) collective-permute-start(bf16[1856,128]{1,0:T(8,128)(2,1)S(1)} %pad_maximum_fusion.refs_0_), channel_id=1, source_target_pairs={{0,1},{1,0},{2,3},{3,2},{4,5},{5,4},{6,7},{7,6},{8,9},{9,8},{10,11... | collective-permute-start | bytes 1425416 | tf_op jit(solution)/shard_map/ppermute | solution.py:319
  27.7 8.2 %collective-permute-start.8 = (bf16[1344,128]{1,0:T(8,128)(2,1)S(1)}, bf16[1344,128]{1,0:T(8,128)(2,1)S(1)}, u32[]{:S(2)}, u32[]{:S(2)}) collective-permute-start(bf16[1344,128]{1,0:T(8,128)(2,1)S(1)} %constant_dynamic-update-slice_fusion.refs_1_), channel_id=1, source_target_pairs={{0,2},{1,5},{2,0},{3,7},{4,6},{5,1},{6,4},{7,3},{8,10},{9,13},{10,... | collective-permute-start | bytes 1032200 | tf_op jit(solution)/shard_map/ppermute | solution.py:324
  29.0 2.1 %collective-permute-start.13 = (bf16[960,128]{1,0:T(8,128)(2,1)S(1)}, bf16[960,128]{1,0:T(8,128)(2,1)S(1)}, u32[]{:S(2)}, u32[]{:S(2)}) collective-permute-start(bf16[960,128]{1,0:T(8,128)(2,1)S(1)} %slice.39), channel_id=1, source_target_pairs={{0,1},{1,0},{2,3},{3,2},{4,5},{5,4},{6,7},{7,6},{8,9},{9,8},{10,11... | collective-permute-start | bytes 737288 | tf_op jit(solution)/shard_map/ppermute | solution.py:319
  29.4 1.7 %collective-permute-start.11 = (bf16[896,128]{1,0:T(8,128)(2,1)S(1)}, bf16[896,128]{1,0:T(8,128)(2,1)S(1)}, u32[]{:S(2)}, u32[]{:S(2)}) collective-permute-start(bf16[896,128]{1,0:T(8,128)(2,1)S(1)} %slice.38), channel_id=1, source_target_pairs={{0,1},{1,0},{2,3},{3,2},{4,5},{5,4},{6,7},{7,6},{8,9},{9,8},{10,11... | collective-permute-start | bytes 688136 | tf_op jit(solution)/shard_map/ppermute | solution.py:319
  29.7 1.4 %collective-permute-start.12 = (bf16[256,128]{1,0:T(8,128)(2,1)S(1)}, bf16[256,128]{1,0:T(8,128)(2,1)S(1)}, u32[]{:S(2)}, u32[]{:S(2)}) collective-permute-start(bf16[256,128]{1,0:T(8,128)(2,1)S(1)} %collective-permute-done.4.refs_6_.refs_7_), channel_id=1, source_target_pairs={{0,1},{1,0},{2,3},{3,2},{4,5},{5,4},{6,7},{7,6},{8,9},{9,8},{10,11... | collective-permute-start | bytes 196616 | tf_op jit(solution)/shard_map/ppermute | solution.py:319
  36.0 2.1 %collective-permute-start.14 = (bf16[1344,128]{1,0:T(8,128)(2,1)S(1)}, bf16[1344,128]{1,0:T(8,128)(2,1)S(1)}, u32[]{:S(2)}, u32[]{:S(2)}) collective-permute-start(bf16[1344,128]{1,0:T(8,128)(2,1)S(1)} %collective-permute-done.8.refs_2_), channel_id=1, source_target_pairs={{0,1},{1,0},{2,3},{3,2},{4,5},{5,4},{6,7},{7,6},{8,9},{9,8},{10,11... | collective-permute-start | bytes 1032200 | tf_op jit(solution)/shard_map/ppermute | solution.py:319
  49.5 6.7 %collective-permute-start.19 = (bf16[896,128]{1,0:T(8,128)(2,1)S(1)}, bf16[896,128]{1,0:T(8,128)(2,1)S(1)}, u32[]{:S(2)}, u32[]{:S(2)}) collective-permute-start(bf16[896,128]{1,0:T(8,128)(2,1)S(1)} %get-tuple-element.48), channel_id=1, source_target_pairs={{0,2},{1,5},{2,0},{3,7},{4,6},{5,1},{6,4},{7,3},{8,10},{9,13},{10,... | collective-permute-start | bytes 688136 | tf_op jit(solution)/shard_map/ppermute | solution.py:324
  55.9 6.1 %collective-permute-start.15 = (bf16[896,128]{1,0:T(8,128)(2,1)S(1)}, bf16[896,128]{1,0:T(8,128)(2,1)S(1)}, u32[]{:S(2)}, u32[]{:S(2)}) collective-permute-start(bf16[896,128]{1,0:T(8,128)(2,1)S(1)} %shard_map.63), channel_id=1, source_target_pairs={{0,2},{1,5},{2,0},{3,7},{4,6},{5,1},{6,4},{7,3},{8,10},{9,13},{10,... | collective-permute-start | bytes 688136 | tf_op jit(solution)/shard_map/ppermute | solution.py:324
  56.2 10.0 %collective-permute-start.20 = (bf16[896,128]{1,0:T(8,128)(2,1)S(1)}, bf16[896,128]{1,0:T(8,128)(2,1)S(1)}, u32[]{:S(2)}, u32[]{:S(2)}) collective-permute-start(bf16[896,128]{1,0:T(8,128)(2,1)S(1)} %add_convert_fusion.own_a), channel_id=1, source_target_pairs={{0,4},{1,3},{2,6},{3,1},{4,0},{5,7},{6,2},{7,5},{8,12},{9,11},{10,... | collective-permute-start | bytes 688136 | tf_op jit(solution)/shard_map/ppermute | solution.py:324
  62.1 4.9 %collective-permute-start.16 = (bf16[896,128]{1,0:T(8,128)(2,1)S(1)}, bf16[896,128]{1,0:T(8,128)(2,1)S(1)}, u32[]{:S(2)}, u32[]{:S(2)}) collective-permute-start(bf16[896,128]{1,0:T(8,128)(2,1)S(1)} %add_convert_fusion.1.own_a), channel_id=1, source_target_pairs={{0,4},{1,3},{2,6},{3,1},{4,0},{5,7},{6,2},{7,5},{8,12},{9,11},{10,... | collective-permute-start | bytes 688136 | tf_op jit(solution)/shard_map/ppermute | solution.py:324
  63.0 7.5 %collective-permute-start.21 = (bf16[896,128]{1,0:T(8,128)(2,1)S(1)}, bf16[896,128]{1,0:T(8,128)(2,1)S(1)}, u32[]{:S(2)}, u32[]{:S(2)}) collective-permute-start(bf16[896,128]{1,0:T(8,128)(2,1)S(1)} %add_convert_fusion.own_a), channel_id=1, source_target_pairs={{0,1},{1,0},{2,3},{3,2},{4,5},{5,4},{6,7},{7,6},{8,9},{9,8},{10,11... | collective-permute-start | bytes 688136 | tf_op jit(solution)/shard_map/ppermute | solution.py:319
  66.3 4.2 %collective-permute-start.22 = (bf16[896,128]{1,0:T(8,128)(2,1)S(1)}, bf16[896,128]{1,0:T(8,128)(2,1)S(1)}, u32[]{:S(2)}, u32[]{:S(2)}) collective-permute-start(bf16[896,128]{1,0:T(8,128)(2,1)S(1)} %collective-permute-done.20.own_b), channel_id=1, source_target_pairs={{0,1},{1,0},{2,3},{3,2},{4,5},{5,4},{6,7},{7,6},{8,9},{9,8},{10,11... | collective-permute-start | bytes 688136 | tf_op jit(solution)/shard_map/ppermute | solution.py:319
  66.3 5.9 %collective-permute-start.17 = (bf16[896,128]{1,0:T(8,128)(2,1)S(1)}, bf16[896,128]{1,0:T(8,128)(2,1)S(1)}, u32[]{:S(2)}, u32[]{:S(2)}) collective-permute-start(bf16[896,128]{1,0:T(8,128)(2,1)S(1)} %add_convert_fusion.1.own_a), channel_id=1, source_target_pairs={{0,1},{1,0},{2,3},{3,2},{4,5},{5,4},{6,7},{7,6},{8,9},{9,8},{10,11... | collective-permute-start | bytes 688136 | tf_op jit(solution)/shard_map/ppermute | solution.py:319
  67.0 5.1 %collective-permute-start.18 = (bf16[896,128]{1,0:T(8,128)(2,1)S(1)}, bf16[896,128]{1,0:T(8,128)(2,1)S(1)}, u32[]{:S(2)}, u32[]{:S(2)}) collective-permute-start(bf16[896,128]{1,0:T(8,128)(2,1)S(1)} %collective-permute-done.16.own_b), channel_id=1, source_target_pairs={{0,1},{1,0},{2,3},{3,2},{4,5},{5,4},{6,7},{7,6},{8,9},{9,8},{10,11... | collective-permute-start | bytes 688136 | tf_op jit(solution)/shard_map/ppermute | solution.py:319

commit v8 on v7

--- a/solution.py
+++ b/solution.py
@@ -512,6 +512,8 @@
             met = after(traded, early_terms) if group else cross(own, 2, 4)
             half = (own.astype(F32) + met.astype(F32)).astype(BF)
             other = cross(half, 4, 2)
+            if grads:
+                other = after(other, grads[0])
             kernel, parts = both_kernel, (half, other, exchange(half, 1), exchange(other, 1))
         else:
             level = [own] + [exchange(own, k * replicas) for k in range(1, micro_count)]

time: 74.1 us -> 74.1 us (level)
  starting transfers between devices: 25.8 us -> 24.2 us
  waiting for transfers between devices: 18.2 us -> 19.5 us
    ppermute x13, starting transfers between devices: 11.5 us -> 9.81 us  [exchange(): return lax.ppermute(block, 'space', [(i, i ^ mask) for i in range(count)])]
    ppermute x13, waiting for transfers between devices: 2.19 us -> 3.3 us  [exchange(): return lax.ppermute(block, 'space', [(i, i ^ mask) for i in range(count)])]
  transfers between devices with their start and end apart: 23 -> 23, of which waited for: 7 -> 8; matrix products, arithmetic and copies ran while one was open for 0% -> 0% of each run, Pallas kernels for 19% -> 19%
where the time goes in v8:
time: 74.1 us; the launch traced here: 73.6 us
  Pallas kernels  27.2 us (37%)
  starting transfers between devices  24.2 us (33%)
  waiting for transfers between devices  19.5 us (26%)
  other arithmetic  1.58 us (2%)
  between operations  1.05 us (1%)
    pallas_call x7, Pallas kernels, call(): pl.pallas_call(kernel, out_shape=outs, in_specs=specs, out_specs=[far if...  27.2 us
    ppermute x13, starting transfers between devices, exchange(): return lax.ppermute(block, 'space', [(i, i ^ mask) for i in range(count)])  9.81 us
    ppermute x2, waiting for transfers between devices, gather_paired(): lax.ppermute(after(part[group], *near[:group]), 'section', across)  9.72 us
    ppermute x2, starting transfers between devices, gather_paired(): lax.ppermute(after(mine[group], *near), ('section', 'space'), route)  6.94 us
    ppermute x6, starting transfers between devices, cross(): lax.ppermute(block, 'space', [(i, i ^ (second if i % 2 else first)) for i...  6.32 us
    ppermute x6, waiting for transfers between devices, cross(): lax.ppermute(block, 'space', [(i, i ^ (second if i % 2 else first)) for i...  5.02 us
    ppermute x13, waiting for transfers between devices, exchange(): return lax.ppermute(block, 'space', [(i, i ^ mask) for i in range(count)])  3.3 us
  transfers between devices with their start and end apart: 23, of which 8 were waited for; matrix products, arithmetic and copies ran while one was open for 0% of the time, Pallas kernels for 19%

profile of v8, /device:TPU:1, one launch (start us, length us, event | category | flops | bytes accessed | tf_op | source)
XLA Modules:
  0.0 73.6 jit_solution(17896307986311152750)
XLA Ops:
  0.7 1.3 %fusion = bf16[2,896,128]{2,1,0:T(8,128)(2,1)S(1)} fusion(bf16[2,64,128]{2,1,0:T(8,128)(2,1)} %bitcast.27, bf16[2,1728,128]{2,1,0:T(8,128)(2,1)} %bitcast.24, pred[]{:T(512)S(6)} %eq.7), kind=kLoop, calls=%fused_computation.2 | loop fusion | flops 1146880 | bytes 1835009 | tf_op jit(solution)/shard_map/jit(_where)/select_n | solution.py:337
  2.1 4.2 %collective-permute-start = (bf16[896,128]{1,0:T(8,128)(2,1)S(1)}, bf16[896,128]{1,0:T(8,128)(2,1)S(1)}, u32[]{:S(2)}, u32[]{:S(2)}) collective-permute-start(bf16[896,128]{1,0:T(8,128)(2,1)S(1)} %get-tuple-element.59), channel_id=1, source_target_pairs={{0,8},{1,25},{2,10},{3,27},{4,12},{5,29},{6,14},{7,31},{8,16},{9,1... | collective-permute-start | bytes 688136 | tf_op jit(solution)/shard_map/ppermute | solution.py:355
  6.4 1.1 %collective-permute-done.2.token = bf16[16,128]{1,0:T(8,128)(2,1)S(1)} collective-permute-done((bf16[16,128]{1,0:T(8,128)(2,1)S(1)}, bf16[16,128]{1,0:T(8,128)(2,1)S(1)}, u32[]{:S(2)}, u32[]{:S(2)}) %collective-permute-start.2) | collective-permute-done | bytes 4128 | tf_op jit(solution)/shard_map/ppermute | solution.py:319
  7.5 0.8 %shard_map.59 = (bf16[256,128]{1,0:T(8,128)(2,1)S(1)}, bf16[256,128]{1,0:T(8,128)(2,1)S(1)}, bf16[256,128]{1,0:T(8,128)(2,1)S(1)}, bf16[512,128]{1,0:T(8,128)(2,1)S(1)}) custom-call(s32[3]{0:T(128)S(1)} %pad_add_fusion.me_ref, bf16[4,128,128]{2,1,0:T(8,128)(2,1)S(1)} %bitcast.28, bf16[4,128,128]{2,1,0:T(8,128)(2,1)S(1)} %bitcast.29, ...), custom_call_target="tpu_custom_call" | custom-call | flops 104857600 | bytes 1048576 | tf_op jit(solution)/shard_map/pallas_call | solution.py:305
  8.6 1.1 %collective-permute-start.1 = (bf16[448,128]{1,0:T(8,128)(2,1)S(1)}, bf16[448,128]{1,0:T(8,128)(2,1)S(1)}, u32[]{:S(2)}, u32[]{:S(2)}) collective-permute-start(bf16[448,128]{1,0:T(8,128)(2,1)S(1)} %get-tuple-element.57), channel_id=1, source_target_pairs={{0,16},{8,24},{16,0},{24,8},{1,17},{9,25},{17,1},{25,9},{2,18},{10... | collective-permute-start | bytes 344072 | tf_op jit(solution)/shard_map/ppermute | solution.py:356
  9.7 2.2 %collective-permute-start.4 = (bf16[256,128]{1,0:T(8,128)(2,1)S(1)}, bf16[256,128]{1,0:T(8,128)(2,1)S(1)}, u32[]{:S(2)}, u32[]{:S(2)}) collective-permute-start(bf16[256,128]{1,0:T(8,128)(2,1)S(1)} %get-tuple-element.31), channel_id=1, source_target_pairs={{0,6},{1,7},{2,4},{3,5},{4,2},{5,3},{6,0},{7,1},{8,14},{9,15},{10,... | collective-permute-start | bytes 196616 | tf_op jit(solution)/shard_map/ppermute | solution.py:319
  11.9 2.7 %collective-permute-start.6 = (bf16[896,128]{1,0:T(8,128)(2,1)S(1)}, bf16[896,128]{1,0:T(8,128)(2,1)S(1)}, u32[]{:S(2)}, u32[]{:S(2)}) collective-permute-start(bf16[896,128]{1,0:T(8,128)(2,1)S(1)} %get-tuple-element.33), channel_id=1, source_target_pairs={{0,8},{1,25},{2,10},{3,27},{4,12},{5,29},{6,14},{7,31},{8,16},{9,1... | collective-permute-start | bytes 688136 | tf_op jit(solution)/shard_map/ppermute | solution.py:355
  14.6 3.0 %collective-permute-done.1 = bf16[448,128]{1,0:T(8,128)(2,1)S(1)} collective-permute-done((bf16[448,128]{1,0:T(8,128)(2,1)S(1)}, bf16[448,128]{1,0:T(8,128)(2,1)S(1)}, u32[]{:S(2)}, u32[]{:S(2)}) %collective-permute-start.1) | collective-permute-done | bytes 114720 | tf_op jit(solution)/shard_map/ppermute | solution.py:356
  17.6 1.3 %collective-permute-start.5 = (bf16[1856,128]{1,0:T(8,128)(2,1)S(1)}, bf16[1856,128]{1,0:T(8,128)(2,1)S(1)}, u32[]{:S(2)}, u32[]{:S(2)}) collective-permute-start(bf16[1856,128]{1,0:T(8,128)(2,1)S(1)} %pad_maximum_fusion.refs_0_), channel_id=1, source_target_pairs={{0,2},{1,5},{2,0},{3,7},{4,6},{5,1},{6,4},{7,3},{8,10},{9,13},{10,... | collective-permute-start | bytes 1425416 | tf_op jit(solution)/shard_map/ppermute | solution.py:324
  18.9 1.4 %collective-permute-done.6 = bf16[896,128]{1,0:T(8,128)(2,1)S(1)} collective-permute-done((bf16[896,128]{1,0:T(8,128)(2,1)S(1)}, bf16[896,128]{1,0:T(8,128)(2,1)S(1)}, u32[]{:S(2)}, u32[]{:S(2)}) %collective-permute-start.6) | collective-permute-done | bytes 229408 | tf_op jit(solution)/shard_map/ppermute | solution.py:355
  20.4 6.7 %collective-permute-done.7 = bf16[448,128]{1,0:T(8,128)(2,1)S(1)} collective-permute-done((bf16[448,128]{1,0:T(8,128)(2,1)S(1)}, bf16[448,128]{1,0:T(8,128)(2,1)S(1)}, u32[]{:S(2)}, u32[]{:S(2)}) %collective-permute-start.7) | collective-permute-done | bytes 114720 | tf_op jit(solution)/shard_map/ppermute | solution.py:356
  27.2 0.5 collective-permute-start.10
  27.7 1.2 %collective-permute-start.8 = (bf16[1344,128]{1,0:T(8,128)(2,1)S(1)}, bf16[1344,128]{1,0:T(8,128)(2,1)S(1)}, u32[]{:S(2)}, u32[]{:S(2)}) collective-permute-start(bf16[1344,128]{1,0:T(8,128)(2,1)S(1)} %constant_dynamic-update-slice_fusion.refs_1_), channel_id=1, source_target_pairs={{0,2},{1,5},{2,0},{3,7},{4,6},{5,1},{6,4},{7,3},{8,10},{9,13},{10,... | collective-permute-start | bytes 1032200 | tf_op jit(solution)/shard_map/ppermute | solution.py:324
  29.0 0.4 collective-permute-start.13
  29.7 0.3 collective-permute-start.12
  30.0 1.1 %collective-permute-done.12.refs_7_.refs_8_ = bf16[256,128]{1,0:T(8,128)(2,1)S(1)} collective-permute-done((bf16[256,128]{1,0:T(8,128)(2,1)S(1)}, bf16[256,128]{1,0:T(8,128)(2,1)S(1)}, u32[]{:S(2)}, u32[]{:S(2)}) %collective-permute-start.12) | collective-permute-done | bytes 65568 | tf_op jit(solution)/shard_map/ppermute | solution.py:319
  31.1 4.9 %shard_map.60 = (f32[1024,128]{1,0:T(8,128)S(1)}, bf16[4,1280,256]{2,1,0:T(8,128)(2,1)S(1)}, bf16[4,1024,256]{2,1,0:T(8,128)(2,1)S(1)}, bf16[2,10,128,384]{3,2,1...) custom-call(s32[3]{0:T(128)S(1)} %pad_add_fusion.me_ref, ...), custom_call_target="tpu_custom_call" | custom-call | flops 209715200 | bytes 2097152 | tf_op jit(solution)/shard_map/pallas_call | solution.py:305
  36.3 1.8 %shard_map.61 = (f32[1024,128]{1,0:T(8,128)S(1)}, bf16[4,1024,256]{2,1,0:T(8,128)(2,1)S(1)}, bf16[2,10,128,384]{3,2,1,0:T(8,128)(2,1)S(1)}, bf16[2,1024,256]{2,1,0:T(8,128)(2,1)S(1)}) custom-call(s32[3]{0:T(128)S(1)} %pad_add_fusion.me_ref, ...), custom_call_target="tpu_custom_call", output_to_operand_aliasing={{0}: (3, {}), {1}: (4, {}), {2}: (5, {}), {3}: (6, {})} | custom-call | flops 209715200 | bytes 2097152 | tf_op jit(solution)/shard_map/pallas_call | solution.py:305
  38.1 11.4 %shard_map.62 = (f32[1024,128]{1,0:T(8,128)S(1)}, bf16[896,128]{1,0:T(8,128)(2,1)S(1)}) custom-call(s32[3]{0:T(128)S(1)} %pad_add_fusion.me_ref, bf16[2,1,1728,128]{3,2,1,0:T(8,128)(2,1)S(1)} %bitcast.26, bf16[2,1,64,128]{3,2,1,0:T(8,128)(2,1)S(1)} %copy-done.1, bf16[1856,128]{1,0:T(8,128)(2,1)S(1)} %collective-permute-done.5.refs_1_.refs_0_, ...), custom_call_target="tpu_custom_call" | custom-call | flops 4194304000 | bytes 41943040 | tf_op jit(solution)/shard_map/pallas_call | solution.py:305
  49.5 1.3 %collective-permute-start.17 = (bf16[896,128]{1,0:T(8,128)(2,1)S(1)}, bf16[896,128]{1,0:T(8,128)(2,1)S(1)}, u32[]{:S(2)}, u32[]{:S(2)}) collective-permute-start(bf16[896,128]{1,0:T(8,128)(2,1)S(1)} %get-tuple-element.49), channel_id=1, source_target_pairs={{0,2},{1,5},{2,0},{3,7},{4,6},{5,1},{6,4},{7,3},{8,10},{9,13},{10,... | collective-permute-start | bytes 688136 | tf_op jit(solution)/shard_map/ppermute | solution.py:324
  50.8 5.0 %shard_map.63 = bf16[896,128]{1,0:T(8,128)(2,1)S(1)} custom-call(s32[3]{0:T(128)S(1)} %pad_add_fusion.me_ref, f32[1024,128]{1,0:T(8,128)S(1)} %get-tuple-element.45.up_in, bf16[4,1280,256]{2,1,0:T(8,128)(2,1)S(1)} %get-tuple-element.39.folded, bf16[4,1024,256]{2,1,0:T(8,128)(2,1)S(1)} %get-tuple-element.46.slope, ...), custom_call_target="tpu_custom_call" | custom-call | flops 2097152000 | bytes 20971520 | tf_op jit(solution)/shard_map/pallas_call | solution.py:305
  55.9 1.1 %collective-permute-start.18 = (bf16[896,128]{1,0:T(8,128)(2,1)S(1)}, bf16[896,128]{1,0:T(8,128)(2,1)S(1)}, u32[]{:S(2)}, u32[]{:S(2)}) collective-permute-start(bf16[896,128]{1,0:T(8,128)(2,1)S(1)} %add_convert_fusion.own_a), channel_id=1, source_target_pairs={{0,4},{1,3},{2,6},{3,1},{4,0},{5,7},{6,2},{7,5},{8,12},{9,11},{10,... | collective-permute-start | bytes 688136 | tf_op jit(solution)/shard_map/ppermute | solution.py:324
  57.0 0.4 collective-permute-start.15
  57.4 1.4 %collective-permute-start.19 = (bf16[896,128]{1,0:T(8,128)(2,1)S(1)}, bf16[896,128]{1,0:T(8,128)(2,1)S(1)}, u32[]{:S(2)}, u32[]{:S(2)}) collective-permute-start(bf16[896,128]{1,0:T(8,128)(2,1)S(1)} %add_convert_fusion.own_a), channel_id=1, source_target_pairs={{0,1},{1,0},{2,3},{3,2},{4,5},{5,4},{6,7},{7,6},{8,9},{9,8},{10,11... | collective-permute-start | bytes 688136 | tf_op jit(solution)/shard_map/ppermute | solution.py:319
  58.7 2.6 %collective-permute-done.18.own_b = bf16[896,128]{1,0:T(8,128)(2,1)S(1)} collective-permute-done((bf16[896,128]{1,0:T(8,128)(2,1)S(1)}, bf16[896,128]{1,0:T(8,128)(2,1)S(1)}, u32[]{:S(2)}, u32[]{:S(2)}) %collective-permute-start.18) | collective-permute-done | bytes 229408 | tf_op jit(solution)/shard_map/ppermute | solution.py:324
  61.4 3.1 %collective-permute-start.20 = (bf16[896,128]{1,0:T(8,128)(2,1)S(1)}, bf16[896,128]{1,0:T(8,128)(2,1)S(1)}, u32[]{:S(2)}, u32[]{:S(2)}) collective-permute-start(bf16[896,128]{1,0:T(8,128)(2,1)S(1)} %collective-permute-done.18.own_b), channel_id=1, source_target_pairs={{0,1},{1,0},{2,3},{3,2},{4,5},{5,4},{6,7},{7,6},{8,9},{9,8},{10,11... | collective-permute-start | bytes 688136 | tf_op jit(solution)/shard_map/ppermute | solution.py:319
  64.6 1.0 %collective-permute-start.16 = (bf16[896,128]{1,0:T(8,128)(2,1)S(1)}, bf16[896,128]{1,0:T(8,128)(2,1)S(1)}, u32[]{:S(2)}, u32[]{:S(2)}) collective-permute-start(bf16[896,128]{1,0:T(8,128)(2,1)S(1)} %add_convert_fusion.1.own_a), channel_id=1, source_target_pairs={{0,4},{1,3},{2,6},{3,1},{4,0},{5,7},{6,2},{7,5},{8,12},{9,11},{10,... | collective-permute-start | bytes 688136 | tf_op jit(solution)/shard_map/ppermute | solution.py:324
  65.8 1.6 %shard_map.64 = (f32[2,1,1728,128]{3,2,1,0:T(8,128)}, f32[2,1,64,128]{3,2,1,0:T(8,128)}) custom-call(s32[3]{0:T(128)S(1)} %pad_add_fusion.me_ref, bf16[896,128]{1,0:T(8,128)(2,1)S(1)} %add_convert_fusion.own_a, bf16[896,128]{1,0:T(8,128)(2,1)S(1)} %collective-permute-done.18.own_b, bf16[896,128]{1,0:T(8,128)(2,1)S(1)} %collective-permute-done.19.far_a, ...), custom_call_target="tpu_custom_call" | custom-call | flops 6553600 | bytes 65536 | tf_op jit(solution)/shard_map/pallas_call | solution.py:305
  67.5 2.4 %collective-permute-done.16.own_b = bf16[896,128]{1,0:T(8,128)(2,1)S(1)} collective-permute-done((bf16[896,128]{1,0:T(8,128)(2,1)S(1)}, bf16[896,128]{1,0:T(8,128)(2,1)S(1)}, u32[]{:S(2)}, u32[]{:S(2)}) %collective-permute-start.16) | collective-permute-done | bytes 229408 | tf_op jit(solution)/shard_map/ppermute | solution.py:324
  69.8 0.9 %collective-permute-start.22 = (bf16[896,128]{1,0:T(8,128)(2,1)S(1)}, bf16[896,128]{1,0:T(8,128)(2,1)S(1)}, u32[]{:S(2)}, u32[]{:S(2)}) collective-permute-start(bf16[896,128]{1,0:T(8,128)(2,1)S(1)} %collective-permute-done.16.own_b), channel_id=1, source_target_pairs={{0,1},{1,0},{2,3},{3,2},{4,5},{5,4},{6,7},{7,6},{8,9},{9,8},{10,11... | collective-permute-start | bytes 688136 | tf_op jit(solution)/shard_map/ppermute | solution.py:319
  70.7 1.1 %collective-permute-done.22.far_b = bf16[896,128]{1,0:T(8,128)(2,1)S(1)} collective-permute-done((bf16[896,128]{1,0:T(8,128)(2,1)S(1)}, bf16[896,128]{1,0:T(8,128)(2,1)S(1)}, u32[]{:S(2)}, u32[]{:S(2)}) %collective-permute-start.22) | collective-permute-done | bytes 229408 | tf_op jit(solution)/shard_map/ppermute | solution.py:319
  71.8 1.6 %shard_map.65 = (f32[2,1,1728,128]{3,2,1,0:T(8,128)}, f32[2,1,64,128]{3,2,1,0:T(8,128)}) custom-call(s32[3]{0:T(128)S(1)} %pad_add_fusion.me_ref, bf16[896,128]{1,0:T(8,128)(2,1)S(1)} %add_convert_fusion.1.own_a, bf16[896,128]{1,0:T(8,128)(2,1)S(1)} %collective-permute-done.16.own_b, ...), custom_call_target="tpu_custom_call", output_to_operand_aliasing={{0}: (5, {}), {1}: (6, {})} | custom-call | flops 6553600 | bytes 65536 | tf_op jit(solution)/shard_map/pallas_call | solution.py:305
  (42 shorter events, 1.5 us)
Async XLA Ops:
  0.6 6.9 %copy-start.2 = (bf16[4,64,1,2,128]{4,3,2,1,0:T(2,128)(2,1)S(1)}, bf16[4,64,1,2,128]{4,3,2,1,0:T(2,128)(2,1)}, u32[]{:S(2)}) copy-start(bf16[4,64,1,2,128]{4,3,2,1,0:T(2,128)(2,1)} %param.4) | copy-start | bytes 393220
  0.6 6.8 %copy-start.3 = (bf16[4,64,1,2,128]{4,3,2,1,0:T(2,128)(2,1)S(1)}, bf16[4,64,1,2,128]{4,3,2,1,0:T(2,128)(2,1)}, u32[]{:S(2)}) copy-start(bf16[4,64,1,2,128]{4,3,2,1,0:T(2,128)(2,1)} %param.5) | copy-start | bytes 393220
  2.1 29.0 %copy-start = (bf16[2,1,128,1728]{2,3,1,0:T(8,128)(2,1)S(1)}, bf16[2,1,128,1728]{2,3,1,0:T(8,128)(2,1)}, u32[]{:S(2)}) copy-start(bf16[2,1,128,1728]{2,3,1,0:T(8,128)(2,1)} %param.6) | copy-start | bytes 2654212
  2.1 29.0 %copy-start.1 = (bf16[2,1,64,128]{3,2,1,0:T(8,128)(2,1)S(1)}, bf16[2,1,64,128]{3,2,1,0:T(8,128)(2,1)}, u32[]{:S(2)}) copy-start(bf16[2,1,64,128]{3,2,1,0:T(8,128)(2,1)} %mix.3) | copy-start | bytes 98308
  2.1 9.8 %collective-permute-start = (bf16[896,128]{1,0:T(8,128)(2,1)S(1)}, bf16[896,128]{1,0:T(8,128)(2,1)S(1)}, u32[]{:S(2)}, u32[]{:S(2)}) collective-permute-start(bf16[896,128]{1,0:T(8,128)(2,1)S(1)} %get-tuple-element.59), channel_id=1, source_target_pairs={{0,8},{1,25},{2,10},{3,27},{4,12},{5,29},{6,14},{7,31},{8,16},{9,1... | collective-permute-start | bytes 688136 | tf_op jit(solution)/shard_map/ppermute | solution.py:355
  6.3 1.2 %collective-permute-start.2 = (bf16[16,128]{1,0:T(8,128)(2,1)S(1)}, bf16[16,128]{1,0:T(8,128)(2,1)S(1)}, u32[]{:S(2)}, u32[]{:S(2)}) collective-permute-start(bf16[16,128]{1,0:T(8,128)(2,1)S(1)} %slice_bitcast_fusion.2), channel_id=1, source_target_pairs={{0,1},{1,0},{2,3},{3,2},{4,5},{5,4},{6,7},{7,6},{8,9},{9,8},{10,11... | collective-permute-start | bytes 12296 | tf_op jit(solution)/shard_map/ppermute | solution.py:319
  8.3 3.6 %collective-permute-start.3 = (bf16[512,128]{1,0:T(8,128)(2,1)S(1)}, bf16[512,128]{1,0:T(8,128)(2,1)S(1)}, u32[]{:S(2)}, u32[]{:S(2)}) collective-permute-start(bf16[512,128]{1,0:T(8,128)(2,1)S(1)} %get-tuple-element.30), channel_id=1, source_target_pairs={{0,1},{1,0},{2,3},{3,2},{4,5},{5,4},{6,7},{7,6},{8,9},{9,8},{10,11... | collective-permute-start | bytes 393224 | tf_op jit(solution)/shard_map/ppermute | solution.py:319
  8.6 9.0 %collective-permute-start.1 = (bf16[448,128]{1,0:T(8,128)(2,1)S(1)}, bf16[448,128]{1,0:T(8,128)(2,1)S(1)}, u32[]{:S(2)}, u32[]{:S(2)}) collective-permute-start(bf16[448,128]{1,0:T(8,128)(2,1)S(1)} %get-tuple-element.57), channel_id=1, source_target_pairs={{0,16},{8,24},{16,0},{24,8},{1,17},{9,25},{17,1},{25,9},{2,18},{10... | collective-permute-start | bytes 344072 | tf_op jit(solution)/shard_map/ppermute | solution.py:356
  9.7 7.9 %collective-permute-start.4 = (bf16[256,128]{1,0:T(8,128)(2,1)S(1)}, bf16[256,128]{1,0:T(8,128)(2,1)S(1)}, u32[]{:S(2)}, u32[]{:S(2)}) collective-permute-start(bf16[256,128]{1,0:T(8,128)(2,1)S(1)} %get-tuple-element.31), channel_id=1, source_target_pairs={{0,6},{1,7},{2,4},{3,5},{4,2},{5,3},{6,0},{7,1},{8,14},{9,15},{10,... | collective-permute-start | bytes 196616 | tf_op jit(solution)/shard_map/ppermute | solution.py:319
  11.9 8.5 %collective-permute-start.6 = (bf16[896,128]{1,0:T(8,128)(2,1)S(1)}, bf16[896,128]{1,0:T(8,128)(2,1)S(1)}, u32[]{:S(2)}, u32[]{:S(2)}) collective-permute-start(bf16[896,128]{1,0:T(8,128)(2,1)S(1)} %get-tuple-element.33), channel_id=1, source_target_pairs={{0,8},{1,25},{2,10},{3,27},{4,12},{5,29},{6,14},{7,31},{8,16},{9,1... | collective-permute-start | bytes 688136 | tf_op jit(solution)/shard_map/ppermute | solution.py:355
  14.6 12.5 %collective-permute-start.7 = (bf16[448,128]{1,0:T(8,128)(2,1)S(1)}, bf16[448,128]{1,0:T(8,128)(2,1)S(1)}, u32[]{:S(2)}, u32[]{:S(2)}) collective-permute-start(bf16[448,128]{1,0:T(8,128)(2,1)S(1)} %get-tuple-element.34), channel_id=1, source_target_pairs={{0,16},{8,24},{16,0},{24,8},{1,17},{9,25},{17,1},{25,9},{2,18},{10... | collective-permute-start | bytes 344072 | tf_op jit(solution)/shard_map/ppermute | solution.py:356
  17.6 11.3 %collective-permute-start.5 = (bf16[1856,128]{1,0:T(8,128)(2,1)S(1)}, bf16[1856,128]{1,0:T(8,128)(2,1)S(1)}, u32[]{:S(2)}, u32[]{:S(2)}) collective-permute-start(bf16[1856,128]{1,0:T(8,128)(2,1)S(1)} %pad_maximum_fusion.refs_0_), channel_id=1, source_target_pairs={{0,2},{1,5},{2,0},{3,7},{4,6},{5,1},{6,4},{7,3},{8,10},{9,13},{10,... | collective-permute-start | bytes 1425416 | tf_op jit(solution)/shard_map/ppermute | solution.py:324
  27.2 1.8 %collective-permute-start.9 = (bf16[1344,128]{1,0:T(8,128)(2,1)S(1)}, bf16[1344,128]{1,0:T(8,128)(2,1)S(1)}, u32[]{:S(2)}, u32[]{:S(2)}) collective-permute-start(bf16[1344,128]{1,0:T(8,128)(2,1)S(1)} %constant_dynamic-update-slice_fusion.refs_1_), channel_id=1, source_target_pairs={{0,1},{1,0},{2,3},{3,2},{4,5},{5,4},{6,7},{7,6},{8,9},{9,8},{10,11... | collective-permute-start | bytes 1032200 | tf_op jit(solution)/shard_map/ppermute | solution.py:319
  27.2 3.8 %collective-permute-start.10 = (bf16[1856,128]{1,0:T(8,128)(2,1)S(1)}, bf16[1856,128]{1,0:T(8,128)(2,1)S(1)}, u32[]{:S(2)}, u32[]{:S(2)}) collective-permute-start(bf16[1856,128]{1,0:T(8,128)(2,1)S(1)} %pad_maximum_fusion.refs_0_), channel_id=1, source_target_pairs={{0,1},{1,0},{2,3},{3,2},{4,5},{5,4},{6,7},{7,6},{8,9},{9,8},{10,11... | collective-permute-start | bytes 1425416 | tf_op jit(solution)/shard_map/ppermute | solution.py:319
  27.7 8.2 %collective-permute-start.8 = (bf16[1344,128]{1,0:T(8,128)(2,1)S(1)}, bf16[1344,128]{1,0:T(8,128)(2,1)S(1)}, u32[]{:S(2)}, u32[]{:S(2)}) collective-permute-start(bf16[1344,128]{1,0:T(8,128)(2,1)S(1)} %constant_dynamic-update-slice_fusion.refs_1_), channel_id=1, source_target_pairs={{0,2},{1,5},{2,0},{3,7},{4,6},{5,1},{6,4},{7,3},{8,10},{9,13},{10,... | collective-permute-start | bytes 1032200 | tf_op jit(solution)/shard_map/ppermute | solution.py:324
  29.0 2.1 %collective-permute-start.13 = (bf16[960,128]{1,0:T(8,128)(2,1)S(1)}, bf16[960,128]{1,0:T(8,128)(2,1)S(1)}, u32[]{:S(2)}, u32[]{:S(2)}) collective-permute-start(bf16[960,128]{1,0:T(8,128)(2,1)S(1)} %slice.39), channel_id=1, source_target_pairs={{0,1},{1,0},{2,3},{3,2},{4,5},{5,4},{6,7},{7,6},{8,9},{9,8},{10,11... | collective-permute-start | bytes 737288 | tf_op jit(solution)/shard_map/ppermute | solution.py:319
  29.4 1.7 %collective-permute-start.11 = (bf16[896,128]{1,0:T(8,128)(2,1)S(1)}, bf16[896,128]{1,0:T(8,128)(2,1)S(1)}, u32[]{:S(2)}, u32[]{:S(2)}) collective-permute-start(bf16[896,128]{1,0:T(8,128)(2,1)S(1)} %slice.38), channel_id=1, source_target_pairs={{0,1},{1,0},{2,3},{3,2},{4,5},{5,4},{6,7},{7,6},{8,9},{9,8},{10,11... | collective-permute-start | bytes 688136 | tf_op jit(solution)/shard_map/ppermute | solution.py:319
  29.7 1.4 %collective-permute-start.12 = (bf16[256,128]{1,0:T(8,128)(2,1)S(1)}, bf16[256,128]{1,0:T(8,128)(2,1)S(1)}, u32[]{:S(2)}, u32[]{:S(2)}) collective-permute-start(bf16[256,128]{1,0:T(8,128)(2,1)S(1)} %collective-permute-done.4.refs_6_.refs_7_), channel_id=1, source_target_pairs={{0,1},{1,0},{2,3},{3,2},{4,5},{5,4},{6,7},{7,6},{8,9},{9,8},{10,11... | collective-permute-start | bytes 196616 | tf_op jit(solution)/shard_map/ppermute | solution.py:319
  36.0 2.1 %collective-permute-start.14 = (bf16[1344,128]{1,0:T(8,128)(2,1)S(1)}, bf16[1344,128]{1,0:T(8,128)(2,1)S(1)}, u32[]{:S(2)}, u32[]{:S(2)}) collective-permute-start(bf16[1344,128]{1,0:T(8,128)(2,1)S(1)} %collective-permute-done.8.refs_2_), channel_id=1, source_target_pairs={{0,1},{1,0},{2,3},{3,2},{4,5},{5,4},{6,7},{7,6},{8,9},{9,8},{10,11... | collective-permute-start | bytes 1032200 | tf_op jit(solution)/shard_map/ppermute | solution.py:319
  49.5 6.4 %collective-permute-start.17 = (bf16[896,128]{1,0:T(8,128)(2,1)S(1)}, bf16[896,128]{1,0:T(8,128)(2,1)S(1)}, u32[]{:S(2)}, u32[]{:S(2)}) collective-permute-start(bf16[896,128]{1,0:T(8,128)(2,1)S(1)} %get-tuple-element.49), channel_id=1, source_target_pairs={{0,2},{1,5},{2,0},{3,7},{4,6},{5,1},{6,4},{7,3},{8,10},{9,13},{10,... | collective-permute-start | bytes 688136 | tf_op jit(solution)/shard_map/ppermute | solution.py:324
  55.9 5.4 %collective-permute-start.18 = (bf16[896,128]{1,0:T(8,128)(2,1)S(1)}, bf16[896,128]{1,0:T(8,128)(2,1)S(1)}, u32[]{:S(2)}, u32[]{:S(2)}) collective-permute-start(bf16[896,128]{1,0:T(8,128)(2,1)S(1)} %add_convert_fusion.own_a), channel_id=1, source_target_pairs={{0,4},{1,3},{2,6},{3,1},{4,0},{5,7},{6,2},{7,5},{8,12},{9,11},{10,... | collective-permute-start | bytes 688136 | tf_op jit(solution)/shard_map/ppermute | solution.py:324
  57.0 7.5 %collective-permute-start.15 = (bf16[896,128]{1,0:T(8,128)(2,1)S(1)}, bf16[896,128]{1,0:T(8,128)(2,1)S(1)}, u32[]{:S(2)}, u32[]{:S(2)}) collective-permute-start(bf16[896,128]{1,0:T(8,128)(2,1)S(1)} %shard_map.63), channel_id=1, source_target_pairs={{0,2},{1,5},{2,0},{3,7},{4,6},{5,1},{6,4},{7,3},{8,10},{9,13},{10,... | collective-permute-start | bytes 688136 | tf_op jit(solution)/shard_map/ppermute | solution.py:324
  57.4 8.4 %collective-permute-start.19 = (bf16[896,128]{1,0:T(8,128)(2,1)S(1)}, bf16[896,128]{1,0:T(8,128)(2,1)S(1)}, u32[]{:S(2)}, u32[]{:S(2)}) collective-permute-start(bf16[896,128]{1,0:T(8,128)(2,1)S(1)} %add_convert_fusion.own_a), channel_id=1, source_target_pairs={{0,1},{1,0},{2,3},{3,2},{4,5},{5,4},{6,7},{7,6},{8,9},{9,8},{10,11... | collective-permute-start | bytes 688136 | tf_op jit(solution)/shard_map/ppermute | solution.py:319
  61.4 4.4 %collective-permute-start.20 = (bf16[896,128]{1,0:T(8,128)(2,1)S(1)}, bf16[896,128]{1,0:T(8,128)(2,1)S(1)}, u32[]{:S(2)}, u32[]{:S(2)}) collective-permute-start(bf16[896,128]{1,0:T(8,128)(2,1)S(1)} %collective-permute-done.18.own_b), channel_id=1, source_target_pairs={{0,1},{1,0},{2,3},{3,2},{4,5},{5,4},{6,7},{7,6},{8,9},{9,8},{10,11... | collective-permute-start | bytes 688136 | tf_op jit(solution)/shard_map/ppermute | solution.py:319
  64.6 5.2 %collective-permute-start.16 = (bf16[896,128]{1,0:T(8,128)(2,1)S(1)}, bf16[896,128]{1,0:T(8,128)(2,1)S(1)}, u32[]{:S(2)}, u32[]{:S(2)}) collective-permute-start(bf16[896,128]{1,0:T(8,128)(2,1)S(1)} %add_convert_fusion.1.own_a), channel_id=1, source_target_pairs={{0,4},{1,3},{2,6},{3,1},{4,0},{5,7},{6,2},{7,5},{8,12},{9,11},{10,... | collective-permute-start | bytes 688136 | tf_op jit(solution)/shard_map/ppermute | solution.py:324
  65.6 5.1 %collective-permute-start.21 = (bf16[896,128]{1,0:T(8,128)(2,1)S(1)}, bf16[896,128]{1,0:T(8,128)(2,1)S(1)}, u32[]{:S(2)}, u32[]{:S(2)}) collective-permute-start(bf16[896,128]{1,0:T(8,128)(2,1)S(1)} %add_convert_fusion.1.own_a), channel_id=1, source_target_pairs={{0,1},{1,0},{2,3},{3,2},{4,5},{5,4},{6,7},{7,6},{8,9},{9,8},{10,11... | collective-permute-start | bytes 688136 | tf_op jit(solution)/shard_map/ppermute | solution.py:319
  69.8 2.0 %collective-permute-start.22 = (bf16[896,128]{1,0:T(8,128)(2,1)S(1)}, bf16[896,128]{1,0:T(8,128)(2,1)S(1)}, u32[]{:S(2)}, u32[]{:S(2)}) collective-permute-start(bf16[896,128]{1,0:T(8,128)(2,1)S(1)} %collective-permute-done.16.own_b), channel_id=1, source_target_pairs={{0,1},{1,0},{2,3},{3,2},{4,5},{5,4},{6,7},{7,6},{8,9},{9,8},{10,11... | collective-permute-start | bytes 688136 | tf_op jit(solution)/shard_map/ppermute | solution.py:319
